TPU v7x, 32 devices: a whole 2x2x4 slice. The times are simulated.
32 devices in a mesh: cluster: 4 (over z), member: 8 (over y, x, core).
Axes of the slice: x: 2, y: 2, z: 4, core: 2. Of those that a mesh axis runs over, the one named last changes fastest.
Arguments:
- factors: float32 [64, 1024, 1024], P(('cluster', 'member')), as said below
- panels: float32 [64, 1024, 256], P(('cluster', 'member')), may hold values from -0.09375 to 0.09375
- sizes: int32 [64], P(('cluster', 'member')), may hold values from 512 to 1024
- glue_index: int32 [64, 256], P(('cluster', 'member')), may hold values from 0 to 1023, as said below
- loads: float32 [4096, 256], P(('cluster', 'member')), may hold values from -6 to 6
Outputs:
- dual_rows: float32 [4096, 1024], P(('cluster', 'member'))
- products: float32 [4096, 256], P(('cluster', 'member'))
Inputs may be any that keep to these rules, and one draw needn't show every extreme that they name: `glue_index`: the 256 entries of one subdomain are distinct; at most 64 of them lie in any one aligned block of 1024 // 8 dual rows, and every subdomain has 64 in some block. `factors`: strictly upper entries are zero; diagonal entries positive.
All inputs are finite; a program needn't handle non-finite values.
Results may differ from a plain program's by a relative error of at most 0.0003.
Values sent between devices are 32-bit elements; how exact they have to be, the bound alone decides.
No kernel may reach another device: no remote copies, remote signals or barrier semaphores. Data moves between devices by JAX's collectives and lax.ppermute only.
A program may use at most 192 MiB of HBM per device.

v0:
```python
import jax
import jax.numpy as jnp
from jax import lax
from jax.sharding import PartitionSpec as P

BLOCK = 128
NDUAL = 1024
IFACE = 8


PRECISE = lax.Precision.HIGHEST


def extended(value, sides, width):
    for axis, dim in sides:
        peers, length = (lax.axis_size(axis), value.shape[dim])
        up = [(i, (i + 1) % peers) for i in range(peers)]
        down = [(j, i) for i, j in up]
        last = lax.slice_in_dim(value, length - width, length, axis=dim)
        leading = lax.slice_in_dim(value, 0, width, axis=dim)
        before = lax.ppermute(last, axis, up)
        after = lax.ppermute(leading, axis, down)
        value = jnp.concatenate([before, value, after], axis=dim)
    return value


def inner_rows(left_side, right_side):
    return lax.dot_general(
        left_side,
        right_side,
        (((0,), (0,)), ((), ())),
        precision=PRECISE,
        preferred_element_type=jnp.float32,
    )


def live_lower(factor, live_size, first_row, row_count):
    full_rows = lax.dynamic_slice_in_dim(factor, first_row, row_count, 0)
    row_ids = first_row + lax.broadcasted_iota(jnp.int32, full_rows.shape, 0)
    col_ids = lax.broadcasted_iota(jnp.int32, full_rows.shape, 1)
    keeping = (row_ids < live_size) & (col_ids < live_size) & (col_ids <= row_ids)
    return jnp.where(keeping, full_rows, (row_ids == col_ids).astype(jnp.float32))


def solve_panel(factor, gluing, live_size):
    stride = BLOCK
    row_ids = lax.broadcasted_iota(jnp.int32, gluing.shape, 0)
    masked = jnp.where(row_ids < live_size, gluing, jnp.zeros_like(gluing))
    blocks = (live_size + stride - 1) // stride

    def advance(block_index, solved):
        first_row = block_index * stride
        band_rows = live_lower(factor, live_size, first_row, stride)
        remainder = lax.dynamic_slice_in_dim(masked, first_row, stride, 0) - jnp.dot(
            band_rows, solved, precision=PRECISE, preferred_element_type=jnp.float32
        )
        square = lax.dynamic_slice_in_dim(band_rows, first_row, stride, 1)
        solved_block = lax.linalg.triangular_solve(square, remainder, left_side=True, lower=True)
        return lax.dynamic_update_slice_in_dim(solved, solved_block, first_row, 0)

    return lax.fori_loop(0, blocks, advance, jnp.zeros_like(masked))


def on_device(factors, panels, sizes, glue_index, loads):
    dual_order = NDUAL
    members = lax.axis_size("member")
    row_share = loads.shape[0]
    sub_count = factors.shape[0]
    panel_width = glue_index.shape[1]
    columns = lax.broadcasted_iota(jnp.int32, (panel_width, dual_order), 1)
    local_duals = []
    for sub_slot in range(sub_count):
        solved = solve_panel(factors[sub_slot], panels[sub_slot], sizes[sub_slot])
        local_duals.append(inner_rows(solved, solved))
    capacity = 2 * panel_width // members
    slot_total = members * capacity
    slot_ids = lax.broadcasted_iota(jnp.int32, (slot_total, panel_width), 0)
    earlier = lax.broadcasted_iota(jnp.int32, (panel_width, panel_width), 1) < lax.broadcasted_iota(
        jnp.int32, (panel_width, panel_width), 0
    )
    value_list = []
    label_list = []
    for sub_slot in range(sub_count):
        glue = glue_index[sub_slot]
        owner = glue // row_share
        same_owner = (owner[:, None] == owner[None, :]) & earlier
        rank = jnp.sum(same_owner.astype(jnp.int32), axis=1)
        target = owner * capacity + rank
        dispatch = slot_ids == target[None, :]
        values = jnp.dot(
            dispatch.astype(jnp.float32),
            local_duals[sub_slot],
            precision=PRECISE,
            preferred_element_type=jnp.float32,
        )
        filled = jnp.sum(dispatch.astype(jnp.int32), axis=1)
        label_sum = jnp.sum(jnp.where(dispatch, (glue % row_share)[None, :], 0), axis=1)
        labels = jnp.where(filled > 0, label_sum, row_share)
        value_list.append(values.reshape(members, capacity, panel_width))
        label_list.append(labels.reshape(members, capacity))
    sent_values = jnp.concatenate(value_list, axis=1)
    sent_labels = jnp.concatenate(label_list, axis=1)
    sent_columns = jnp.broadcast_to(glue_index[None, :, :], (members, sub_count, panel_width))
    got_values, got_labels, got_columns = (
        lax.all_to_all(sent_values, "member", split_axis=0, concat_axis=0, tiled=True),
        lax.all_to_all(sent_labels, "member", split_axis=0, concat_axis=0, tiled=True),
        lax.all_to_all(sent_columns, "member", split_axis=0, concat_axis=0, tiled=True),
    )
    owned_ids = lax.broadcasted_iota(jnp.int32, (row_share, capacity), 0)

    def place_source(summed, items):
        source_values, source_labels, source_columns = items
        for sub_slot in range(sub_count):
            block_values = source_values[sub_slot * capacity : (sub_slot + 1) * capacity]
            block_labels = source_labels[sub_slot * capacity : (sub_slot + 1) * capacity]
            column_map = (source_columns[sub_slot][:, None] == columns).astype(jnp.float32)
            spread = jnp.dot(
                block_values, column_map, precision=PRECISE, preferred_element_type=jnp.float32
            )
            row_map = (owned_ids == block_labels[None, :]).astype(jnp.float32)
            summed = summed + jnp.dot(
                row_map, spread, precision=PRECISE, preferred_element_type=jnp.float32
            )
        return (summed, None)

    dual_rows, unused = lax.scan(
        place_source,
        jnp.zeros((row_share, dual_order), jnp.float32),
        (got_values, got_labels, got_columns),
    )
    raw_rows = jnp.dot(
        dual_rows,
        lax.all_gather(loads, "member", axis=0, tiled=True),
        precision=PRECISE,
        preferred_element_type=jnp.float32,
    )
    width_iface = IFACE
    padded = extended(raw_rows, (("cluster", 0),), width_iface)
    previous_rows = padded[:width_iface]
    middle = padded[width_iface : width_iface + row_share]
    next_rows = padded[width_iface + row_share :]
    between = jnp.zeros((row_share - 2 * width_iface, raw_rows.shape[1]), jnp.float32)
    products = middle + jnp.concatenate([previous_rows, between, next_rows], axis=0)
    return (dual_rows, products)


def solution(mesh):
    return jax.shard_map(
        on_device,
        mesh=mesh,
        in_specs=(
            P(("cluster", "member"), None, None),
            P(("cluster", "member"), None, None),
            P(("cluster", "member")),
            P(("cluster", "member"), None),
            P(("cluster", "member"), None),
        ),
        out_specs=(P(("cluster", "member"), None), P(("cluster", "member"), None)),
        check_vma=False,
    )
```

profile of v0, /device:TPU:0, one launch (start us, length us, event | category | flops | bytes accessed | tf_op | source)
XLA Modules:
  0.0 316.6 jit_solution(8405743592939917529)
XLA Ops:
  11.2 5.2 %all-to-all-start = ((s32[8,1,128]{2,1,0:T(1,128)}), s32[8,1,128]{2,1,0:T(1,128)S(1)}, u32[]{:S(2)}, u32[]{:S(2)}) async-start(s32[8,1,128]{2,1,0:T(1,128)} %bitcast.14), calls=%async_computation | async-start | bytes 8192 | tf_op jit(solution)/shard_map/all_to_all | solution.py:106
  20.1 8.5 %slice_bitcast_fusion.3 = (f32[1024,1024]{1,0:T(8,128)}, f32[1024,1024]{1,0:T(8,128)}) fusion(f32[2,1024,1024]{2,1,0:T(8,128)} %param.13), kind=kLoop, calls=%fused_computation.48 | loop fusion | bytes 16777216 | tf_op jit(solution)/shard_map/squeeze | solution.py:73
  28.6 1.6 bitcast_select_fusion.1
  30.2 114.2 %while.33 = (s32[]{:T(128)}, f32[1024,256]{1,0:T(8,128)S(1)}, s32[]{:T(128)}, s32[]{:T(128)}, f32[1024,1024]{1,0:T(8,128)}, /*index=5*/f32[1024,256]{1,0:T(8,128)}, s32[]{:T(128)}, s32[]{:T(128)}, s32[]{:T(128)}, s32[]{:T(128)}) while((s32[]{:T(128)}, f32[1024,256]{1,0:T(8,128)S(1)}, s32[]{:T(128)}, s32[]{:T(128)}, f32[1024,1024]{1,0:T(8,128)}, ...), condition=%wide.region_5.7_spmd, body=%wide.region_4.6_spmd.sunk | while | flops 453838208 | bytes 3345843 | solution.py:61
  32.8 9.8 %custom-call.10 = f32[1,128,128]{1,2,0:T(8,128)S(1)} custom-call(f32[1,128,128]{2,1,0:T(8,128)S(1)} %select_bitcast_fusion.5), custom_call_target="InvertDiagBlocksLowerTriangular" | custom-call | tf_op jit(solution)/shard_map/while/body/triangular_solve/custom-call.1 | solution.py:58
  42.6 1.5 convolution_subtract_fusion.5
  47.1 9.8 %custom-call.10 = f32[1,128,128]{1,2,0:T(8,128)S(1)} custom-call(f32[1,128,128]{2,1,0:T(8,128)S(1)} %select_bitcast_fusion.5), custom_call_target="InvertDiagBlocksLowerTriangular" | custom-call | tf_op jit(solution)/shard_map/while/body/triangular_solve/custom-call.1 | solution.py:58
  56.9 1.5 convolution_subtract_fusion.5
  61.4 9.8 %custom-call.10 = f32[1,128,128]{1,2,0:T(8,128)S(1)} custom-call(f32[1,128,128]{2,1,0:T(8,128)S(1)} %select_bitcast_fusion.5), custom_call_target="InvertDiagBlocksLowerTriangular" | custom-call | tf_op jit(solution)/shard_map/while/body/triangular_solve/custom-call.1 | solution.py:58
  71.2 1.5 convolution_subtract_fusion.5
  75.6 9.8 %custom-call.10 = f32[1,128,128]{1,2,0:T(8,128)S(1)} custom-call(f32[1,128,128]{2,1,0:T(8,128)S(1)} %select_bitcast_fusion.5), custom_call_target="InvertDiagBlocksLowerTriangular" | custom-call | tf_op jit(solution)/shard_map/while/body/triangular_solve/custom-call.1 | solution.py:58
  85.5 1.5 convolution_subtract_fusion.5
  89.9 9.8 %custom-call.10 = f32[1,128,128]{1,2,0:T(8,128)S(1)} custom-call(f32[1,128,128]{2,1,0:T(8,128)S(1)} %select_bitcast_fusion.5), custom_call_target="InvertDiagBlocksLowerTriangular" | custom-call | tf_op jit(solution)/shard_map/while/body/triangular_solve/custom-call.1 | solution.py:58
  104.2 9.8 %custom-call.10 = f32[1,128,128]{1,2,0:T(8,128)S(1)} custom-call(f32[1,128,128]{2,1,0:T(8,128)S(1)} %select_bitcast_fusion.5), custom_call_target="InvertDiagBlocksLowerTriangular" | custom-call | tf_op jit(solution)/shard_map/while/body/triangular_solve/custom-call.1 | solution.py:58
  118.5 9.8 %custom-call.10 = f32[1,128,128]{1,2,0:T(8,128)S(1)} custom-call(f32[1,128,128]{2,1,0:T(8,128)S(1)} %select_bitcast_fusion.5), custom_call_target="InvertDiagBlocksLowerTriangular" | custom-call | tf_op jit(solution)/shard_map/while/body/triangular_solve/custom-call.1 | solution.py:58
  132.7 9.8 %custom-call.10 = f32[1,128,128]{1,2,0:T(8,128)S(1)} custom-call(f32[1,128,128]{2,1,0:T(8,128)S(1)} %select_bitcast_fusion.5), custom_call_target="InvertDiagBlocksLowerTriangular" | custom-call | tf_op jit(solution)/shard_map/while/body/triangular_solve/custom-call.1 | solution.py:58
  144.4 1.8 fusion.25
  146.8 79.6 %while.32 = (s32[]{:T(128)}, f32[1024,256]{1,0:T(8,128)S(1)}, s32[]{:T(128)}, s32[]{:T(128)}, f32[1024,1024]{1,0:T(8,128)}, /*index=5*/f32[1024,256]{1,0:T(8,128)S(1)}, s32[]{:T(128)}, s32[]{:T(128)}, s32[]{:T(128)}, s32[]{:T(128)}) while((s32[]{:T(128)}, f32[1024,256]{1,0:T(8,128)S(1)}, s32[]{:T(128)}, s32[]{:T(128)}, ...), condition=%wide.region_2.4_spmd, body=%wide.region_1.3_spmd.sunk | while | flops 453838208 | bytes 3345843 | solution.py:61
  149.3 9.8 %custom-call.9 = f32[1,128,128]{1,2,0:T(8,128)S(1)} custom-call(f32[1,128,128]{2,1,0:T(8,128)S(1)} %select_bitcast_fusion.4), custom_call_target="InvertDiagBlocksLowerTriangular" | custom-call | tf_op jit(solution)/shard_map/while/body/triangular_solve/custom-call.1 | solution.py:58
  162.5 9.8 %custom-call.9 = f32[1,128,128]{1,2,0:T(8,128)S(1)} custom-call(f32[1,128,128]{2,1,0:T(8,128)S(1)} %select_bitcast_fusion.4), custom_call_target="InvertDiagBlocksLowerTriangular" | custom-call | tf_op jit(solution)/shard_map/while/body/triangular_solve/custom-call.1 | solution.py:58
  175.7 9.8 %custom-call.9 = f32[1,128,128]{1,2,0:T(8,128)S(1)} custom-call(f32[1,128,128]{2,1,0:T(8,128)S(1)} %select_bitcast_fusion.4), custom_call_target="InvertDiagBlocksLowerTriangular" | custom-call | tf_op jit(solution)/shard_map/while/body/triangular_solve/custom-call.1 | solution.py:58
  189.0 9.8 %custom-call.9 = f32[1,128,128]{1,2,0:T(8,128)S(1)} custom-call(f32[1,128,128]{2,1,0:T(8,128)S(1)} %select_bitcast_fusion.4), custom_call_target="InvertDiagBlocksLowerTriangular" | custom-call | tf_op jit(solution)/shard_map/while/body/triangular_solve/custom-call.1 | solution.py:58
  202.2 9.8 %custom-call.9 = f32[1,128,128]{1,2,0:T(8,128)S(1)} custom-call(f32[1,128,128]{2,1,0:T(8,128)S(1)} %select_bitcast_fusion.4), custom_call_target="InvertDiagBlocksLowerTriangular" | custom-call | tf_op jit(solution)/shard_map/while/body/triangular_solve/custom-call.1 | solution.py:58
  215.5 9.8 %custom-call.9 = f32[1,128,128]{1,2,0:T(8,128)S(1)} custom-call(f32[1,128,128]{2,1,0:T(8,128)S(1)} %select_bitcast_fusion.4), custom_call_target="InvertDiagBlocksLowerTriangular" | custom-call | tf_op jit(solution)/shard_map/while/body/triangular_solve/custom-call.1 | solution.py:58
  226.4 1.8 fusion.24
  229.3 30.7 %all-to-all-start.2 = ((s32[8,2,256]{2,1,0:T(2,128)}), s32[8,2,256]{2,1,0:T(2,128)S(1)}, u32[]{:S(2)}, u32[]{:S(2)}) async-start(s32[8,2,256]{2,1,0:T(2,128)} %broadcast_in_dim.56), calls=%async_computation.2 | async-start | bytes 32768 | tf_op jit(solution)/shard_map/all_to_all | solution.py:107
  261.2 3.6 %all-to-all-done.2 = s32[8,2,256]{2,1,0:T(2,128)S(1)} async-done(((s32[8,2,256]{2,1,0:T(2,128)}), s32[8,2,256]{2,1,0:T(2,128)S(1)}, u32[]{:S(2)}, u32[]{:S(2)}) %all-to-all-start.2) | async-done | bytes 16416 | tf_op jit(solution)/shard_map/all_to_all | solution.py:107
  264.8 3.6 %all-to-all-start.1 = ((f32[8,128,256]{2,1,0:T(8,128)}), f32[8,128,256]{2,1,0:T(8,128)S(1)}, u32[]{:S(2)}, u32[]{:S(2)}) async-start(f32[8,128,256]{2,1,0:T(8,128)} %pad_maximum_fusion), calls=%async_computation.1 | async-start | bytes 2097152 | tf_op jit(solution)/shard_map/all_to_all | solution.py:105
  269.1 16.0 %all-to-all-done.1 = f32[8,128,256]{2,1,0:T(8,128)S(1)} async-done(((f32[8,128,256]{2,1,0:T(8,128)}), f32[8,128,256]{2,1,0:T(8,128)S(1)}, u32[]{:S(2)}, u32[]{:S(2)}) %all-to-all-start.1) | async-done | bytes 1048608 | tf_op jit(solution)/shard_map/all_to_all | solution.py:105
  285.1 16.3 %while.34 = (s32[]{:T(128)}, f32[128,1024]{1,0:T(8,128)S(1)}, s32[8,128]{1,0:T(8,128)S(1)}, f32[8,128,256]{2,1,0:T(8,128)S(1)}, s32[8,2,256]{2,1,0:T(2,128)S(1)}, /*index=5*/s32[]{:T(128)}, s32[]{:T(128)}, s32[]{}, s32[]{}) while((s32[]{:T(128)}, f32[128,1024]{1,0:T(8,128)S(1)}, s32[8,128]{1,0:T(8,128)S(1)}, ...), condition=%wide.region_11.13_spmd.clone.clone, body=%wide.region_10.12_spmd.clone.clone.sunk | while | flops 604913664 | bytes 3285655 | solution.py:126
  301.5 2.0 fusion.26
  304.3 3.1 collective-permute-start.1
  (192 shorter events, 78.0 us)
Async XLA Ops:
  11.2 217.5 %all-to-all-start = ((s32[8,1,128]{2,1,0:T(1,128)}), s32[8,1,128]{2,1,0:T(1,128)S(1)}, u32[]{:S(2)}, u32[]{:S(2)}) async-start(s32[8,1,128]{2,1,0:T(1,128)} %bitcast.14), calls=%async_computation | async-start | bytes 8192 | tf_op jit(solution)/shard_map/all_to_all | solution.py:106
  20.1 8.5 %copy-start.1 = (f32[2,1024,256]{2,1,0:T(8,128)S(1)}, f32[2,1024,256]{2,1,0:T(8,128)}, u32[]{:S(2)}) copy-start(f32[2,1024,256]{2,1,0:T(8,128)} %param.14) | copy-start | bytes 6291460
  146.8 81.9 %copy-start.2 = (s32[2,256]{1,0:T(2,128)S(1)}, s32[2,256]{1,0:T(2,128)}, u32[]{:S(2)}) copy-start(s32[2,256]{1,0:T(2,128)} %param.16) | copy-start | bytes 6148
  229.3 35.4 %all-to-all-start.2 = ((s32[8,2,256]{2,1,0:T(2,128)}), s32[8,2,256]{2,1,0:T(2,128)S(1)}, u32[]{:S(2)}, u32[]{:S(2)}) async-start(s32[8,2,256]{2,1,0:T(2,128)} %broadcast_in_dim.56), calls=%async_computation.2 | async-start | bytes 32768 | tf_op jit(solution)/shard_map/all_to_all | solution.py:107
  264.8 20.3 %all-to-all-start.1 = ((f32[8,128,256]{2,1,0:T(8,128)}), f32[8,128,256]{2,1,0:T(8,128)S(1)}, u32[]{:S(2)}, u32[]{:S(2)}) async-start(f32[8,128,256]{2,1,0:T(8,128)} %pad_maximum_fusion), calls=%async_computation.1 | async-start | bytes 2097152 | tf_op jit(solution)/shard_map/all_to_all | solution.py:105
  268.3 33.1 %all-gather.2.cloned.1.call-start = ((), (), s32[]{:S(2)}) async-start(), calls=%async_computation.3 | async-start | bytes 1179648 | tf_op jit(solution)/shard_map/all_gather | solution.py:133
  301.4 8.3 %copy-start = (f32[128,1024]{1,0:T(8,128)}, f32[128,1024]{1,0:T(8,128)S(1)}, u32[]{:S(2)}) copy-start(f32[128,1024]{1,0:T(8,128)S(1)} %get-tuple-element.110) | copy-start | bytes 1572868
  303.5 5.5 %collective-permute-start = (f32[8,256]{1,0:T(8,128)S(1)}, f32[8,256]{1,0:T(8,128)S(1)}, u32[]{:S(2)}, u32[]{:S(2)}) collective-permute-start(f32[8,256]{1,0:T(8,128)S(1)} %get-tuple-element.208), channel_id=1, source_target_pairs={{0,8},{8,16},{16,24},{24,0},{1,9},{9,17},{17,25},{25,1},{2,10},{10... | collective-permute-start | bytes 24584 | tf_op jit(solution)/shard_map/ppermute | solution.py:21
  304.3 4.8 %collective-permute-start.1 = (f32[8,256]{1,0:T(8,128)S(1)}, f32[8,256]{1,0:T(8,128)S(1)}, u32[]{:S(2)}, u32[]{:S(2)}) collective-permute-start(f32[8,256]{1,0:T(8,128)S(1)} %get-tuple-element.209), channel_id=1, source_target_pairs={{8,0},{16,8},{24,16},{0,24},{9,1},{17,9},{25,17},{1,25},{10,2},{18... | collective-permute-start | bytes 24584 | tf_op jit(solution)/shard_map/ppermute | solution.py:22
Sparse Core Ops, SparseCore 0:
  271.1 22.2 all-gather.1
where the time goes:
time: 318 us; the launch traced here: 317 us
  other arithmetic  180 us (57%)
  starting transfers between devices  43.3 us (14%)
  matrix products  42.4 us (13%)
  waiting for transfers between devices  21.9 us (7%)
  between operations  15.5 us (5%)
  local copies, waits for them, and re-layouts  11.6 us (4%)
    another operation x28, other arithmetic, advance(): lax.linalg.triangular_solve(square, remainder, left_side=True, lower=True)  138 us
    all_to_all x1, starting transfers between devices, on_device(): lax.all_to_all(sent_columns, 'member', split_axis=0, concat_axis=0, tiled...  30.7 us
    select_n x14, other arithmetic, live_lower(): jnp.where(keeping, full_rows, (row_ids == col_ids).astype(jnp.float32))  17.5 us
    dot_general x14, matrix products, advance(): jnp.dot(band_rows, solved, precision=PRECISE, preferred_element_type=jnp....  16.2 us
    all_to_all x1, waiting for transfers between devices, on_device(): lax.all_to_all(sent_values, 'member', split_axis=0, concat_axis=0, tiled=...  16 us
    dot_general x16, matrix products, place_source(): jnp.dot(block_values, column_map, precision=PRECISE, preferred_element_ty...  9.15 us
    squeeze x1, local copies, waits for them, and re-layouts, on_device(): solved = solve_panel(factors[sub_slot], panels[sub_slot], sizes[sub_slot])  8.48 us
    lt x14, other arithmetic, live_lower(): row_ids < live_size  8.37 us
  transfers between devices with their start and end apart: 6, of which 3 were waited for; matrix products, arithmetic and copies ran while one was open for 72% of the time, Pallas kernels for 0%

commit v1 on v0

v1 whole, which is shorter than its diff:
```python
import functools
import jax, jax.numpy as jnp
from jax import lax
from jax.experimental import pallas as pl
from jax.experimental.pallas import tpu as pltpu
F32, BF = jnp.float32, jnp.bfloat16
from jax.sharding import PartitionSpec as P

STRIDE, BASE = 128, 32
NDUAL, IFACE = 1024, 8

def split(v):
    hi = v.astype(BF)
    return hi, (v - hi.astype(F32)).astype(BF)

def mm(a, b, dims=(((1,), (0,)), ((), ()))):
    return lax.dot_general(a, b, dims, preferred_element_type=F32)

def mm3(a, b):
    ah, al = a
    bh, bl = b
    return mm(ah, bh) + (mm(al, bh) + mm(ah, bl))

def iota(shape, dim):
    return lax.broadcasted_iota(jnp.int32, shape, dim)

def invert_blocks(blocks):
    count = len(blocks)
    slabs = STRIDE // BASE
    lane = iota((BASE, STRIDE), 1)
    row = iota((BASE, STRIDE), 0)
    group, local = lane // BASE, lane % BASE
    compact = []
    for block in blocks:
        packed = block[:BASE]
        for q in range(1, slabs):
            packed = jnp.where(group == q, block[q * BASE:(q + 1) * BASE], packed)
        compact.append(packed)
    scaled, recips = [], []
    for packed in compact:
        diag = jnp.sum(jnp.where(row == local, packed, 0.0), axis=0, keepdims=True)
        recip = 1.0 / diag
        recips.append(recip)
        scaled.append(jnp.where(row > local, packed * recip, 0.0))
    parts = BASE // 8
    eye = (row == local).astype(F32)
    lane8 = iota((8, STRIDE), 1)
    base8 = (lane8 // BASE) * BASE
    row8 = iota((8, STRIDE), 0)
    out = []
    for k in range(count):
        work = [eye[g * 8:(g + 1) * 8] for g in range(parts)]
        for j in range(BASE - 1):
            pivot = work[j // 8][j % 8:j % 8 + 1]
            for g in range(j // 8, parts):
                column = jnp.take_along_axis(scaled[k][g * 8:(g + 1) * 8], base8 + j, axis=1, mode="promise_in_bounds")
                work[g] = work[g] - column * pivot
        for g in range(parts):
            rec = jnp.take_along_axis(jnp.broadcast_to(recips[k], (8, STRIDE)), base8 + row8 + g * 8, axis=1, mode="promise_in_bounds")
            work[g] = work[g] * rec
        out.append(jnp.concatenate(work, axis=0))
    full_lane = iota((STRIDE, STRIDE), 1)
    full_row = iota((STRIDE, STRIDE), 0)
    result = []
    for block, packed in zip(blocks, out):
        inverse = jnp.concatenate([jnp.where(group == q, packed, 0.0) for q in range(slabs)], axis=0)
        size = BASE
        while size < STRIDE:
            pick = ((full_row // size) % 2 == 1) & (full_lane // size == full_row // size - 1)
            below = jnp.where(pick, block, 0.0)
            inv2 = split(inverse)
            inverse = inverse - mm3(inv2, split(mm3(split(below), inv2)))
            size *= 2
        result.append(inverse)
    return result

def solve_kernel(members, sizes_ref, glue_ref, f_ref, p_ref, out_ref, rest, solved_hi, solved_lo):
    subs, order, width = p_ref.shape
    steps = order // STRIDE
    row = iota((STRIDE, STRIDE), 0)
    col = iota((STRIDE, STRIDE), 1)
    prow = iota((STRIDE, width), 0)
    inverses = []
    for s in range(subs):
        blocks = []
        for j in range(steps):
            a = j * STRIDE
            d = f_ref[s, a:a + STRIDE, a:a + STRIDE]
            keep = (row + a < sizes_ref[s]) & (col <= row)
            blocks.append(jnp.where(keep, d, (row == col).astype(F32)))
        inverses.append([split(v) for v in invert_blocks(blocks)])
    for j in range(steps):
        a = j * STRIDE
        for s in range(subs):
            now = (p_ref if j == 0 else rest)[s, a:a + STRIDE]
            now = jnp.where(prow + a < sizes_ref[s], now, 0.0)
            x = split(mm3(inverses[s][j], split(now)))
            solved_hi[s, a:a + STRIDE] = x[0]
            solved_lo[s, a:a + STRIDE] = x[1]
            for i in range(j + 1, steps):
                b = i * STRIDE
                before = (p_ref if j == 0 else rest)[s, b:b + STRIDE]
                rest[s, b:b + STRIDE] = before - mm3(split(f_ref[s, b:b + STRIDE, a:a + STRIDE]), x)
    capacity = 2 * width // members
    share = out_ref.shape[1]
    glue = glue_ref[...]
    dims = (((0,), (0,)), ((), ()))
    before = (iota((width, width), 0) < iota((width, width), 1)).astype(BF)
    dual_order = NDUAL
    for s in range(subs):
        hi, lo = solved_hi[s], solved_lo[s]
        cross = mm(hi, lo, dims)
        dual = mm(hi, hi, dims) + (cross + cross.T)
        dh, dl = split(dual)
        line = glue[s:s + 1]
        owner = line // (dual_order // members)
        owners = (iota((members, width), 0) == owner)
        ranks = mm(owners.astype(BF), before)
        rank = jnp.sum(jnp.where(owners, ranks, 0.0), axis=0, keepdims=True).astype(jnp.int32)
        target = owner * capacity + rank
        dispatch = (iota((members * capacity, width), 0) == target).astype(BF)
        values = mm(dispatch, dh) + mm(dispatch, dl)
        for k in range(members):
            out_ref[k, s * capacity:(s + 1) * capacity] = values[k * capacity:(k + 1) * capacity]

def solve(factors, panels, sizes, glue, members):
    subs, order, width = panels.shape
    capacity = 2 * width // members
    vm = pl.BlockSpec(memory_space=pltpu.VMEM)
    return pl.pallas_call(
        functools.partial(solve_kernel, members),
        out_shape=jax.ShapeDtypeStruct((members, subs * capacity, width), F32),
        in_specs=[pl.BlockSpec(memory_space=pltpu.SMEM), vm, vm, vm],
        out_specs=vm,
        scratch_shapes=[pltpu.VMEM((subs, order, width), F32), pltpu.VMEM((subs, order, width), BF), pltpu.VMEM((subs, order, width), BF)],
        compiler_params=pltpu.CompilerParams(vmem_limit_bytes=48 << 20),
        cost_estimate=pl.CostEstimate(flops=20_000_000_000, bytes_accessed=12 << 20, transcendentals=0),
        name="solve",
    )(sizes, glue, factors, panels)


def routes_kernel(subs, place_ref, got_ref, line_ref, rows_ref, high_ref, low_ref):
    members, block, nrhs = got_ref.shape
    share = NDUAL // members
    slots = rows_ref.shape[2]
    width = nrhs
    capacity = slots // subs
    loads = jnp.concatenate([got_ref[k, :share] for k in range(members)], axis=0)
    loads_high, loads_low = split(loads)
    lines = jnp.concatenate([got_ref[k, share:share + subs] for k in range(members)], axis=0)
    line_ref[...] = lines.astype(jnp.int32)
    glue = lines.astype(jnp.int32)
    standing = lines.T.astype(jnp.int32)
    first = place_ref[0] * share
    mine = ((glue >= first) & (glue < first + share))
    before = (iota((width, width), 0) < iota((width, width), 1)).astype(BF)
    ranks = mm(mine.astype(BF), before).astype(jnp.int32)
    ranks = jnp.where(mine, ranks, -1)
    for k in range(members):
        for s in range(subs):
            i = k * subs + s
            at_row = (iota((share, width), 0) + first == glue[i:i + 1]).astype(BF)
            rank = jnp.where(ranks[i:i + 1] >= 0, ranks[i:i + 1] + s * capacity, -1)
            at_slot = (iota((slots, width), 0) == rank).astype(BF)
            rows_ref[k, s * share:(s + 1) * share] = mm(at_row, at_slot, (((1,), (1,)), ((), ()))).astype(BF)
            spread = (iota((width, NDUAL), 1) == standing[:, i:i + 1]).astype(BF)
            high_ref[i] = mm(spread, loads_high).astype(BF)
            low_ref[i] = mm(spread, loads_low).astype(BF)


def raw_kernel(subs, values_ref, rows_ref, high_ref, low_ref, raw_ref, first_ref, last_ref, wide_high, wide_low):
    members, slots, width = values_ref.shape
    share, nrhs = raw_ref.shape
    total = jnp.zeros((share, nrhs), F32)
    for k in range(members):
        vh, vl = split(values_ref[k])
        rows = rows_ref[k]
        wh = mm(rows, vh).astype(BF)
        wl = mm(rows, vl).astype(BF)
        for s in range(subs):
            i = k * subs + s
            part = (wh[s * share:(s + 1) * share], wl[s * share:(s + 1) * share])
            wide_high[i] = part[0]
            wide_low[i] = part[1]
            total = total + mm3(part, (high_ref[i], low_ref[i]))
    raw_ref[...] = total
    first_ref[...] = total[:IFACE]
    last_ref[...] = total[share - IFACE:]


def place_kernel(line_ref, wide_high, wide_low, dual_ref):
    count, share, width = wide_high.shape
    total = jnp.zeros(dual_ref.shape, F32)
    for i in range(count):
        columns = (iota((NDUAL, width), 0) == line_ref[i:i + 1]).astype(BF)
        dims = (((1,), (1,)), ((), ()))
        total = total + (mm(wide_high[i], columns, dims) + mm(wide_low[i], columns, dims))
    dual_ref[...] = total


def call(kernel, outs, args, flops, name, smem=0):
    vm = pl.BlockSpec(memory_space=pltpu.VMEM)
    specs = [pl.BlockSpec(memory_space=pltpu.SMEM)] * smem + [vm] * (len(args) - smem)
    return pl.pallas_call(
        kernel,
        out_shape=outs,
        in_specs=specs,
        out_specs=jax.tree.map(lambda _: vm, outs),
        compiler_params=pltpu.CompilerParams(vmem_limit_bytes=48 << 20),
        cost_estimate=pl.CostEstimate(flops=flops, bytes_accessed=4 << 20, transcendentals=0),
        name=name,
    )(*args)


def on_device(factors, panels, sizes, glue_index, loads):
    members = lax.axis_size("member")
    subs, order, width = panels.shape
    share, nrhs = loads.shape
    capacity = 2 * width // members
    slots = subs * capacity
    count = members * subs
    shape = jax.ShapeDtypeStruct
    padding = jnp.zeros((-subs % 8, width), F32)
    mine = jnp.concatenate([loads, glue_index.astype(F32), padding], axis=0)
    everyone = jnp.broadcast_to(mine[None], (members,) + mine.shape)
    got = lax.all_to_all(everyone, "member", split_axis=0, concat_axis=0, tiled=True)
    values = solve(factors, panels, sizes, glue_index, members)
    place = lax.axis_index("member").astype(jnp.int32).reshape(1)
    lines, rows, high, low = call(
        functools.partial(routes_kernel, subs),
        (
            shape((count, width), jnp.int32),
            shape((members, subs * share, slots), BF),
            shape((count, width, nrhs), BF),
            shape((count, width, nrhs), BF),
        ),
        (place, got),
        6_000_000_000,
        "routes",
        smem=1,
    )
    values = lax.all_to_all(values, "member", split_axis=0, concat_axis=0, tiled=True)
    raw, first, last, wide_high, wide_low = call(
        functools.partial(raw_kernel, subs),
        (
            shape((share, nrhs), F32),
            shape((IFACE, nrhs), F32),
            shape((IFACE, nrhs), F32),
            shape((count, share, width), BF),
            shape((count, share, width), BF),
        ),
        (values, rows, high, low),
        2_000_000_000,
        "raw",
    )
    peers = lax.axis_size("cluster")
    up = [(i, (i + 1) % peers) for i in range(peers)]
    down = [(j, i) for i, j in up]
    before = lax.ppermute(last, "cluster", up)
    after = lax.ppermute(first, "cluster", down)
    dual_rows = call(
        place_kernel, shape((share, NDUAL), F32), (lines, wide_high, wide_low), 4_000_000_000, "place"
    )
    between = jnp.zeros((share - 2 * IFACE, nrhs), F32)
    products = raw + jnp.concatenate([before, between, after], axis=0)
    return (dual_rows, products)


def solution(mesh):
    shards = ("cluster", "member")
    return jax.shard_map(
        on_device,
        mesh=mesh,
        in_specs=(P(shards, None, None), P(shards, None, None), P(shards), P(shards, None), P(shards, None)),
        out_specs=(P(shards, None), P(shards, None)),
        check_vma=False,
    )
```

time: 318 us -> 63.8 us (0.20)
  other arithmetic: 180 us -> 2.56 us
  matrix products: 42.4 us -> 0 us
  Pallas kernels: 0 us -> 33.9 us
  starting transfers between devices: 43.3 us -> 13 us
  between operations: 15.5 us -> 0.71 us
  waiting for transfers between devices: 21.9 us -> 7.7 us
  local copies, waits for them, and re-layouts: 11.6 us -> 5.46 us
    another operation x28 -> x0, other arithmetic: 138 us -> none  [advance(): lax.linalg.triangular_solve(square, remainder, left_side=True, lower=True)]
    dot_general x51 -> x0, matrix products: 38 us -> none  [the longest x14 16.2 us: advance(): jnp.dot(band_rows, solved, precision=PRECISE, preferred_element_type=jnp....]
    pallas_call x0 -> x4, Pallas kernels: none -> 33.9 us  [the longest x1 18.8 us: solve(): pl.pallas_call(functools.partial(solve_kernel, members), out_shape=jax.Sh...]
    all_to_all x3 -> x2, starting transfers between devices: 39.4 us -> 9.36 us  [the longest x1 5.17 us: on_device(): lax.all_to_all(everyone, 'member', split_axis=0, concat_axis=0, tiled=True)]
    select_n x22 -> x0, other arithmetic: 21.4 us -> none  [the longest x14 17.5 us: live_lower(): jnp.where(keeping, full_rows, (row_ids == col_ids).astype(jnp.float32))]
    lt x29 -> x0, other arithmetic: 17.9 us -> none  [the longest x14 8.37 us: live_lower(): row_ids < live_size]
    all_to_all x3 -> x2, waiting for transfers between devices: 19.6 us -> 7.7 us  [the longest x1 7.7 us: on_device(): lax.all_to_all(values, 'member', split_axis=0, concat_axis=0, tiled=True)]
    squeeze x1 -> x0, local copies, waits for them, and re-layouts: 8.48 us -> none  [on_device(): solved = solve_panel(factors[sub_slot], panels[sub_slot], sizes[sub_slot])]
  transfers between devices with their start and end apart: 6 -> 4, of which waited for: 3 -> 1; matrix products, arithmetic and copies ran while one was open for 72% -> 0% of each run, Pallas kernels for 0% -> 48%
where the time goes in v1:
time: 63.8 us; the launch traced here: 63.4 us
  Pallas kernels  33.9 us (53%)
  starting transfers between devices  13 us (20%)
  waiting for transfers between devices  7.7 us (12%)
  local copies, waits for them, and re-layouts  5.46 us (9%)
  other arithmetic  2.56 us (4%)
  between operations  0.71 us (1%)
    pallas_call x1, Pallas kernels, solve(): pl.pallas_call(functools.partial(solve_kernel, members), out_shape=jax.Sh...  18.8 us
    pallas_call x3, Pallas kernels, call(): pl.pallas_call(kernel, out_shape=outs, in_specs=specs, out_specs=jax.tree...  15.2 us
    all_to_all x1, waiting for transfers between devices, on_device(): lax.all_to_all(values, 'member', split_axis=0, concat_axis=0, tiled=True)  7.7 us
    all_to_all x1, starting transfers between devices, on_device(): lax.all_to_all(everyone, 'member', split_axis=0, concat_axis=0, tiled=True)  5.17 us
    unnamed x12, local copies, waits for them, and re-layouts  4.23 us
    all_to_all x1, starting transfers between devices, on_device(): lax.all_to_all(values, 'member', split_axis=0, concat_axis=0, tiled=True)  4.19 us
    ppermute x1, starting transfers between devices, on_device(): after = lax.ppermute(first, 'cluster', down)  3.66 us
  transfers between devices with their start and end apart: 4, of which 1 were waited for; matrix products, arithmetic and copies ran while one was open for 0% of the time, Pallas kernels for 48%

profile of v1, /device:TPU:0, one launch (start us, length us, event | category | flops | bytes accessed | tf_op | source)
XLA Modules:
  0.0 63.4 jit_solution(10633281327714764090)
XLA Ops:
  0.6 0.0 copy-start
  0.6 0.0 copy-start.2
  0.7 0.0 copy-start.1
  0.7 0.8 %convert_element_type.3 = f32[2,256]{1,0:T(2,128)S(1)} convert(s32[2,256]{1,0:T(2,128)} %glue_ref.1) | non-fusion elementwise | flops 512 | bytes 4096 | tf_op jit(solution)/shard_map/convert_element_type | solution.py:224
  1.5 0.1 pad.5.clone
  1.6 1.0 %maximum_maximum_fusion = f32[136,256]{1,0:T(8,128)S(1)} fusion(f32[2,256]{1,0:T(2,128)S(1)} %convert_element_type.3, f32[128,256]{1,0:T(8,128)} %param.9, f32[136]{0:T(256)S(1)} %pad.5.clone), kind=kLoop, calls=%fused_computation | loop fusion | flops 69632 | bytes 272928 | tf_op jit(solution)/shard_map/concatenate | solution.py:224
  2.6 1.1 %broadcast_in_dim.13 = f32[8,136,256]{2,1,0:T(8,128)} broadcast(f32[136,256]{1,0:T(8,128)S(1)} %maximum_maximum_fusion), dimensions={1,2} | broadcast | bytes 1253376 | tf_op jit(solution)/shard_map/broadcast_in_dim | solution.py:225
  3.6 5.2 %all-to-all-start = ((f32[8,136,256]{2,1,0:T(8,128)}), f32[8,136,256]{2,1,0:T(8,128)S(1)}, u32[]{:S(2)}, u32[]{:S(2)}) async-start(f32[8,136,256]{2,1,0:T(8,128)} %broadcast_in_dim.13), calls=%async_computation | async-start | bytes 2228224 | tf_op jit(solution)/shard_map/all_to_all | solution.py:226
  8.8 0.0 copy-done
  8.8 0.0 copy-done.2
  8.8 0.0 copy-done.1
  8.8 18.8 %solve.1 = f32[8,128,256]{2,1,0:T(8,128)} custom-call(s32[2]{0:T(128)S(1)} %copy-done.2, s32[2,256]{1,0:T(2,128)S(1)} %copy-done, f32[2,1024,1024]{2,1,0:T(8,128)} %f_ref.1, f32[2,1024,256]{2,1,0:T(8,128)S(1)} %copy-done.1), custom_call_target="tpu_custom_call" | custom-call | flops 20000000000 | bytes 12582912 | tf_op jit(solution)/shard_map/solve/pallas_call | solution.py:130
  27.6 0.0 all-to-all-done.got_ref
  27.6 4.2 %all-to-all-start.1 = ((f32[8,128,256]{2,1,0:T(8,128)}), f32[8,128,256]{2,1,0:T(8,128)S(1)}, u32[]{:S(2)}, u32[]{:S(2)}) async-start(f32[8,128,256]{2,1,0:T(8,128)} %solve.1), calls=%async_computation.1 | async-start | bytes 2097152 | tf_op jit(solution)/shard_map/all_to_all | solution.py:242
  31.8 0.1 pad.1.clone
  31.9 5.0 %routes.1 = (s32[16,256]{1,0:T(8,128)S(1)}, bf16[8,256,128]{2,1,0:T(8,128)(2,1)S(1)}, bf16[16,256,256]{2,1,0:T(8,128)(2,1)S(1)}, bf16[16,256,256]{2,1,0:T(8,128)(2,1)S(1)}) custom-call(s32[1]{0:T(128)} %bitcast.place_ref, f32[8,136,256]{2,1,0:T(8,128)S(1)} %all-to-all-done.got_ref), custom_call_target="tpu_custom_call" | custom-call | flops 6000000000 | bytes 4194304 | tf_op jit(solution)/shard_map/routes/pallas_call | solution.py:204
  36.9 0.0 copy-start.3
  36.9 1.3 %copy-done.3 = bf16[16,256,256]{2,1,0:T(8,128)(2,1)} copy-done((bf16[16,256,256]{2,1,0:T(8,128)(2,1)}, bf16[16,256,256]{2,1,0:T(8,128)(2,1)S(1)}, u32[]{:S(2)}) %copy-start.3) | copy-done | bytes 2097176
  38.2 0.0 copy-start.5
  38.2 1.3 %copy-done.5 = bf16[16,256,256]{2,1,0:T(8,128)(2,1)} copy-done((bf16[16,256,256]{2,1,0:T(8,128)(2,1)}, bf16[16,256,256]{2,1,0:T(8,128)(2,1)S(1)}, u32[]{:S(2)}) %copy-start.5) | copy-done | bytes 2097176
  39.5 7.7 %all-to-all-done.1.values_ref = f32[8,128,256]{2,1,0:T(8,128)S(1)} async-done(((f32[8,128,256]{2,1,0:T(8,128)}), f32[8,128,256]{2,1,0:T(8,128)S(1)}, u32[]{:S(2)}, u32[]{:S(2)}) %all-to-all-start.1) | async-done | bytes 1048608 | tf_op jit(solution)/shard_map/all_to_all | solution.py:242
  47.2 0.0 copy-start.4
  47.2 1.6 %copy-done.4 = bf16[16,256,256]{2,1,0:T(8,128)(2,1)S(1)} copy-done((bf16[16,256,256]{2,1,0:T(8,128)(2,1)S(1)}, bf16[16,256,256]{2,1,0:T(8,128)(2,1)}, u32[]{:S(2)}) %copy-start.4) | copy-done | bytes 2097176
  48.8 3.7 %raw.1 = (f32[128,256]{1,0:T(8,128)S(1)}, f32[8,256]{1,0:T(8,128)S(1)}, f32[8,256]{1,0:T(8,128)S(1)}, bf16[16,128,256]{2,1,0:T(8,128)(2,1)S(1)}, bf16[16,128,256]{2,1,0:T(8,128)(2,1)S(1)}) custom-call(f32[8,128,256]{2,1,0:T(8,128)S(1)} %all-to-all-done.1.values_ref, bf16[8,256,128]{2,1,0:T(8,128)(2,1)S(1)} %get-tuple-element.12.rows_ref, ...), custom_call_target="tpu_custom_call" | custom-call | flops 2000000000 | bytes 4194304 | tf_op jit(solution)/shard_map/raw/pallas_call | solution.py:204
  52.5 3.7 %collective-permute-start.1 = (f32[8,256]{1,0:T(8,128)S(1)}, f32[8,256]{1,0:T(8,128)S(1)}, u32[]{:S(2)}, u32[]{:S(2)}) collective-permute-start(f32[8,256]{1,0:T(8,128)S(1)} %get-tuple-element.19), channel_id=1, source_target_pairs={{8,0},{16,8},{24,16},{0,24},{9,1},{17,9},{25,17},{1,25},{10,2},{18... | collective-permute-start | bytes 24584 | tf_op jit(solution)/shard_map/ppermute | solution.py:260
  56.2 0.0 collective-permute-start
  56.2 6.5 %place.1 = f32[128,1024]{1,0:T(8,128)} custom-call(s32[16,256]{1,0:T(8,128)S(1)} %get-tuple-element.11.line_ref, bf16[16,128,256]{2,1,0:T(8,128)(2,1)S(1)} %get-tuple-element.15.wide_high, bf16[16,128,256]{2,1,0:T(8,128)(2,1)S(1)} %get-tuple-element.16.wide_low), custom_call_target="tpu_custom_call" | custom-call | flops 4000000000 | bytes 4194304 | tf_op jit(solution)/shard_map/place/pallas_call | solution.py:204
  62.6 0.0 collective-permute-done.1
  62.6 0.0 collective-permute-done
  62.7 0.7 %maximum_add_fusion = f32[128,256]{1,0:T(8,128)} fusion(f32[128,256]{1,0:T(8,128)S(1)} %get-tuple-element.17, f32[8,256]{1,0:T(8,128)S(1)} %collective-permute-done.1, f32[8,256]{1,0:T(8,128)S(1)} %collective-permute-done, f32[128]{0:T(128)S(1)} %pad.1.clone), kind=kLoop, calls=%fused_computation.1 | loop fusion | flops 98304 | bytes 279040 | tf_op jit(solution)/shard_map/add | solution.py:265
  (2 shorter events, 0.0 us)
Async XLA Ops:
  0.6 8.2 %copy-start = (s32[2,256]{1,0:T(2,128)S(1)}, s32[2,256]{1,0:T(2,128)}, u32[]{:S(2)}) copy-start(s32[2,256]{1,0:T(2,128)} %glue_ref.1) | copy-start | bytes 6148
  0.6 8.2 %copy-start.2 = (s32[2]{0:T(128)S(1)}, s32[2]{0:T(128)}, u32[]{:S(2)}) copy-start(s32[2]{0:T(128)} %sizes_ref.1) | copy-start | bytes 28
  0.7 8.2 %copy-start.1 = (f32[2,1024,256]{2,1,0:T(8,128)S(1)}, f32[2,1024,256]{2,1,0:T(8,128)}, u32[]{:S(2)}) copy-start(f32[2,1024,256]{2,1,0:T(8,128)} %p_ref.1) | copy-start | bytes 6291460
  3.6 24.0 %all-to-all-start = ((f32[8,136,256]{2,1,0:T(8,128)}), f32[8,136,256]{2,1,0:T(8,128)S(1)}, u32[]{:S(2)}, u32[]{:S(2)}) async-start(f32[8,136,256]{2,1,0:T(8,128)} %broadcast_in_dim.13), calls=%async_computation | async-start | bytes 2228224 | tf_op jit(solution)/shard_map/all_to_all | solution.py:226
  27.6 19.6 %all-to-all-start.1 = ((f32[8,128,256]{2,1,0:T(8,128)}), f32[8,128,256]{2,1,0:T(8,128)S(1)}, u32[]{:S(2)}, u32[]{:S(2)}) async-start(f32[8,128,256]{2,1,0:T(8,128)} %solve.1), calls=%async_computation.1 | async-start | bytes 2097152 | tf_op jit(solution)/shard_map/all_to_all | solution.py:242
  36.9 1.3 %copy-start.3 = (bf16[16,256,256]{2,1,0:T(8,128)(2,1)}, bf16[16,256,256]{2,1,0:T(8,128)(2,1)S(1)}, u32[]{:S(2)}) copy-start(bf16[16,256,256]{2,1,0:T(8,128)(2,1)S(1)} %get-tuple-element.13.high_ref) | copy-start | bytes 6291460
  38.2 1.3 %copy-start.5 = (bf16[16,256,256]{2,1,0:T(8,128)(2,1)}, bf16[16,256,256]{2,1,0:T(8,128)(2,1)S(1)}, u32[]{:S(2)}) copy-start(bf16[16,256,256]{2,1,0:T(8,128)(2,1)S(1)} %get-tuple-element.14.low_ref) | copy-start | bytes 6291460
  47.2 1.6 %copy-start.4 = (bf16[16,256,256]{2,1,0:T(8,128)(2,1)S(1)}, bf16[16,256,256]{2,1,0:T(8,128)(2,1)}, u32[]{:S(2)}) copy-start(bf16[16,256,256]{2,1,0:T(8,128)(2,1)} %copy-done.3) | copy-start | bytes 6291460
  52.5 10.1 %collective-permute-start.1 = (f32[8,256]{1,0:T(8,128)S(1)}, f32[8,256]{1,0:T(8,128)S(1)}, u32[]{:S(2)}, u32[]{:S(2)}) collective-permute-start(f32[8,256]{1,0:T(8,128)S(1)} %get-tuple-element.19), channel_id=1, source_target_pairs={{8,0},{16,8},{24,16},{0,24},{9,1},{17,9},{25,17},{1,25},{10,2},{18... | collective-permute-start | bytes 24584 | tf_op jit(solution)/shard_map/ppermute | solution.py:260
  56.2 6.5 %collective-permute-start = (f32[8,256]{1,0:T(8,128)S(1)}, f32[8,256]{1,0:T(8,128)S(1)}, u32[]{:S(2)}, u32[]{:S(2)}) collective-permute-start(f32[8,256]{1,0:T(8,128)S(1)} %get-tuple-element.18), channel_id=1, source_target_pairs={{0,8},{8,16},{16,24},{24,0},{1,9},{9,17},{17,25},{25,1},{2,10},{10... | collective-permute-start | bytes 24584 | tf_op jit(solution)/shard_map/ppermute | solution.py:259

commit v2 on v1

v2 whole, which is shorter than its diff:
```python
import functools
import jax, jax.numpy as jnp
from jax import lax
from jax.experimental import pallas as pl
from jax.experimental.pallas import tpu as pltpu
F32, BF = jnp.float32, jnp.bfloat16
from jax.sharding import PartitionSpec as P

STRIDE, BASE = 128, 16
NDUAL, IFACE = 1024, 8

def split(v):
    hi = v.astype(BF)
    return hi, (v - hi.astype(F32)).astype(BF)

def mm(a, b, dims=(((1,), (0,)), ((), ()))):
    return lax.dot_general(a, b, dims, preferred_element_type=F32)

def mm3(a, b):
    ah, al = a
    bh, bl = b
    return mm(ah, bh) + (mm(al, bh) + mm(ah, bl))

def iota(shape, dim):
    return lax.broadcasted_iota(jnp.int32, shape, dim)

def mmk(a, b):
    ah, al = a
    bh, bl = b
    return mm(jnp.concatenate([ah, al], axis=1), jnp.concatenate([bh, bh], axis=0)) + mm(ah, bl)


def turn(v, by):
    return pltpu.roll(v, by, 1)


def split32(v):
    hi = v.astype(BF).astype(F32)
    return hi, v - hi


def eliminate(packs):
    lane = iota((BASE, STRIDE), 1)
    row = iota((BASE, STRIDE), 0)
    local = lane % BASE
    parts = BASE // 8
    start = (iota((8, STRIDE), 1) // BASE) * BASE
    row8 = iota((8, STRIDE), 0)
    eye = (row == local).astype(F32)
    recips, works, pieces = [], [], []
    for packed in packs:
        diag = jnp.sum(jnp.where(row == local, packed, 0.0), axis=0, keepdims=True)
        recip = 1.0 / diag
        scaled = jnp.where(row > local, packed * recip, 0.0)
        recips.append(jnp.broadcast_to(recip, (8, STRIDE)))
        works.append([eye[g * 8:(g + 1) * 8] for g in range(parts)])
        pieces.append([scaled[g * 8:(g + 1) * 8] for g in range(parts)])
    for j in range(BASE - 1):
        for work, piece in zip(works, pieces):
            pivot = work[j // 8][j % 8:j % 8 + 1]
            for g in range((j + 1) // 8, parts):
                column = jnp.take_along_axis(piece[g], start + j, axis=1, mode="promise_in_bounds")
                work[g] = work[g] - column * pivot
    for work, recip in zip(works, recips):
        for g in range(parts):
            work[g] = work[g] * jnp.take_along_axis(recip, start + (row8 + g * 8), axis=1, mode="promise_in_bounds")
    return [jnp.concatenate(work, axis=0) for work in works]


def slabs_of(v, size):
    return [v[r:r + size] for r in range(0, v.shape[0], size)]


def invert_blocks(blocks):
    lane = iota((BASE, STRIDE), 1)
    packs = []
    for block in blocks:
        packed = block[:BASE]
        for q, slab in enumerate(slabs_of(block, BASE)):
            packed = jnp.where(lane // BASE == q, slab, packed) if q else packed
        packs.append(packed)
    inners = eliminate(packs)
    states = [[jnp.where(lane // BASE == q, inner, 0.0) for q in range(STRIDE // BASE)] for inner in inners]
    size = BASE
    while size < STRIDE:
        half = iota((STRIDE // 2, STRIDE), 1) // size
        even = half % 2 == 0
        pair = (half // 2 == iota((STRIDE // 2, STRIDE), 0) // size) & even
        products = []
        for block, slabs in zip(blocks, states):
            ch, cl = split32(jnp.where(pair, jnp.concatenate(slabs_of(block, size)[1::2], axis=0), 0.0))
            a = jnp.concatenate([ch + turn(cl, size), ch], axis=1).astype(BF)
            tops = [split(v) for v in slabs[0::2]]
            w = [v[0] for v in tops for _ in range(2)] + [v[1] for v in tops for _ in range(2)]
            products.append(mm(a, jnp.concatenate(w, axis=0)))
        belows = []
        for product, slabs in zip(products, states):
            xh, xl = split32(jnp.concatenate(slabs[1::2], axis=0))
            a = jnp.concatenate([xh + turn(xl, STRIDE - size), xh], axis=1).astype(BF)
            th, tl = split(product)
            w = [v for v in slabs_of(th, size) for _ in range(2)] + [v for v in slabs_of(tl, size) for _ in range(2)]
            belows.append(slabs_of(mm(a, jnp.concatenate(w, axis=0)), size))
        states = [
            [jnp.concatenate([top, low - add], axis=0) for top, low, add in zip(slabs[0::2], slabs[1::2], below)]
            for slabs, below in zip(states, belows)
        ]
        size *= 2
    return [slabs[0] for slabs in states]


BATCH = 16


def solve_kernel(members, sizes_ref, glue_ref, far_ref, p_ref, out_ref, rest, f_ref, corner_sems, strip_sems):
    subs, order, width = p_ref.shape
    wide = 2 * STRIDE
    corner_copies, strip_copies = [], {}
    for s in range(subs):
        for step, a in enumerate(range(0, order, wide)):
            square = (s, pl.ds(a, wide), pl.ds(a, wide))
            corner_copies.append(pltpu.make_async_copy(far_ref.at[square], f_ref.at[square], corner_sems.at[s, step]))
    for step, a in enumerate(range(0, order - wide, wide)):
        for s in range(subs):
            strip = (s, pl.ds(a + wide, order - a - wide), pl.ds(a, wide))
            strip_copies[s, a] = pltpu.make_async_copy(far_ref.at[strip], f_ref.at[strip], strip_sems.at[s, step])
    for copy in corner_copies:
        copy.start()
    for copy in strip_copies.values():
        copy.start()
    for copy in corner_copies:
        copy.wait()
    row = iota((STRIDE, STRIDE), 0)
    col = iota((STRIDE, STRIDE), 1)
    prow = iota((wide, width), 0)
    dims = (((0,), (0,)), ((), ()))
    squares = [jnp.zeros((width, width), F32)] * subs
    crosses = [jnp.zeros((width, width), F32)] * subs
    places = [(s, a) for a in range(0, order, STRIDE) for s in range(subs)]
    small = {}
    for first in range(0, len(places), BATCH):
        batch = places[first:first + BATCH]
        blocks = []
        for s, a in batch:
            d = f_ref[s, a:a + STRIDE, a:a + STRIDE]
            keep = (row + a < sizes_ref[s]) & (col <= row)
            blocks.append(jnp.where(keep, d, (row == col).astype(F32)))
        for place, inverse in zip(batch, invert_blocks(blocks)):
            small[place] = split(inverse)
    heads = [(s, a) for a in range(0, order, wide) for s in range(subs)]
    corners = []
    for s, a in heads:
        b = a + STRIDE
        corner = jnp.where(row + b < sizes_ref[s], f_ref[s, b:b + STRIDE, a:b], 0.0)
        corners.append(split(mmk(split(corner), small[s, a])))
    inverses = {}
    for (s, a), corner in zip(heads, corners):
        above, below = small[s, a], small[s, a + STRIDE]
        turned = split(-mmk(below, corner))
        blank = jnp.zeros((STRIDE, STRIDE), BF)
        inverses[s, a] = [
            jnp.concatenate([jnp.concatenate([u, blank], axis=1), jnp.concatenate([t, l], axis=1)], axis=0)
            for u, t, l in zip(above, turned, below)
        ]

    def source(a):
        return p_ref if a < wide else rest

    for a in range(0, order, wide):
        solved = []
        for s in range(subs):
            now = jnp.where(prow + a < sizes_ref[s], source(a)[s, a:a + wide], 0.0)
            solved.append(split(mm3(inverses[s, a], split(now))))
        if a + wide < order:
            for s in range(subs):
                strip_copies[s, a].wait()
        for c in range(a + wide, order, wide):
            for s in range(subs):
                rest[s, c:c + wide] = source(a)[s, c:c + wide] - mm3(split(f_ref[s, c:c + wide, a:a + wide]), solved[s])
        for s in range(subs):
            hi, lo = solved[s]
            squares[s] = squares[s] + mm(hi, hi, dims)
            crosses[s] = crosses[s] + mm(hi, lo, dims)
    capacity = 2 * width // members
    glue = glue_ref[...]
    before = (iota((width, width), 0) < iota((width, width), 1)).astype(BF)
    dual_order = NDUAL
    for s in range(subs):
        dh, dl = split(squares[s] + (crosses[s] + crosses[s].T))
        line = glue[s:s + 1]
        owner = line // (dual_order // members)
        owners = (iota((members, width), 0) == owner)
        ranks = mm(owners.astype(BF), before)
        rank = jnp.sum(jnp.where(owners, ranks, 0.0), axis=0, keepdims=True).astype(jnp.int32)
        target = owner * capacity + rank
        dispatch = (iota((members * capacity, width), 0) == target).astype(BF)
        values = mm(dispatch, dh) + mm(dispatch, dl)
        for k in range(members):
            out_ref[k, s * capacity:(s + 1) * capacity] = values[k * capacity:(k + 1) * capacity]

def solve(factors, panels, sizes, glue, members):
    subs, order, width = panels.shape
    capacity = 2 * width // members
    vm = pl.BlockSpec(memory_space=pltpu.VMEM)
    return pl.pallas_call(
        functools.partial(solve_kernel, members),
        out_shape=jax.ShapeDtypeStruct((members, subs * capacity, width), F32),
        in_specs=[pl.BlockSpec(memory_space=pltpu.SMEM), vm, pl.BlockSpec(memory_space=pltpu.HBM), vm],
        out_specs=vm,
        scratch_shapes=[
            pltpu.VMEM((subs, order, width), F32),
            pltpu.VMEM((subs, order, order), F32),
            pltpu.SemaphoreType.DMA((subs, order // (2 * STRIDE))),
            pltpu.SemaphoreType.DMA((subs, order // (2 * STRIDE))),
        ],
        compiler_params=pltpu.CompilerParams(vmem_limit_bytes=54 << 20),
        cost_estimate=pl.CostEstimate(flops=10_000_000_000, bytes_accessed=12 << 20, transcendentals=0),
        name="solve",
    )(sizes, glue, factors, panels)


def pack_kernel(loads_ref, glue_ref, out_ref):
    members, rows, nrhs = out_ref.shape
    half, lines = loads_ref.shape[0] // 2, glue_ref.shape[0] // 2
    blank = jnp.zeros((rows - half - lines, nrhs), F32)
    for k in range(members):
        part = k % 2
        out_ref[k, :half] = loads_ref[part * half:(part + 1) * half]
        line = glue_ref[part * lines:(part + 1) * lines].astype(F32)
        out_ref[k, half:] = jnp.concatenate([line, blank], axis=0)


def routes_kernel(subs, place_ref, own_ref, twin_ref, stand_ref, rows_ref, high_ref, low_ref):
    members, block, width = own_ref.shape
    share = NDUAL // members
    half, lines = share // 2, subs // 2
    slots = rows_ref.shape[2]
    capacity = slots // subs
    first_core = place_ref[0] % 2 == 0
    halves = (
        jnp.where(first_core, own_ref[...], twin_ref[...]),
        jnp.where(first_core, twin_ref[...], own_ref[...]),
    )
    glue = []
    for k in range(members):
        for part in range(2):
            row = k * share + part * half
            load = split(halves[part][k, :half])
            high_ref[row:row + half] = load[0]
            low_ref[row:row + half] = load[1]
            glue.append(halves[part][k, half:half + lines])
    glue = jnp.concatenate(glue, axis=0)
    stand_ref[...] = glue.T.astype(jnp.int32)
    glue = glue.astype(jnp.int32)
    first = place_ref[0] * share
    mine = (glue >= first) & (glue < first + share)
    before = (iota((width, width), 0) < iota((width, width), 1)).astype(BF)
    ranks = mm(mine.astype(BF), before).astype(jnp.int32)
    for k in range(members):
        for s in range(subs):
            i = k * subs + s
            at_row = (iota((share, width), 0) + first == glue[i:i + 1]).astype(BF)
            rank = jnp.where(mine[i:i + 1], ranks[i:i + 1] + s * capacity, -1)
            at_slot = (iota((slots, width), 0) == rank).astype(BF)
            rows_ref[k, s * share:(s + 1) * share] = mm(at_row, at_slot, (((1,), (1,)), ((), ()))).astype(BF)


def finish_kernel(subs, values_ref, rows_ref, stand_ref, high_ref, low_ref, dual_ref, raw_ref, first_ref, last_ref):
    members, slots, width = values_ref.shape
    share, nrhs = raw_ref.shape
    total = jnp.zeros((2 * share, NDUAL), F32)
    for k in range(members):
        moved = mm(rows_ref[k], jnp.concatenate(split(values_ref[k]), axis=1)).astype(BF)
        for s in range(subs):
            i = k * subs + s
            part = moved[s * share:(s + 1) * share]
            columns = (iota((width, NDUAL), 1) == stand_ref[:, i:i + 1]).astype(BF)
            total = total + mm(jnp.concatenate([part[:, :width], part[:, width:]], axis=0), columns)
    dual = total[:share] + total[share:]
    dual_ref[...] = dual
    raw = mm3(split(dual), (high_ref[...], low_ref[...]))
    raw_ref[...] = raw
    first_ref[...] = raw[:IFACE]
    last_ref[...] = raw[share - IFACE:]


def call(kernel, outs, args, flops, name, smem=0):
    vm = pl.BlockSpec(memory_space=pltpu.VMEM)
    specs = [pl.BlockSpec(memory_space=pltpu.SMEM)] * smem + [vm] * (len(args) - smem)
    return pl.pallas_call(
        kernel,
        out_shape=outs,
        in_specs=specs,
        out_specs=jax.tree.map(lambda _: vm, outs),
        compiler_params=pltpu.CompilerParams(vmem_limit_bytes=16 << 20),
        cost_estimate=pl.CostEstimate(flops=flops, bytes_accessed=4 << 20, transcendentals=0),
        name=name,
    )(*args)


def on_device(factors, panels, sizes, glue_index, loads):
    members = lax.axis_size("member")
    subs, order, width = panels.shape
    share, nrhs = loads.shape
    capacity = 2 * width // members
    slots = subs * capacity
    count = members * subs
    shape = jax.ShapeDtypeStruct
    packed = call(pack_kernel, shape((members, share // 2 + 8 * (-(-subs // 16)), nrhs), F32), (loads, glue_index), 1_000_000, "pack")
    own = lax.all_to_all(packed, "member", split_axis=0, concat_axis=0, tiled=True)
    values = solve(factors, panels, sizes, glue_index, members)
    twin = lax.ppermute(own, "member", [(i, i ^ 1) for i in range(members)])
    place = lax.axis_index("member").astype(jnp.int32).reshape(1)
    stand, rows, high, low = call(
        functools.partial(routes_kernel, subs),
        (
            shape((width, count), jnp.int32),
            shape((members, subs * share, slots), BF),
            shape((NDUAL, nrhs), BF),
            shape((NDUAL, nrhs), BF),
        ),
        (place, own, twin),
        2_000_000_000,
        "routes",
        smem=1,
    )
    values = lax.all_to_all(values, "member", split_axis=0, concat_axis=0, tiled=True)
    dual_rows, raw, first, last = call(
        functools.partial(finish_kernel, subs),
        (
            shape((share, NDUAL), F32),
            shape((share, nrhs), F32),
            shape((IFACE, nrhs), F32),
            shape((IFACE, nrhs), F32),
        ),
        (values, rows, stand, high, low),
        5_000_000_000,
        "finish",
    )
    peers = lax.axis_size("cluster")
    up = [(i, (i + 1) % peers) for i in range(peers)]
    down = [(j, i) for i, j in up]
    before = lax.ppermute(last, "cluster", up)
    after = lax.ppermute(first, "cluster", down)
    between = jnp.zeros((share - 2 * IFACE, nrhs), F32)
    products = raw + jnp.concatenate([before, between, after], axis=0)
    return (dual_rows, products)


def solution(mesh):
    shards = ("cluster", "member")
    return jax.shard_map(
        on_device,
        mesh=mesh,
        in_specs=(P(shards, None, None), P(shards, None, None), P(shards), P(shards, None), P(shards, None)),
        out_specs=(P(shards, None), P(shards, None)),
        check_vma=False,
    )
```

time: 63.8 us -> 51.6 us (0.81)
  Pallas kernels: 33.9 us -> 17.8 us
  waiting for transfers between devices: 7.7 us -> 14.8 us
  local copies, waits for them, and re-layouts: 5.46 us -> 3.49 us
  other arithmetic: 2.56 us -> 0.74 us
  starting transfers between devices: 13 us -> 13.7 us
    pallas_call x3, Pallas kernels: 15.2 us -> 6.47 us  [call(): pl.pallas_call(kernel, out_shape=outs, in_specs=specs, out_specs=jax.tree...]
    pallas_call x1, Pallas kernels: 18.8 us -> 11.3 us  [solve(): pl.pallas_call(functools.partial(solve_kernel, members), out_shape=jax.Sh...]
    all_to_all x1, waiting for transfers between devices: 7.7 us -> 11.6 us  [on_device(): lax.all_to_all(values, 'member', split_axis=0, concat_axis=0, tiled=True)]
    ppermute x0 -> x1, waiting for transfers between devices: none -> 1.68 us  [on_device(): twin = lax.ppermute(own, 'member', [(i, i ^ 1) for i in range(members)])]
    ppermute x1, starting transfers between devices: 0.01 us -> 1.56 us  [on_device(): before = lax.ppermute(last, 'cluster', up)]
    ppermute x1, waiting for transfers between devices: 0.01 us -> 1.54 us  [on_device(): before = lax.ppermute(last, 'cluster', up)]
    ppermute x1, starting transfers between devices: 3.66 us -> 2.26 us  [on_device(): after = lax.ppermute(first, 'cluster', down)]
    broadcast_in_dim x2 -> x0, local copies, waits for them, and re-layouts: 1.08 us -> none  [the longest x1 1.08 us: on_device(): everyone = jnp.broadcast_to(mine[None], (members,) + mine.shape)]
  transfers between devices with their start and end apart: 4 -> 5, of which waited for: 1 -> 3; matrix products, arithmetic and copies ran while one was open for 0% -> 0% of each run, Pallas kernels for 48% -> 24%
where the time goes in v2:
time: 51.6 us; the launch traced here: 51.2 us
  Pallas kernels  17.8 us (34%)
  waiting for transfers between devices  14.8 us (29%)
  starting transfers between devices  13.7 us (27%)
  local copies, waits for them, and re-layouts  3.49 us (7%)
  other arithmetic  0.74 us (1%)
  between operations  0.67 us (1%)
    all_to_all x1, waiting for transfers between devices, on_device(): lax.all_to_all(values, 'member', split_axis=0, concat_axis=0, tiled=True)  11.6 us
    pallas_call x1, Pallas kernels, solve(): pl.pallas_call(functools.partial(solve_kernel, members), out_shape=jax.Sh...  11.3 us
    pallas_call x3, Pallas kernels, call(): pl.pallas_call(kernel, out_shape=outs, in_specs=specs, out_specs=jax.tree...  6.47 us
    all_to_all x1, starting transfers between devices, on_device(): lax.all_to_all(packed, 'member', split_axis=0, concat_axis=0, tiled=True)  5.17 us
    all_to_all x1, starting transfers between devices, on_device(): lax.all_to_all(values, 'member', split_axis=0, concat_axis=0, tiled=True)  4.21 us
    unnamed x8, local copies, waits for them, and re-layouts  3.41 us
    ppermute x1, starting transfers between devices, on_device(): after = lax.ppermute(first, 'cluster', down)  2.26 us
    ppermute x1, waiting for transfers between devices, on_device(): twin = lax.ppermute(own, 'member', [(i, i ^ 1) for i in range(members)])  1.68 us
  transfers between devices with their start and end apart: 5, of which 3 were waited for; matrix products, arithmetic and copies ran while one was open for 0% of the time, Pallas kernels for 24%

profile of v2, /device:TPU:0, one launch (start us, length us, event | category | flops | bytes accessed | tf_op | source)
XLA Modules:
  0.0 51.2 jit_solution(13334191102266443245)
XLA Ops:
  0.6 0.0 copy-start
  0.6 0.9 %copy-done = f32[128,256]{1,0:T(8,128)S(1)} copy-done((f32[128,256]{1,0:T(8,128)S(1)}, f32[128,256]{1,0:T(8,128)}, u32[]{:S(2)}) %copy-start) | copy-done | bytes 131096
  1.5 0.0 copy-start.1
  1.5 0.7 %copy-done.1 = s32[2,256]{1,0:T(2,128)S(1)} copy-done((s32[2,256]{1,0:T(2,128)S(1)}, s32[2,256]{1,0:T(2,128)}, u32[]{:S(2)}) %copy-start.1) | copy-done | bytes 2072
  2.2 0.9 %pack.1 = f32[8,72,256]{2,1,0:T(8,128)} custom-call(f32[128,256]{1,0:T(8,128)S(1)} %copy-done, s32[2,256]{1,0:T(2,128)S(1)} %copy-done.1), custom_call_target="tpu_custom_call" | custom-call | flops 1000000 | bytes 4194304 | tf_op jit(solution)/shard_map/pack/pallas_call | solution.py:289
  3.1 5.2 %all-to-all-start.1 = ((f32[8,72,256]{2,1,0:T(8,128)}), f32[8,72,256]{2,1,0:T(8,128)S(1)}, u32[]{:S(2)}, u32[]{:S(2)}) async-start(f32[8,72,256]{2,1,0:T(8,128)} %pack.1), calls=%async_computation.1 | async-start | bytes 1179648 | tf_op jit(solution)/shard_map/all_to_all | solution.py:309
  8.3 11.3 %solve.1 = f32[8,128,256]{2,1,0:T(8,128)} custom-call(s32[2]{0:T(128)} %sizes_ref.1, s32[2,256]{1,0:T(2,128)} %glue_ref.3, f32[2,1024,1024]{2,1,0:T(8,128)} %far_ref.1, f32[2,1024,256]{2,1,0:T(8,128)} %p_ref.1), custom_call_target="tpu_custom_call" | custom-call | flops 10000000000 | bytes 12582912 | tf_op jit(solution)/shard_map/solve/pallas_call | solution.py:204
  19.6 0.0 all-to-all-done.1.own_ref
  19.6 4.2 %all-to-all-start = ((f32[8,128,256]{2,1,0:T(8,128)}), f32[8,128,256]{2,1,0:T(8,128)S(1)}, u32[]{:S(2)}, u32[]{:S(2)}) async-start(f32[8,128,256]{2,1,0:T(8,128)} %solve.1), calls=%async_computation | async-start | bytes 2097152 | tf_op jit(solution)/shard_map/all_to_all | solution.py:326
  23.8 0.5 collective-permute-start
  24.3 1.7 %collective-permute-done.twin_ref = f32[8,72,256]{2,1,0:T(8,128)S(1)} collective-permute-done((f32[8,72,256]{2,1,0:T(8,128)S(1)}, f32[8,72,256]{2,1,0:T(8,128)S(1)}, u32[]{:S(2)}, u32[]{:S(2)}) %collective-permute-start) | collective-permute-done | bytes 589856 | tf_op jit(solution)/shard_map/ppermute | solution.py:311
  26.0 0.8 %routes.1 = (s32[256,16]{1,0:T(8,128)S(1)}, bf16[8,256,128]{2,1,0:T(8,128)(2,1)S(1)}, bf16[1024,256]{1,0:T(8,128)(2,1)S(1)}, bf16[1024,256]{1,0:T(8,128)(2,1)S(1)}) custom-call(s32[1]{0:T(128)} %bitcast.place_ref, f32[8,72,256]{2,1,0:T(8,128)S(1)} %all-to-all-done.1.own_ref, f32[8,72,256]{2,1,0:T(8,128)S(1)} %collective-permute-done.twin_ref), custom_call_target="tpu_custom_call" | custom-call | flops 2000000000 | bytes 4194304 | tf_op jit(solution)/shard_map/routes/pallas_call | solution.py:289
  26.9 0.0 copy-start.2
  26.9 0.8 %copy-done.2 = bf16[1024,256]{1,0:T(8,128)(2,1)} copy-done((bf16[1024,256]{1,0:T(8,128)(2,1)}, bf16[1024,256]{1,0:T(8,128)(2,1)S(1)}, u32[]{:S(2)}) %copy-start.2) | copy-done | bytes 524312
  27.7 11.6 %all-to-all-done.values_ref = f32[8,128,256]{2,1,0:T(8,128)S(1)} async-done(((f32[8,128,256]{2,1,0:T(8,128)}), f32[8,128,256]{2,1,0:T(8,128)S(1)}, u32[]{:S(2)}, u32[]{:S(2)}) %all-to-all-start) | async-done | bytes 1048608 | tf_op jit(solution)/shard_map/all_to_all | solution.py:326
  39.2 0.0 copy-start.3
  39.2 1.0 %copy-done.3 = bf16[1024,256]{1,0:T(8,128)(2,1)S(1)} copy-done((bf16[1024,256]{1,0:T(8,128)(2,1)S(1)}, bf16[1024,256]{1,0:T(8,128)(2,1)}, u32[]{:S(2)}) %copy-start.3) | copy-done | bytes 524312
  40.3 4.7 %finish.1 = (f32[128,1024]{1,0:T(8,128)}, f32[128,256]{1,0:T(8,128)S(1)}, f32[8,256]{1,0:T(8,128)S(1)}, f32[8,256]{1,0:T(8,128)S(1)}) custom-call(f32[8,128,256]{2,1,0:T(8,128)S(1)} %all-to-all-done.values_ref, bf16[8,256,128]{2,1,0:T(8,128)(2,1)S(1)} %get-tuple-element.10.rows_ref, s32[256,16]{1,0:T(8,128)S(1)} %get-tuple-element.11.stand_ref, ...), custom_call_target="tpu_custom_call" | custom-call | flops 5000000000 | bytes 4194304 | tf_op jit(solution)/shard_map/finish/pallas_call | solution.py:289
  45.0 1.6 %collective-permute-start.1 = (f32[8,256]{1,0:T(8,128)S(1)}, f32[8,256]{1,0:T(8,128)S(1)}, u32[]{:S(2)}, u32[]{:S(2)}) collective-permute-start(f32[8,256]{1,0:T(8,128)S(1)} %get-tuple-element.16), channel_id=1, source_target_pairs={{0,8},{8,16},{16,24},{24,0},{1,9},{9,17},{17,25},{25,1},{2,10},{10... | collective-permute-start | bytes 24584 | tf_op jit(solution)/shard_map/ppermute | solution.py:342
  46.6 2.3 %collective-permute-start.2 = (f32[8,256]{1,0:T(8,128)S(1)}, f32[8,256]{1,0:T(8,128)S(1)}, u32[]{:S(2)}, u32[]{:S(2)}) collective-permute-start(f32[8,256]{1,0:T(8,128)S(1)} %get-tuple-element.17), channel_id=1, source_target_pairs={{8,0},{16,8},{24,16},{0,24},{9,1},{17,9},{25,17},{1,25},{10,2},{18... | collective-permute-start | bytes 24584 | tf_op jit(solution)/shard_map/ppermute | solution.py:343
  48.8 0.1 pad.1.clone
  48.9 1.5 %collective-permute-done.1 = f32[8,256]{1,0:T(8,128)S(1)} collective-permute-done((f32[8,256]{1,0:T(8,128)S(1)}, f32[8,256]{1,0:T(8,128)S(1)}, u32[]{:S(2)}, u32[]{:S(2)}) %collective-permute-start.1) | collective-permute-done | bytes 8224 | tf_op jit(solution)/shard_map/ppermute | solution.py:342
  50.5 0.0 collective-permute-done.2
  50.5 0.7 %maximum_add_fusion = f32[128,256]{1,0:T(8,128)} fusion(f32[128,256]{1,0:T(8,128)S(1)} %get-tuple-element.15, f32[8,256]{1,0:T(8,128)S(1)} %collective-permute-done.2, f32[8,256]{1,0:T(8,128)S(1)} %collective-permute-done.1, f32[128]{0:T(128)S(1)} %pad.1.clone), kind=kLoop, calls=%fused_computation | loop fusion | flops 98304 | bytes 279040 | tf_op jit(solution)/shard_map/add | solution.py:345
  (1 shorter events, 0.0 us)
Async XLA Ops:
  0.6 0.9 %copy-start = (f32[128,256]{1,0:T(8,128)S(1)}, f32[128,256]{1,0:T(8,128)}, u32[]{:S(2)}) copy-start(f32[128,256]{1,0:T(8,128)} %loads_ref.1) | copy-start | bytes 393220
  1.5 0.7 %copy-start.1 = (s32[2,256]{1,0:T(2,128)S(1)}, s32[2,256]{1,0:T(2,128)}, u32[]{:S(2)}) copy-start(s32[2,256]{1,0:T(2,128)} %glue_ref.3) | copy-start | bytes 6148
  3.1 16.5 %all-to-all-start.1 = ((f32[8,72,256]{2,1,0:T(8,128)}), f32[8,72,256]{2,1,0:T(8,128)S(1)}, u32[]{:S(2)}, u32[]{:S(2)}) async-start(f32[8,72,256]{2,1,0:T(8,128)} %pack.1), calls=%async_computation.1 | async-start | bytes 1179648 | tf_op jit(solution)/shard_map/all_to_all | solution.py:309
  19.6 19.6 %all-to-all-start = ((f32[8,128,256]{2,1,0:T(8,128)}), f32[8,128,256]{2,1,0:T(8,128)S(1)}, u32[]{:S(2)}, u32[]{:S(2)}) async-start(f32[8,128,256]{2,1,0:T(8,128)} %solve.1), calls=%async_computation | async-start | bytes 2097152 | tf_op jit(solution)/shard_map/all_to_all | solution.py:326
  23.8 2.2 %collective-permute-start = (f32[8,72,256]{2,1,0:T(8,128)S(1)}, f32[8,72,256]{2,1,0:T(8,128)S(1)}, u32[]{:S(2)}, u32[]{:S(2)}) collective-permute-start(f32[8,72,256]{2,1,0:T(8,128)S(1)} %all-to-all-done.1.own_ref), channel_id=1, source_target_pairs={{0,1},{1,0},{2,3},{3,2},{4,5},{5,4},{6,7},{7,6},{8,9},{9,8},{10,11... | collective-permute-start | bytes 1769480 | tf_op jit(solution)/shard_map/ppermute | solution.py:311
  26.9 0.8 %copy-start.2 = (bf16[1024,256]{1,0:T(8,128)(2,1)}, bf16[1024,256]{1,0:T(8,128)(2,1)S(1)}, u32[]{:S(2)}) copy-start(bf16[1024,256]{1,0:T(8,128)(2,1)S(1)} %get-tuple-element.13.low_ref) | copy-start | bytes 1572868
  39.2 1.0 %copy-start.3 = (bf16[1024,256]{1,0:T(8,128)(2,1)S(1)}, bf16[1024,256]{1,0:T(8,128)(2,1)}, u32[]{:S(2)}) copy-start(bf16[1024,256]{1,0:T(8,128)(2,1)} %copy-done.2) | copy-start | bytes 1572868
  45.0 5.4 %collective-permute-start.1 = (f32[8,256]{1,0:T(8,128)S(1)}, f32[8,256]{1,0:T(8,128)S(1)}, u32[]{:S(2)}, u32[]{:S(2)}) collective-permute-start(f32[8,256]{1,0:T(8,128)S(1)} %get-tuple-element.16), channel_id=1, source_target_pairs={{0,8},{8,16},{16,24},{24,0},{1,9},{9,17},{17,25},{25,1},{2,10},{10... | collective-permute-start | bytes 24584 | tf_op jit(solution)/shard_map/ppermute | solution.py:342
  46.6 3.9 %collective-permute-start.2 = (f32[8,256]{1,0:T(8,128)S(1)}, f32[8,256]{1,0:T(8,128)S(1)}, u32[]{:S(2)}, u32[]{:S(2)}) collective-permute-start(f32[8,256]{1,0:T(8,128)S(1)} %get-tuple-element.17), channel_id=1, source_target_pairs={{8,0},{16,8},{24,16},{0,24},{9,1},{17,9},{25,17},{1,25},{10,2},{18... | collective-permute-start | bytes 24584 | tf_op jit(solution)/shard_map/ppermute | solution.py:343

commit v3 on v2

--- a/solution.py
+++ b/solution.py
@@ -111,24 +111,28 @@
 BATCH = 16
 
 
-def solve_kernel(members, sizes_ref, glue_ref, far_ref, p_ref, out_ref, rest, f_ref, corner_sems, strip_sems):
+def solve_kernel(members, sizes_ref, glue_ref, far_ref, p_ref, out_ref, rest, f_ref, square_sems, corner_sems, strip_sems, panel_sem):
     subs, order, width = p_ref.shape
     wide = 2 * STRIDE
-    corner_copies, strip_copies = [], {}
-    for s in range(subs):
-        for step, a in enumerate(range(0, order, wide)):
-            square = (s, pl.ds(a, wide), pl.ds(a, wide))
-            corner_copies.append(pltpu.make_async_copy(far_ref.at[square], f_ref.at[square], corner_sems.at[s, step]))
+    square_copies, corner_copies, strip_copies = {}, {}, {}
+
+    def fetch(s, rows, columns, sem):
+        part = (s, rows, columns)
+        copy = pltpu.make_async_copy(far_ref.at[part], f_ref.at[part], sem)
+        copy.start()
+        return copy
+
+    for step, a in enumerate(range(0, order, STRIDE)):
+        for s in range(subs):
+            square_copies[s, a] = fetch(s, pl.ds(a, STRIDE), pl.ds(a, STRIDE), square_sems.at[s, step])
+    for step, a in enumerate(range(0, order, wide)):
+        for s in range(subs):
+            corner_copies[s, a] = fetch(s, pl.ds(a + STRIDE, STRIDE), pl.ds(a, STRIDE), corner_sems.at[s, step])
+    panel_copy = pltpu.make_async_copy(p_ref, rest, panel_sem)
+    panel_copy.start()
     for step, a in enumerate(range(0, order - wide, wide)):
         for s in range(subs):
-            strip = (s, pl.ds(a + wide, order - a - wide), pl.ds(a, wide))
-            strip_copies[s, a] = pltpu.make_async_copy(far_ref.at[strip], f_ref.at[strip], strip_sems.at[s, step])
-    for copy in corner_copies:
-        copy.start()
-    for copy in strip_copies.values():
-        copy.start()
-    for copy in corner_copies:
-        copy.wait()
+            strip_copies[s, a] = fetch(s, pl.ds(a + wide, order - a - wide), pl.ds(a, wide), strip_sems.at[s, step])
     row = iota((STRIDE, STRIDE), 0)
     col = iota((STRIDE, STRIDE), 1)
     prow = iota((wide, width), 0)
@@ -141,6 +145,7 @@
         batch = places[first:first + BATCH]
         blocks = []
         for s, a in batch:
+            square_copies[s, a].wait()
             d = f_ref[s, a:a + STRIDE, a:a + STRIDE]
             keep = (row + a < sizes_ref[s]) & (col <= row)
             blocks.append(jnp.where(keep, d, (row == col).astype(F32)))
@@ -150,6 +155,7 @@
     corners = []
     for s, a in heads:
         b = a + STRIDE
+        corner_copies[s, a].wait()
         corner = jnp.where(row + b < sizes_ref[s], f_ref[s, b:b + STRIDE, a:b], 0.0)
         corners.append(split(mmk(split(corner), small[s, a])))
     inverses = {}
@@ -162,20 +168,18 @@
             for u, t, l in zip(above, turned, below)
         ]
 
-    def source(a):
-        return p_ref if a < wide else rest
-
+    panel_copy.wait()
     for a in range(0, order, wide):
         solved = []
         for s in range(subs):
-            now = jnp.where(prow + a < sizes_ref[s], source(a)[s, a:a + wide], 0.0)
+            now = jnp.where(prow + a < sizes_ref[s], rest[s, a:a + wide], 0.0)
             solved.append(split(mm3(inverses[s, a], split(now))))
         if a + wide < order:
             for s in range(subs):
                 strip_copies[s, a].wait()
         for c in range(a + wide, order, wide):
             for s in range(subs):
-                rest[s, c:c + wide] = source(a)[s, c:c + wide] - mm3(split(f_ref[s, c:c + wide, a:a + wide]), solved[s])
+                rest[s, c:c + wide] = rest[s, c:c + wide] - mm3(split(f_ref[s, c:c + wide, a:a + wide]), solved[s])
         for s in range(subs):
             hi, lo = solved[s]
             squares[s] = squares[s] + mm(hi, hi, dims)
@@ -201,16 +205,19 @@
     subs, order, width = panels.shape
     capacity = 2 * width // members
     vm = pl.BlockSpec(memory_space=pltpu.VMEM)
+    far = pl.BlockSpec(memory_space=pltpu.HBM)
     return pl.pallas_call(
         functools.partial(solve_kernel, members),
         out_shape=jax.ShapeDtypeStruct((members, subs * capacity, width), F32),
-        in_specs=[pl.BlockSpec(memory_space=pltpu.SMEM), vm, pl.BlockSpec(memory_space=pltpu.HBM), vm],
+        in_specs=[pl.BlockSpec(memory_space=pltpu.SMEM), vm, far, far],
         out_specs=vm,
         scratch_shapes=[
             pltpu.VMEM((subs, order, width), F32),
             pltpu.VMEM((subs, order, order), F32),
+            pltpu.SemaphoreType.DMA((subs, order // STRIDE)),
             pltpu.SemaphoreType.DMA((subs, order // (2 * STRIDE))),
             pltpu.SemaphoreType.DMA((subs, order // (2 * STRIDE))),
+            pltpu.SemaphoreType.DMA,
         ],
         compiler_params=pltpu.CompilerParams(vmem_limit_bytes=54 << 20),
         cost_estimate=pl.CostEstimate(flops=10_000_000_000, bytes_accessed=12 << 20, transcendentals=0),
@@ -229,11 +236,11 @@
         out_ref[k, half:] = jnp.concatenate([line, blank], axis=0)
 
 
-def routes_kernel(subs, place_ref, own_ref, twin_ref, stand_ref, rows_ref, high_ref, low_ref):
+def routes_kernel(subs, place_ref, own_ref, twin_ref, stand_ref, label_ref, high_ref, low_ref):
     members, block, width = own_ref.shape
     share = NDUAL // members
     half, lines = share // 2, subs // 2
-    slots = rows_ref.shape[2]
+    slots = label_ref.shape[1]
     capacity = slots // subs
     first_core = place_ref[0] % 2 == 0
     halves = (
@@ -255,21 +262,27 @@
     mine = (glue >= first) & (glue < first + share)
     before = (iota((width, width), 0) < iota((width, width), 1)).astype(BF)
     ranks = mm(mine.astype(BF), before).astype(jnp.int32)
+    local = jnp.where(mine, glue - first + 1, 0).astype(F32).astype(BF)
+    labels = []
     for k in range(members):
+        found = jnp.full((1, slots), -1.0, F32)
         for s in range(subs):
             i = k * subs + s
-            at_row = (iota((share, width), 0) + first == glue[i:i + 1]).astype(BF)
             rank = jnp.where(mine[i:i + 1], ranks[i:i + 1] + s * capacity, -1)
             at_slot = (iota((slots, width), 0) == rank).astype(BF)
-            rows_ref[k, s * share:(s + 1) * share] = mm(at_row, at_slot, (((1,), (1,)), ((), ()))).astype(BF)
-
-
-def finish_kernel(subs, values_ref, rows_ref, stand_ref, high_ref, low_ref, dual_ref, raw_ref, first_ref, last_ref):
+            line = mm(local[i:i + 1], at_slot, (((1,), (1,)), ((), ())))
+            found = jnp.where(line > 0.5, line + (s * share - 1), found)
+        labels.append(found)
+    label_ref[...] = jnp.concatenate(labels, axis=0).astype(jnp.int32)
+
+
+def finish_kernel(subs, values_ref, label_ref, stand_ref, high_ref, low_ref, dual_ref, raw_ref, first_ref, last_ref):
     members, slots, width = values_ref.shape
     share, nrhs = raw_ref.shape
     total = jnp.zeros((2 * share, NDUAL), F32)
     for k in range(members):
-        moved = mm(rows_ref[k], jnp.concatenate(split(values_ref[k]), axis=1)).astype(BF)
+        rows = (iota((subs * share, slots), 0) == label_ref[k:k + 1]).astype(BF)
+        moved = mm(rows, jnp.concatenate(split(values_ref[k]), axis=1)).astype(BF)
         for s in range(subs):
             i = k * subs + s
             part = moved[s * share:(s + 1) * share]
@@ -283,7 +296,7 @@
     last_ref[...] = raw[share - IFACE:]
 
 
-def call(kernel, outs, args, flops, name, smem=0):
+def call(kernel, outs, args, flops, name, smem=0, grant=16):
     vm = pl.BlockSpec(memory_space=pltpu.VMEM)
     specs = [pl.BlockSpec(memory_space=pltpu.SMEM)] * smem + [vm] * (len(args) - smem)
     return pl.pallas_call(
@@ -291,7 +304,7 @@
         out_shape=outs,
         in_specs=specs,
         out_specs=jax.tree.map(lambda _: vm, outs),
-        compiler_params=pltpu.CompilerParams(vmem_limit_bytes=16 << 20),
+        compiler_params=pltpu.CompilerParams(vmem_limit_bytes=grant << 20),
         cost_estimate=pl.CostEstimate(flops=flops, bytes_accessed=4 << 20, transcendentals=0),
         name=name,
     )(*args)
@@ -305,16 +318,16 @@
     slots = subs * capacity
     count = members * subs
     shape = jax.ShapeDtypeStruct
-    packed = call(pack_kernel, shape((members, share // 2 + 8 * (-(-subs // 16)), nrhs), F32), (loads, glue_index), 1_000_000, "pack")
+    packed = call(pack_kernel, shape((members, share // 2 + 8 * (-(-subs // 16)), nrhs), F32), (loads, glue_index), 1_000_000, "pack", grant=58)
     own = lax.all_to_all(packed, "member", split_axis=0, concat_axis=0, tiled=True)
     values = solve(factors, panels, sizes, glue_index, members)
     twin = lax.ppermute(own, "member", [(i, i ^ 1) for i in range(members)])
     place = lax.axis_index("member").astype(jnp.int32).reshape(1)
-    stand, rows, high, low = call(
+    stand, labels, high, low = call(
         functools.partial(routes_kernel, subs),
         (
             shape((width, count), jnp.int32),
-            shape((members, subs * share, slots), BF),
+            shape((members, slots), jnp.int32),
             shape((NDUAL, nrhs), BF),
             shape((NDUAL, nrhs), BF),
         ),
@@ -332,7 +345,7 @@
             shape((IFACE, nrhs), F32),
             shape((IFACE, nrhs), F32),
         ),
-        (values, rows, stand, high, low),
+        (values, labels, stand, high, low),
         5_000_000_000,
         "finish",
     )

time: 51.6 us -> 49.7 us (0.963)
  local copies, waits for them, and re-layouts: 3.49 us -> 0.08 us
  waiting for transfers between devices: 14.8 us -> 15.7 us
  Pallas kernels: 17.8 us -> 18.6 us
    unnamed x8 -> x0, local copies, waits for them, and re-layouts: 3.41 us -> none
    all_to_all x1, waiting for transfers between devices: 11.6 us -> 12.4 us  [on_device(): lax.all_to_all(values, 'member', split_axis=0, concat_axis=0, tiled=True)]
    pallas_call x3, Pallas kernels: 6.47 us -> 7.3 us  [call(): pl.pallas_call(kernel, out_shape=outs, in_specs=specs, out_specs=jax.tree...]
where the time goes in v3:
time: 49.7 us; the launch traced here: 49.4 us
  Pallas kernels  18.6 us (37%)
  waiting for transfers between devices  15.7 us (32%)
  starting transfers between devices  13.7 us (28%)
  other arithmetic  0.74 us (1%)
  between operations  0.65 us (1%)
    all_to_all x1, waiting for transfers between devices, on_device(): lax.all_to_all(values, 'member', split_axis=0, concat_axis=0, tiled=True)  12.4 us
    pallas_call x1, Pallas kernels, solve(): pl.pallas_call(functools.partial(solve_kernel, members), out_shape=jax.Sh...  11.3 us
    pallas_call x3, Pallas kernels, call(): pl.pallas_call(kernel, out_shape=outs, in_specs=specs, out_specs=jax.tree...  7.3 us
    all_to_all x1, starting transfers between devices, on_device(): lax.all_to_all(packed, 'member', split_axis=0, concat_axis=0, tiled=True)  5.17 us
    all_to_all x1, starting transfers between devices, on_device(): lax.all_to_all(values, 'member', split_axis=0, concat_axis=0, tiled=True)  4.21 us
    ppermute x1, starting transfers between devices, on_device(): after = lax.ppermute(first, 'cluster', down)  2.25 us
    ppermute x1, waiting for transfers between devices, on_device(): twin = lax.ppermute(own, 'member', [(i, i ^ 1) for i in range(members)])  1.68 us
    ppermute x1, starting transfers between devices, on_device(): before = lax.ppermute(last, 'cluster', up)  1.58 us
  transfers between devices with their start and end apart: 5, of which 3 were waited for; matrix products, arithmetic and copies ran while one was open for 0% of the time, Pallas kernels for 24%

profile of v3, /device:TPU:0, one launch (start us, length us, event | category | flops | bytes accessed | tf_op | source)
XLA Modules:
  0.0 49.4 jit_solution(13488194848108041506)
XLA Ops:
  0.6 1.8 %pack.1 = f32[8,72,256]{2,1,0:T(8,128)} custom-call(f32[128,256]{1,0:T(8,128)} %loads_ref.1, s32[2,256]{1,0:T(2,128)} %glue_ref.3), custom_call_target="tpu_custom_call" | custom-call | flops 1000000 | bytes 4194304 | tf_op jit(solution)/shard_map/pack/pallas_call | solution.py:302
  2.4 5.2 %all-to-all-start.1 = ((f32[8,72,256]{2,1,0:T(8,128)}), f32[8,72,256]{2,1,0:T(8,128)S(1)}, u32[]{:S(2)}, u32[]{:S(2)}) async-start(f32[8,72,256]{2,1,0:T(8,128)} %pack.1), calls=%async_computation.1 | async-start | bytes 1179648 | tf_op jit(solution)/shard_map/all_to_all | solution.py:322
  7.6 11.3 %solve.1 = f32[8,128,256]{2,1,0:T(8,128)} custom-call(s32[2]{0:T(128)} %sizes_ref.1, s32[2,256]{1,0:T(2,128)} %glue_ref.3, f32[2,1024,1024]{2,1,0:T(8,128)} %far_ref.1, f32[2,1024,256]{2,1,0:T(8,128)} %p_ref.1), custom_call_target="tpu_custom_call" | custom-call | flops 10000000000 | bytes 12582912 | tf_op jit(solution)/shard_map/solve/pallas_call | solution.py:209
  18.9 0.0 all-to-all-done.1.own_ref
  18.9 4.2 %all-to-all-start = ((f32[8,128,256]{2,1,0:T(8,128)}), f32[8,128,256]{2,1,0:T(8,128)S(1)}, u32[]{:S(2)}, u32[]{:S(2)}) async-start(f32[8,128,256]{2,1,0:T(8,128)} %solve.1), calls=%async_computation | async-start | bytes 2097152 | tf_op jit(solution)/shard_map/all_to_all | solution.py:339
  23.1 0.5 %collective-permute-start = (f32[8,72,256]{2,1,0:T(8,128)S(1)}, f32[8,72,256]{2,1,0:T(8,128)S(1)}, u32[]{:S(2)}, u32[]{:S(2)}) collective-permute-start(f32[8,72,256]{2,1,0:T(8,128)S(1)} %all-to-all-done.1.own_ref), channel_id=1, source_target_pairs={{0,1},{1,0},{2,3},{3,2},{4,5},{5,4},{6,7},{7,6},{8,9},{9,8},{10,11... | collective-permute-start | bytes 1769480 | tf_op jit(solution)/shard_map/ppermute | solution.py:324
  23.6 1.7 %collective-permute-done.twin_ref = f32[8,72,256]{2,1,0:T(8,128)S(1)} collective-permute-done((f32[8,72,256]{2,1,0:T(8,128)S(1)}, f32[8,72,256]{2,1,0:T(8,128)S(1)}, u32[]{:S(2)}, u32[]{:S(2)}) %collective-permute-start) | collective-permute-done | bytes 589856 | tf_op jit(solution)/shard_map/ppermute | solution.py:324
  25.3 0.8 %routes.1 = (s32[256,16]{1,0:T(8,128)S(1)}, s32[8,128]{1,0:T(8,128)S(1)}, bf16[1024,256]{1,0:T(8,128)(2,1)S(1)}, bf16[1024,256]{1,0:T(8,128)(2,1)S(1)}) custom-call(s32[1]{0:T(128)} %bitcast.place_ref, f32[8,72,256]{2,1,0:T(8,128)S(1)} %all-to-all-done.1.own_ref, f32[8,72,256]{2,1,0:T(8,128)S(1)} %collective-permute-done.twin_ref), custom_call_target="tpu_custom_call" | custom-call | flops 2000000000 | bytes 4194304 | tf_op jit(solution)/shard_map/routes/pallas_call | solution.py:302
  26.1 12.4 %all-to-all-done.values_ref = f32[8,128,256]{2,1,0:T(8,128)S(1)} async-done(((f32[8,128,256]{2,1,0:T(8,128)}), f32[8,128,256]{2,1,0:T(8,128)S(1)}, u32[]{:S(2)}, u32[]{:S(2)}) %all-to-all-start) | async-done | bytes 1048608 | tf_op jit(solution)/shard_map/all_to_all | solution.py:339
  38.5 4.7 %finish.1 = (f32[128,1024]{1,0:T(8,128)}, f32[128,256]{1,0:T(8,128)S(1)}, f32[8,256]{1,0:T(8,128)S(1)}, f32[8,256]{1,0:T(8,128)S(1)}) custom-call(f32[8,128,256]{2,1,0:T(8,128)S(1)} %all-to-all-done.values_ref, s32[8,128]{1,0:T(8,128)S(1)} %get-tuple-element.10.label_ref, s32[256,16]{1,0:T(8,128)S(1)} %get-tuple-element.11.stand_ref, ...), custom_call_target="tpu_custom_call" | custom-call | flops 5000000000 | bytes 4194304 | tf_op jit(solution)/shard_map/finish/pallas_call | solution.py:302
  43.2 1.6 %collective-permute-start.1 = (f32[8,256]{1,0:T(8,128)S(1)}, f32[8,256]{1,0:T(8,128)S(1)}, u32[]{:S(2)}, u32[]{:S(2)}) collective-permute-start(f32[8,256]{1,0:T(8,128)S(1)} %get-tuple-element.16), channel_id=1, source_target_pairs={{0,8},{8,16},{16,24},{24,0},{1,9},{9,17},{17,25},{25,1},{2,10},{10... | collective-permute-start | bytes 24584 | tf_op jit(solution)/shard_map/ppermute | solution.py:355
  44.8 2.2 %collective-permute-start.2 = (f32[8,256]{1,0:T(8,128)S(1)}, f32[8,256]{1,0:T(8,128)S(1)}, u32[]{:S(2)}, u32[]{:S(2)}) collective-permute-start(f32[8,256]{1,0:T(8,128)S(1)} %get-tuple-element.17), channel_id=1, source_target_pairs={{8,0},{16,8},{24,16},{0,24},{9,1},{17,9},{25,17},{1,25},{10,2},{18... | collective-permute-start | bytes 24584 | tf_op jit(solution)/shard_map/ppermute | solution.py:356
  47.1 0.1 pad.1.clone
  47.2 1.5 %collective-permute-done.1 = f32[8,256]{1,0:T(8,128)S(1)} collective-permute-done((f32[8,256]{1,0:T(8,128)S(1)}, f32[8,256]{1,0:T(8,128)S(1)}, u32[]{:S(2)}, u32[]{:S(2)}) %collective-permute-start.1) | collective-permute-done | bytes 8224 | tf_op jit(solution)/shard_map/ppermute | solution.py:355
  48.7 0.0 collective-permute-done.2
  48.7 0.7 %maximum_add_fusion = f32[128,256]{1,0:T(8,128)} fusion(f32[128,256]{1,0:T(8,128)S(1)} %get-tuple-element.15, f32[8,256]{1,0:T(8,128)S(1)} %collective-permute-done.2, f32[8,256]{1,0:T(8,128)S(1)} %collective-permute-done.1, f32[128]{0:T(128)S(1)} %pad.1.clone), kind=kLoop, calls=%fused_computation | loop fusion | flops 98304 | bytes 279040 | tf_op jit(solution)/shard_map/add | solution.py:358
  (1 shorter events, 0.0 us)
Async XLA Ops:
  2.4 16.5 %all-to-all-start.1 = ((f32[8,72,256]{2,1,0:T(8,128)}), f32[8,72,256]{2,1,0:T(8,128)S(1)}, u32[]{:S(2)}, u32[]{:S(2)}) async-start(f32[8,72,256]{2,1,0:T(8,128)} %pack.1), calls=%async_computation.1 | async-start | bytes 1179648 | tf_op jit(solution)/shard_map/all_to_all | solution.py:322
  18.9 19.6 %all-to-all-start = ((f32[8,128,256]{2,1,0:T(8,128)}), f32[8,128,256]{2,1,0:T(8,128)S(1)}, u32[]{:S(2)}, u32[]{:S(2)}) async-start(f32[8,128,256]{2,1,0:T(8,128)} %solve.1), calls=%async_computation | async-start | bytes 2097152 | tf_op jit(solution)/shard_map/all_to_all | solution.py:339
  23.1 2.2 %collective-permute-start = (f32[8,72,256]{2,1,0:T(8,128)S(1)}, f32[8,72,256]{2,1,0:T(8,128)S(1)}, u32[]{:S(2)}, u32[]{:S(2)}) collective-permute-start(f32[8,72,256]{2,1,0:T(8,128)S(1)} %all-to-all-done.1.own_ref), channel_id=1, source_target_pairs={{0,1},{1,0},{2,3},{3,2},{4,5},{5,4},{6,7},{7,6},{8,9},{9,8},{10,11... | collective-permute-start | bytes 1769480 | tf_op jit(solution)/shard_map/ppermute | solution.py:324
  43.2 5.4 %collective-permute-start.1 = (f32[8,256]{1,0:T(8,128)S(1)}, f32[8,256]{1,0:T(8,128)S(1)}, u32[]{:S(2)}, u32[]{:S(2)}) collective-permute-start(f32[8,256]{1,0:T(8,128)S(1)} %get-tuple-element.16), channel_id=1, source_target_pairs={{0,8},{8,16},{16,24},{24,0},{1,9},{9,17},{17,25},{25,1},{2,10},{10... | collective-permute-start | bytes 24584 | tf_op jit(solution)/shard_map/ppermute | solution.py:355
  44.8 3.9 %collective-permute-start.2 = (f32[8,256]{1,0:T(8,128)S(1)}, f32[8,256]{1,0:T(8,128)S(1)}, u32[]{:S(2)}, u32[]{:S(2)}) collective-permute-start(f32[8,256]{1,0:T(8,128)S(1)} %get-tuple-element.17), channel_id=1, source_target_pairs={{8,0},{16,8},{24,16},{0,24},{9,1},{17,9},{25,17},{1,25},{10,2},{18... | collective-permute-start | bytes 24584 | tf_op jit(solution)/shard_map/ppermute | solution.py:356

commit v4 on v3

--- a/solution.py
+++ b/solution.py
@@ -111,10 +111,12 @@
 BATCH = 16
 
 
-def solve_kernel(members, sizes_ref, glue_ref, far_ref, p_ref, out_ref, rest, f_ref, square_sems, corner_sems, strip_sems, panel_sem):
+def solve_kernel(members, place_ref, sizes_ref, glue_ref, square_ref, far_ref, p_ref, *refs):
+    out_refs = refs[:members]
+    rest, f_ref, corner_sems, strip_sems, panel_sem = refs[members:]
     subs, order, width = p_ref.shape
     wide = 2 * STRIDE
-    square_copies, corner_copies, strip_copies = {}, {}, {}
+    corner_copies, strip_copies = {}, {}
 
     def fetch(s, rows, columns, sem):
         part = (s, rows, columns)
@@ -122,9 +124,6 @@
         copy.start()
         return copy
 
-    for step, a in enumerate(range(0, order, STRIDE)):
-        for s in range(subs):
-            square_copies[s, a] = fetch(s, pl.ds(a, STRIDE), pl.ds(a, STRIDE), square_sems.at[s, step])
     for step, a in enumerate(range(0, order, wide)):
         for s in range(subs):
             corner_copies[s, a] = fetch(s, pl.ds(a + STRIDE, STRIDE), pl.ds(a, STRIDE), corner_sems.at[s, step])
@@ -145,8 +144,7 @@
         batch = places[first:first + BATCH]
         blocks = []
         for s, a in batch:
-            square_copies[s, a].wait()
-            d = f_ref[s, a:a + STRIDE, a:a + STRIDE]
+            d = square_ref[s, a // STRIDE]
             keep = (row + a < sizes_ref[s]) & (col <= row)
             blocks.append(jnp.where(keep, d, (row == col).astype(F32)))
         for place, inverse in zip(batch, invert_blocks(blocks)):
@@ -195,45 +193,86 @@
         owners = (iota((members, width), 0) == owner)
         ranks = mm(owners.astype(BF), before)
         rank = jnp.sum(jnp.where(owners, ranks, 0.0), axis=0, keepdims=True).astype(jnp.int32)
-        target = owner * capacity + rank
+        target = (owner ^ place_ref[0]) * capacity + rank
         dispatch = (iota((members * capacity, width), 0) == target).astype(BF)
         values = mm(dispatch, dh) + mm(dispatch, dl)
         for k in range(members):
-            out_ref[k, s * capacity:(s + 1) * capacity] = values[k * capacity:(k + 1) * capacity]
-
-def solve(factors, panels, sizes, glue, members):
+            out_refs[k][s * capacity:(s + 1) * capacity] = values[k * capacity:(k + 1) * capacity]
+
+def solve(place, sizes, glue, squares, factors, panels, members):
     subs, order, width = panels.shape
     capacity = 2 * width // members
     vm = pl.BlockSpec(memory_space=pltpu.VMEM)
+    sm = pl.BlockSpec(memory_space=pltpu.SMEM)
     far = pl.BlockSpec(memory_space=pltpu.HBM)
     return pl.pallas_call(
         functools.partial(solve_kernel, members),
-        out_shape=jax.ShapeDtypeStruct((members, subs * capacity, width), F32),
-        in_specs=[pl.BlockSpec(memory_space=pltpu.SMEM), vm, far, far],
-        out_specs=vm,
+        out_shape=[jax.ShapeDtypeStruct((subs * capacity, width), F32)] * members,
+        in_specs=[sm, sm, vm, vm, far, far],
+        out_specs=[vm] * members,
         scratch_shapes=[
             pltpu.VMEM((subs, order, width), F32),
             pltpu.VMEM((subs, order, order), F32),
-            pltpu.SemaphoreType.DMA((subs, order // STRIDE)),
             pltpu.SemaphoreType.DMA((subs, order // (2 * STRIDE))),
             pltpu.SemaphoreType.DMA((subs, order // (2 * STRIDE))),
             pltpu.SemaphoreType.DMA,
         ],
         compiler_params=pltpu.CompilerParams(vmem_limit_bytes=54 << 20),
-        cost_estimate=pl.CostEstimate(flops=10_000_000_000, bytes_accessed=12 << 20, transcendentals=0),
+        cost_estimate=pl.CostEstimate(flops=10_000_000_000, bytes_accessed=8 << 20, transcendentals=0),
         name="solve",
-    )(sizes, glue, factors, panels)
-
-
-def pack_kernel(loads_ref, glue_ref, out_ref):
+    )(place, sizes, glue, squares, factors, panels)
+
+
+def pack_kernel(loads_ref, far_ref, glue_ref, out_ref, square_ref, tail, load_sems, tail_sems, square_sems):
     members, rows, nrhs = out_ref.shape
     half, lines = loads_ref.shape[0] // 2, glue_ref.shape[0] // 2
+    subs, blocks = square_ref.shape[:2]
+    copies = []
+    for k in range(members):
+        rows_of = loads_ref.at[pl.ds(k % 2 * half, half)]
+        copies.append(pltpu.make_async_copy(rows_of, out_ref.at[k, pl.ds(0, half)], load_sems.at[k]))
+    for s in range(subs):
+        for j in range(blocks):
+            block = far_ref.at[s, pl.ds(j * STRIDE, STRIDE), pl.ds(j * STRIDE, STRIDE)]
+            copies.append(pltpu.make_async_copy(block, square_ref.at[s, j], square_sems.at[s, j]))
+    for copy in copies:
+        copy.start()
     blank = jnp.zeros((rows - half - lines, nrhs), F32)
+    for part in range(2):
+        line = glue_ref[part * lines:(part + 1) * lines].astype(F32)
+        tail[part] = jnp.concatenate([line, blank], axis=0)
     for k in range(members):
-        part = k % 2
-        out_ref[k, :half] = loads_ref[part * half:(part + 1) * half]
-        line = glue_ref[part * lines:(part + 1) * lines].astype(F32)
-        out_ref[k, half:] = jnp.concatenate([line, blank], axis=0)
+        copy = pltpu.make_async_copy(tail.at[k % 2], out_ref.at[k, pl.ds(half, rows - half)], tail_sems.at[k])
+        copy.start()
+        copies.append(copy)
+    for copy in copies:
+        copy.wait()
+
+
+def pack(loads, factors, glue, members):
+    subs, order, _ = factors.shape
+    share, nrhs = loads.shape
+    rows = share // 2 + 8 * (-(-subs // 16))
+    vm = pl.BlockSpec(memory_space=pltpu.VMEM)
+    far = pl.BlockSpec(memory_space=pltpu.HBM)
+    return pl.pallas_call(
+        pack_kernel,
+        out_shape=[
+            jax.ShapeDtypeStruct((members, rows, nrhs), F32),
+            jax.ShapeDtypeStruct((subs, order // STRIDE, STRIDE, STRIDE), F32),
+        ],
+        in_specs=[far, far, vm],
+        out_specs=[far, vm],
+        scratch_shapes=[
+            pltpu.VMEM((2, rows - share // 2, nrhs), F32),
+            pltpu.SemaphoreType.DMA((members,)),
+            pltpu.SemaphoreType.DMA((members,)),
+            pltpu.SemaphoreType.DMA((subs, order // STRIDE)),
+        ],
+        compiler_params=pltpu.CompilerParams(vmem_limit_bytes=58 << 20),
+        cost_estimate=pl.CostEstimate(flops=1_000_000, bytes_accessed=3 << 20, transcendentals=0),
+        name="pack",
+    )(loads, factors, glue)
 
 
 def routes_kernel(subs, place_ref, own_ref, twin_ref, stand_ref, label_ref, high_ref, low_ref):
@@ -243,18 +282,15 @@
     slots = label_ref.shape[1]
     capacity = slots // subs
     first_core = place_ref[0] % 2 == 0
-    halves = (
-        jnp.where(first_core, own_ref[...], twin_ref[...]),
-        jnp.where(first_core, twin_ref[...], own_ref[...]),
-    )
     glue = []
     for k in range(members):
+        source = place_ref[0] ^ k
+        pair = own_ref[source], twin_ref[source]
         for part in range(2):
-            row = k * share + part * half
-            load = split(halves[part][k, :half])
-            high_ref[row:row + half] = load[0]
-            low_ref[row:row + half] = load[1]
-            glue.append(halves[part][k, half:half + lines])
+            got = jnp.where(first_core, pair[part], pair[1 - part])
+            row = pl.ds(pl.multiple_of(source * share + part * half, half), half)
+            high_ref[row], low_ref[row] = split(got[:half])
+            glue.append(got[half:half + lines])
     glue = jnp.concatenate(glue, axis=0)
     stand_ref[...] = glue.T.astype(jnp.int32)
     glue = glue.astype(jnp.int32)
@@ -276,13 +312,15 @@
     label_ref[...] = jnp.concatenate(labels, axis=0).astype(jnp.int32)
 
 
-def finish_kernel(subs, values_ref, label_ref, stand_ref, high_ref, low_ref, dual_ref, raw_ref, first_ref, last_ref):
-    members, slots, width = values_ref.shape
+def finish_kernel(subs, order, label_ref, stand_ref, high_ref, low_ref, *refs):
+    values, (dual_ref, raw_ref, first_ref, last_ref) = refs[:-4], refs[-4:]
+    members = len(values)
+    slots, width = values[0].shape
     share, nrhs = raw_ref.shape
     total = jnp.zeros((2 * share, NDUAL), F32)
-    for k in range(members):
+    for k, value in zip(order, values):
         rows = (iota((subs * share, slots), 0) == label_ref[k:k + 1]).astype(BF)
-        moved = mm(rows, jnp.concatenate(split(values_ref[k]), axis=1)).astype(BF)
+        moved = mm(rows, jnp.concatenate(split(value[...]), axis=1)).astype(BF)
         for s in range(subs):
             i = k * subs + s
             part = moved[s * share:(s + 1) * share]
@@ -318,11 +356,18 @@
     slots = subs * capacity
     count = members * subs
     shape = jax.ShapeDtypeStruct
-    packed = call(pack_kernel, shape((members, share // 2 + 8 * (-(-subs // 16)), nrhs), F32), (loads, glue_index), 1_000_000, "pack", grant=58)
+    place = lax.axis_index("member").astype(jnp.int32).reshape(1)
+
+    def across(value, distance):
+        return lax.ppermute(value, "member", [(i, i ^ distance) for i in range(members)])
+
+    packed, squares = pack(loads, factors, glue_index, members)
     own = lax.all_to_all(packed, "member", split_axis=0, concat_axis=0, tiled=True)
-    values = solve(factors, panels, sizes, glue_index, members)
-    twin = lax.ppermute(own, "member", [(i, i ^ 1) for i in range(members)])
-    place = lax.axis_index("member").astype(jnp.int32).reshape(1)
+    values = solve(place, sizes, glue_index, squares, factors, panels, members)
+    own, *values = lax.optimization_barrier((own, *values))
+    arrivals = (0, *range(2, members, 2), *range(3, members, 2), 1)
+    arrived = [across(values[k], k) if k else values[k] for k in arrivals]
+    twin = across(own, 1)
     stand, labels, high, low = call(
         functools.partial(routes_kernel, subs),
         (
@@ -336,16 +381,15 @@
         "routes",
         smem=1,
     )
-    values = lax.all_to_all(values, "member", split_axis=0, concat_axis=0, tiled=True)
     dual_rows, raw, first, last = call(
-        functools.partial(finish_kernel, subs),
+        functools.partial(finish_kernel, subs, arrivals),
         (
             shape((share, NDUAL), F32),
             shape((share, nrhs), F32),
             shape((IFACE, nrhs), F32),
             shape((IFACE, nrhs), F32),
         ),
-        (values, labels, stand, high, low),
+        (labels, stand, high, low, *arrived),
         5_000_000_000,
         "finish",
     )

time: 49.7 us -> 64.1 us (1.29)
  Pallas kernels: 18.6 us -> 35.1 us
  waiting for transfers between devices: 15.7 us -> 10 us
  starting transfers between devices: 13.7 us -> 16.3 us
  local copies, waits for them, and re-layouts: 0.08 us -> 0.98 us
    pallas_call x1 -> x2, Pallas kernels: 11.3 us -> 29.7 us  [the longest x1 19 us: pack(): pl.pallas_call(pack_kernel, out_shape=[jax.ShapeDtypeStruct((members, row...]
    all_to_all x1 -> x0, waiting for transfers between devices: 12.4 us -> none  [on_device(): lax.all_to_all(values, 'member', split_axis=0, concat_axis=0, tiled=True)]
    ppermute x1 -> x8, waiting for transfers between devices: 1.68 us -> 8.47 us  [across(): lax.ppermute(value, 'member', [(i, i ^ distance) for i in range(members)])]
    ppermute x1 -> x8, starting transfers between devices: 0.51 us -> 7.27 us  [across(): lax.ppermute(value, 'member', [(i, i ^ distance) for i in range(members)])]
    all_to_all x1 -> x0, starting transfers between devices: 4.21 us -> none  [on_device(): lax.all_to_all(values, 'member', split_axis=0, concat_axis=0, tiled=True)]
    pallas_call x3 -> x2, Pallas kernels: 7.3 us -> 5.44 us  [call(): pl.pallas_call(kernel, out_shape=outs, in_specs=specs, out_specs=jax.tree...]
    unnamed x0 -> x2, local copies, waits for them, and re-layouts: none -> 0.91 us
  transfers between devices with their start and end apart: 5 -> 11, of which waited for: 3 -> 5; matrix products, arithmetic and copies ran while one was open for 0% -> 0% of each run, Pallas kernels for 24% -> 18%
where the time goes in v4:
time: 64.1 us; the launch traced here: 63.8 us
  Pallas kernels  35.1 us (55%)
  starting transfers between devices  16.3 us (25%)
  waiting for transfers between devices  10 us (16%)
  local copies, waits for them, and re-layouts  0.98 us (2%)
  other arithmetic  0.74 us (1%)
  between operations  0.67 us (1%)
    pallas_call x1, Pallas kernels, pack(): pl.pallas_call(pack_kernel, out_shape=[jax.ShapeDtypeStruct((members, row...  19 us
    pallas_call x1, Pallas kernels, solve(): pl.pallas_call(functools.partial(solve_kernel, members), out_shape=[jax.S...  10.7 us
    ppermute x8, waiting for transfers between devices, across(): lax.ppermute(value, 'member', [(i, i ^ distance) for i in range(members)])  8.47 us
    ppermute x8, starting transfers between devices, across(): lax.ppermute(value, 'member', [(i, i ^ distance) for i in range(members)])  7.27 us
    pallas_call x2, Pallas kernels, call(): pl.pallas_call(kernel, out_shape=outs, in_specs=specs, out_specs=jax.tree...  5.44 us
    all_to_all x1, starting transfers between devices, on_device(): lax.all_to_all(packed, 'member', split_axis=0, concat_axis=0, tiled=True)  5.18 us
    ppermute x1, starting transfers between devices, on_device(): after = lax.ppermute(first, 'cluster', down)  2.27 us
    ppermute x1, starting transfers between devices, on_device(): before = lax.ppermute(last, 'cluster', up)  1.55 us
  transfers between devices with their start and end apart: 11, of which 5 were waited for; matrix products, arithmetic and copies ran while one was open for 0% of the time, Pallas kernels for 18%

profile of v4, /device:TPU:0, one launch (start us, length us, event | category | flops | bytes accessed | tf_op | source)
XLA Modules:
  0.0 63.8 jit_solution(1303978237529244079)
XLA Ops:
  0.6 19.0 %pack.1 = (f32[8,72,256]{2,1,0:T(8,128)}, f32[2,8,128,128]{3,2,1,0:T(8,128)}) custom-call(f32[128,256]{1,0:T(8,128)} %loads_ref.1, f32[2,1024,1024]{2,1,0:T(8,128)} %far_ref.3, s32[2,256]{1,0:T(2,128)} %glue_ref.3), custom_call_target="tpu_custom_call" | custom-call | flops 1000000 | bytes 3145728 | tf_op jit(solution)/shard_map/pack/pallas_call | solution.py:258
  19.6 5.2 %all-to-all-start = ((f32[8,72,256]{2,1,0:T(8,128)}), f32[8,72,256]{2,1,0:T(8,128)S(1)}, u32[]{:S(2)}, u32[]{:S(2)}) async-start(f32[8,72,256]{2,1,0:T(8,128)} %get-tuple-element.29), calls=%async_computation | async-start | bytes 1179648 | tf_op jit(solution)/shard_map/all_to_all | solution.py:365
  24.8 10.7 %solve.1 = (f32[128,256]{1,0:T(8,128)}, f32[128,256]{1,0:T(8,128)}, f32[128,256]{1,0:T(8,128)}, f32[128,256]{1,0:T(8,128)}, f32[128,256]{1,0:T(8,128)}, /*index=...) custom-call(s32[1]{0:T(128)} %bitcast.place_ref, s32[2]{0:T(128)} %sizes_ref.1, s32[2,256]{1,0:T(2,128)} %glue_ref.3, ...), custom_call_target="tpu_custom_call" | custom-call | flops 10000000000 | bytes 8388608 | tf_op jit(solution)/shard_map/solve/pallas_call | solution.py:208
  35.5 0.0 all-to-all-done.own_ref
  35.5 0.6 collective-permute-start
  36.1 1.7 %collective-permute-start.1 = (f32[128,256]{1,0:T(8,128)}, f32[128,256]{1,0:T(8,128)S(1)}, u32[]{:S(2)}, u32[]{:S(2)}) collective-permute-start(f32[128,256]{1,0:T(8,128)} %get-tuple-element.45), channel_id=1, source_target_pairs={{0,2},{1,3},{2,0},{3,1},{4,6},{5,7},{6,4},{7,5},{8,10},{9,11},{10,... | collective-permute-start | bytes 393224 | tf_op jit(solution)/shard_map/ppermute | solution.py:362
  37.8 1.5 %collective-permute-start.2 = (f32[128,256]{1,0:T(8,128)}, f32[128,256]{1,0:T(8,128)S(1)}, u32[]{:S(2)}, u32[]{:S(2)}) collective-permute-start(f32[128,256]{1,0:T(8,128)} %get-tuple-element.46), channel_id=1, source_target_pairs={{0,4},{1,5},{2,6},{3,7},{4,0},{5,1},{6,2},{7,3},{8,12},{9,13},{10,... | collective-permute-start | bytes 393224 | tf_op jit(solution)/shard_map/ppermute | solution.py:362
  39.3 0.4 collective-permute-start.3
  39.6 0.8 %collective-permute-start.4 = (f32[128,256]{1,0:T(8,128)}, f32[128,256]{1,0:T(8,128)S(1)}, u32[]{:S(2)}, u32[]{:S(2)}) collective-permute-start(f32[128,256]{1,0:T(8,128)} %get-tuple-element.48), channel_id=1, source_target_pairs={{0,3},{1,2},{2,1},{3,0},{4,7},{5,6},{6,5},{7,4},{8,11},{9,10},{10,... | collective-permute-start | bytes 393224 | tf_op jit(solution)/shard_map/ppermute | solution.py:362
  40.4 1.7 %collective-permute-done.1.refs_1_ = f32[128,256]{1,0:T(8,128)S(1)} collective-permute-done((f32[128,256]{1,0:T(8,128)}, f32[128,256]{1,0:T(8,128)S(1)}, u32[]{:S(2)}, u32[]{:S(2)}) %collective-permute-start.1) | collective-permute-done | bytes 131104 | tf_op jit(solution)/shard_map/ppermute | solution.py:362
  42.1 0.8 %collective-permute-start.5 = (f32[128,256]{1,0:T(8,128)}, f32[128,256]{1,0:T(8,128)S(1)}, u32[]{:S(2)}, u32[]{:S(2)}) collective-permute-start(f32[128,256]{1,0:T(8,128)} %get-tuple-element.49), channel_id=1, source_target_pairs={{0,5},{1,4},{2,7},{3,6},{4,1},{5,0},{6,3},{7,2},{8,13},{9,12},{10,... | collective-permute-start | bytes 393224 | tf_op jit(solution)/shard_map/ppermute | solution.py:362
  42.9 3.0 %collective-permute-done.2.refs_2_ = f32[128,256]{1,0:T(8,128)S(1)} collective-permute-done((f32[128,256]{1,0:T(8,128)}, f32[128,256]{1,0:T(8,128)S(1)}, u32[]{:S(2)}, u32[]{:S(2)}) %collective-permute-start.2) | collective-permute-done | bytes 131104 | tf_op jit(solution)/shard_map/ppermute | solution.py:362
  46.0 0.0 collective-permute-start.6
  46.0 0.0 collective-permute-done.twin_ref
  46.0 1.6 %collective-permute-start.7 = (f32[128,256]{1,0:T(8,128)}, f32[128,256]{1,0:T(8,128)S(1)}, u32[]{:S(2)}, u32[]{:S(2)}) collective-permute-start(f32[128,256]{1,0:T(8,128)} %get-tuple-element.51), channel_id=1, source_target_pairs={{0,1},{1,0},{2,3},{3,2},{4,5},{5,4},{6,7},{7,6},{8,9},{9,8},{10,11... | collective-permute-start | bytes 393224 | tf_op jit(solution)/shard_map/ppermute | solution.py:362
  47.6 0.7 %routes.1 = (s32[256,16]{1,0:T(8,128)S(1)}, s32[8,128]{1,0:T(8,128)S(1)}, bf16[1024,256]{1,0:T(8,128)(2,1)S(1)}, bf16[1024,256]{1,0:T(8,128)(2,1)S(1)}) custom-call(s32[1]{0:T(128)} %bitcast.place_ref, f32[8,72,256]{2,1,0:T(8,128)S(1)} %all-to-all-done.own_ref, f32[8,72,256]{2,1,0:T(8,128)S(1)} %collective-permute-done.twin_ref), custom_call_target="tpu_custom_call" | custom-call | flops 2000000000 | bytes 4194304 | tf_op jit(solution)/shard_map/routes/pallas_call | solution.py:340
  48.3 0.0 collective-permute-done.3.refs_3_
  48.3 0.0 collective-permute-done.4.refs_4_
  48.3 0.7 %collective-permute-done.5.refs_5_ = f32[128,256]{1,0:T(8,128)S(1)} collective-permute-done((f32[128,256]{1,0:T(8,128)}, f32[128,256]{1,0:T(8,128)S(1)}, u32[]{:S(2)}, u32[]{:S(2)}) %collective-permute-start.5) | collective-permute-done | bytes 131104 | tf_op jit(solution)/shard_map/ppermute | solution.py:362
  49.0 3.0 %collective-permute-done.6.refs_6_ = f32[128,256]{1,0:T(8,128)S(1)} collective-permute-done((f32[128,256]{1,0:T(8,128)}, f32[128,256]{1,0:T(8,128)S(1)}, u32[]{:S(2)}, u32[]{:S(2)}) %collective-permute-start.6) | collective-permute-done | bytes 131104 | tf_op jit(solution)/shard_map/ppermute | solution.py:362
  52.0 0.0 collective-permute-done.7.refs_7_
  52.0 0.0 copy-start
  52.0 0.9 %copy-done = f32[128,256]{1,0:T(8,128)S(1)} copy-done((f32[128,256]{1,0:T(8,128)S(1)}, f32[128,256]{1,0:T(8,128)}, u32[]{:S(2)}) %copy-start) | copy-done | bytes 131096
  52.9 4.7 %finish.1 = (f32[128,1024]{1,0:T(8,128)}, f32[128,256]{1,0:T(8,128)S(1)}, f32[8,256]{1,0:T(8,128)S(1)}, f32[8,256]{1,0:T(8,128)S(1)}) custom-call(s32[8,128]{1,0:T(8,128)S(1)} %get-tuple-element.40.label_ref, s32[256,16]{1,0:T(8,128)S(1)} %get-tuple-element.41.stand_ref, bf16[1024,256]{1,0:T(8,128)(2,1)S(1)} %get-tuple-element.42.high_ref, ...), custom_call_target="tpu_custom_call" | custom-call | flops 5000000000 | bytes 4194304 | tf_op jit(solution)/shard_map/finish/pallas_call | solution.py:340
  57.6 1.6 %collective-permute-start.8 = (f32[8,256]{1,0:T(8,128)S(1)}, f32[8,256]{1,0:T(8,128)S(1)}, u32[]{:S(2)}, u32[]{:S(2)}) collective-permute-start(f32[8,256]{1,0:T(8,128)S(1)} %get-tuple-element.54), channel_id=1, source_target_pairs={{0,8},{8,16},{16,24},{24,0},{1,9},{9,17},{17,25},{25,1},{2,10},{10... | collective-permute-start | bytes 24584 | tf_op jit(solution)/shard_map/ppermute | solution.py:399
  59.2 2.3 %collective-permute-start.9 = (f32[8,256]{1,0:T(8,128)S(1)}, f32[8,256]{1,0:T(8,128)S(1)}, u32[]{:S(2)}, u32[]{:S(2)}) collective-permute-start(f32[8,256]{1,0:T(8,128)S(1)} %get-tuple-element.55), channel_id=1, source_target_pairs={{8,0},{16,8},{24,16},{0,24},{9,1},{17,9},{25,17},{1,25},{10,2},{18... | collective-permute-start | bytes 24584 | tf_op jit(solution)/shard_map/ppermute | solution.py:400
  61.5 0.1 pad.1.clone
  61.6 1.5 %collective-permute-done.8 = f32[8,256]{1,0:T(8,128)S(1)} collective-permute-done((f32[8,256]{1,0:T(8,128)S(1)}, f32[8,256]{1,0:T(8,128)S(1)}, u32[]{:S(2)}, u32[]{:S(2)}) %collective-permute-start.8) | collective-permute-done | bytes 8224 | tf_op jit(solution)/shard_map/ppermute | solution.py:399
  63.1 0.0 collective-permute-done.9
  63.1 0.7 %maximum_add_fusion = f32[128,256]{1,0:T(8,128)} fusion(f32[128,256]{1,0:T(8,128)S(1)} %get-tuple-element.53, f32[8,256]{1,0:T(8,128)S(1)} %collective-permute-done.9, f32[8,256]{1,0:T(8,128)S(1)} %collective-permute-done.8, f32[128]{0:T(128)S(1)} %pad.1.clone), kind=kLoop, calls=%fused_computation | loop fusion | flops 98304 | bytes 279040 | tf_op jit(solution)/shard_map/add | solution.py:402
  (1 shorter events, 0.0 us)
Async XLA Ops:
  19.6 15.9 %all-to-all-start = ((f32[8,72,256]{2,1,0:T(8,128)}), f32[8,72,256]{2,1,0:T(8,128)S(1)}, u32[]{:S(2)}, u32[]{:S(2)}) async-start(f32[8,72,256]{2,1,0:T(8,128)} %get-tuple-element.29), calls=%async_computation | async-start | bytes 1179648 | tf_op jit(solution)/shard_map/all_to_all | solution.py:365
  35.5 10.4 %collective-permute-start = (f32[8,72,256]{2,1,0:T(8,128)S(1)}, f32[8,72,256]{2,1,0:T(8,128)S(1)}, u32[]{:S(2)}, u32[]{:S(2)}) collective-permute-start(f32[8,72,256]{2,1,0:T(8,128)S(1)} %all-to-all-done.own_ref), channel_id=1, source_target_pairs={{0,1},{1,0},{2,3},{3,2},{4,5},{5,4},{6,7},{7,6},{8,9},{9,8},{10,11... | collective-permute-start | bytes 1769480 | tf_op jit(solution)/shard_map/ppermute | solution.py:362
  36.1 6.0 %collective-permute-start.1 = (f32[128,256]{1,0:T(8,128)}, f32[128,256]{1,0:T(8,128)S(1)}, u32[]{:S(2)}, u32[]{:S(2)}) collective-permute-start(f32[128,256]{1,0:T(8,128)} %get-tuple-element.45), channel_id=1, source_target_pairs={{0,2},{1,3},{2,0},{3,1},{4,6},{5,7},{6,4},{7,5},{8,10},{9,11},{10,... | collective-permute-start | bytes 393224 | tf_op jit(solution)/shard_map/ppermute | solution.py:362
  37.8 8.2 %collective-permute-start.2 = (f32[128,256]{1,0:T(8,128)}, f32[128,256]{1,0:T(8,128)S(1)}, u32[]{:S(2)}, u32[]{:S(2)}) collective-permute-start(f32[128,256]{1,0:T(8,128)} %get-tuple-element.46), channel_id=1, source_target_pairs={{0,4},{1,5},{2,6},{3,7},{4,0},{5,1},{6,2},{7,3},{8,12},{9,13},{10,... | collective-permute-start | bytes 393224 | tf_op jit(solution)/shard_map/ppermute | solution.py:362
  39.3 9.0 %collective-permute-start.3 = (f32[128,256]{1,0:T(8,128)}, f32[128,256]{1,0:T(8,128)S(1)}, u32[]{:S(2)}, u32[]{:S(2)}) collective-permute-start(f32[128,256]{1,0:T(8,128)} %get-tuple-element.47), channel_id=1, source_target_pairs={{0,6},{1,7},{2,4},{3,5},{4,2},{5,3},{6,0},{7,1},{8,14},{9,15},{10,... | collective-permute-start | bytes 393224 | tf_op jit(solution)/shard_map/ppermute | solution.py:362
  39.6 8.7 %collective-permute-start.4 = (f32[128,256]{1,0:T(8,128)}, f32[128,256]{1,0:T(8,128)S(1)}, u32[]{:S(2)}, u32[]{:S(2)}) collective-permute-start(f32[128,256]{1,0:T(8,128)} %get-tuple-element.48), channel_id=1, source_target_pairs={{0,3},{1,2},{2,1},{3,0},{4,7},{5,6},{6,5},{7,4},{8,11},{9,10},{10,... | collective-permute-start | bytes 393224 | tf_op jit(solution)/shard_map/ppermute | solution.py:362
  42.1 6.9 %collective-permute-start.5 = (f32[128,256]{1,0:T(8,128)}, f32[128,256]{1,0:T(8,128)S(1)}, u32[]{:S(2)}, u32[]{:S(2)}) collective-permute-start(f32[128,256]{1,0:T(8,128)} %get-tuple-element.49), channel_id=1, source_target_pairs={{0,5},{1,4},{2,7},{3,6},{4,1},{5,0},{6,3},{7,2},{8,13},{9,12},{10,... | collective-permute-start | bytes 393224 | tf_op jit(solution)/shard_map/ppermute | solution.py:362
  46.0 6.0 %collective-permute-start.6 = (f32[128,256]{1,0:T(8,128)}, f32[128,256]{1,0:T(8,128)S(1)}, u32[]{:S(2)}, u32[]{:S(2)}) collective-permute-start(f32[128,256]{1,0:T(8,128)} %get-tuple-element.50), channel_id=1, source_target_pairs={{0,7},{1,6},{2,5},{3,4},{4,3},{5,2},{6,1},{7,0},{8,15},{9,14},{10,... | collective-permute-start | bytes 393224 | tf_op jit(solution)/shard_map/ppermute | solution.py:362
  46.0 6.0 %collective-permute-start.7 = (f32[128,256]{1,0:T(8,128)}, f32[128,256]{1,0:T(8,128)S(1)}, u32[]{:S(2)}, u32[]{:S(2)}) collective-permute-start(f32[128,256]{1,0:T(8,128)} %get-tuple-element.51), channel_id=1, source_target_pairs={{0,1},{1,0},{2,3},{3,2},{4,5},{5,4},{6,7},{7,6},{8,9},{9,8},{10,11... | collective-permute-start | bytes 393224 | tf_op jit(solution)/shard_map/ppermute | solution.py:362
  52.0 0.9 %copy-start = (f32[128,256]{1,0:T(8,128)S(1)}, f32[128,256]{1,0:T(8,128)}, u32[]{:S(2)}) copy-start(f32[128,256]{1,0:T(8,128)} %get-tuple-element.44.refs_0_) | copy-start | bytes 393220
  57.6 5.4 %collective-permute-start.8 = (f32[8,256]{1,0:T(8,128)S(1)}, f32[8,256]{1,0:T(8,128)S(1)}, u32[]{:S(2)}, u32[]{:S(2)}) collective-permute-start(f32[8,256]{1,0:T(8,128)S(1)} %get-tuple-element.54), channel_id=1, source_target_pairs={{0,8},{8,16},{16,24},{24,0},{1,9},{9,17},{17,25},{25,1},{2,10},{10... | collective-permute-start | bytes 24584 | tf_op jit(solution)/shard_map/ppermute | solution.py:399
  59.2 3.9 %collective-permute-start.9 = (f32[8,256]{1,0:T(8,128)S(1)}, f32[8,256]{1,0:T(8,128)S(1)}, u32[]{:S(2)}, u32[]{:S(2)}) collective-permute-start(f32[8,256]{1,0:T(8,128)S(1)} %get-tuple-element.55), channel_id=1, source_target_pairs={{8,0},{16,8},{24,16},{0,24},{9,1},{17,9},{25,17},{1,25},{10,2},{18... | collective-permute-start | bytes 24584 | tf_op jit(solution)/shard_map/ppermute | solution.py:400

commit v5 on v3

--- a/solution.py
+++ b/solution.py
@@ -111,7 +111,9 @@
 BATCH = 16
 
 
-def solve_kernel(members, sizes_ref, glue_ref, far_ref, p_ref, out_ref, rest, f_ref, square_sems, corner_sems, strip_sems, panel_sem):
+def solve_kernel(members, place_ref, sizes_ref, glue_ref, far_ref, p_ref, *refs):
+    out_refs = refs[:members]
+    rest, f_ref, square_sems, corner_sems, strip_sems, panel_sem = refs[members:]
     subs, order, width = p_ref.shape
     wide = 2 * STRIDE
     square_copies, corner_copies, strip_copies = {}, {}, {}
@@ -195,22 +197,23 @@
         owners = (iota((members, width), 0) == owner)
         ranks = mm(owners.astype(BF), before)
         rank = jnp.sum(jnp.where(owners, ranks, 0.0), axis=0, keepdims=True).astype(jnp.int32)
-        target = owner * capacity + rank
+        target = (owner ^ place_ref[0]) * capacity + rank
         dispatch = (iota((members * capacity, width), 0) == target).astype(BF)
         values = mm(dispatch, dh) + mm(dispatch, dl)
         for k in range(members):
-            out_ref[k, s * capacity:(s + 1) * capacity] = values[k * capacity:(k + 1) * capacity]
-
-def solve(factors, panels, sizes, glue, members):
+            out_refs[k][s * capacity:(s + 1) * capacity] = values[k * capacity:(k + 1) * capacity]
+
+def solve(place, sizes, glue, factors, panels, members):
     subs, order, width = panels.shape
     capacity = 2 * width // members
     vm = pl.BlockSpec(memory_space=pltpu.VMEM)
+    sm = pl.BlockSpec(memory_space=pltpu.SMEM)
     far = pl.BlockSpec(memory_space=pltpu.HBM)
     return pl.pallas_call(
         functools.partial(solve_kernel, members),
-        out_shape=jax.ShapeDtypeStruct((members, subs * capacity, width), F32),
-        in_specs=[pl.BlockSpec(memory_space=pltpu.SMEM), vm, far, far],
-        out_specs=vm,
+        out_shape=[jax.ShapeDtypeStruct((subs * capacity, width), F32)] * members,
+        in_specs=[sm, sm, vm, far, far],
+        out_specs=[vm] * members,
         scratch_shapes=[
             pltpu.VMEM((subs, order, width), F32),
             pltpu.VMEM((subs, order, order), F32),
@@ -220,9 +223,9 @@
             pltpu.SemaphoreType.DMA,
         ],
         compiler_params=pltpu.CompilerParams(vmem_limit_bytes=54 << 20),
-        cost_estimate=pl.CostEstimate(flops=10_000_000_000, bytes_accessed=12 << 20, transcendentals=0),
+        cost_estimate=pl.CostEstimate(flops=10_000_000_000, bytes_accessed=8 << 20, transcendentals=0),
         name="solve",
-    )(sizes, glue, factors, panels)
+    )(place, sizes, glue, factors, panels)
 
 
 def pack_kernel(loads_ref, glue_ref, out_ref):
@@ -243,18 +246,15 @@
     slots = label_ref.shape[1]
     capacity = slots // subs
     first_core = place_ref[0] % 2 == 0
-    halves = (
-        jnp.where(first_core, own_ref[...], twin_ref[...]),
-        jnp.where(first_core, twin_ref[...], own_ref[...]),
-    )
     glue = []
     for k in range(members):
+        source = place_ref[0] ^ k
+        pair = own_ref[source], twin_ref[source]
         for part in range(2):
-            row = k * share + part * half
-            load = split(halves[part][k, :half])
-            high_ref[row:row + half] = load[0]
-            low_ref[row:row + half] = load[1]
-            glue.append(halves[part][k, half:half + lines])
+            got = jnp.where(first_core, pair[part], pair[1 - part])
+            row = pl.ds(pl.multiple_of(source * share + part * half, half), half)
+            high_ref[row], low_ref[row] = split(got[:half])
+            glue.append(got[half:half + lines])
     glue = jnp.concatenate(glue, axis=0)
     stand_ref[...] = glue.T.astype(jnp.int32)
     glue = glue.astype(jnp.int32)
@@ -276,24 +276,33 @@
     label_ref[...] = jnp.concatenate(labels, axis=0).astype(jnp.int32)
 
 
-def finish_kernel(subs, values_ref, label_ref, stand_ref, high_ref, low_ref, dual_ref, raw_ref, first_ref, last_ref):
-    members, slots, width = values_ref.shape
-    share, nrhs = raw_ref.shape
+def placed(subs, sources, label_ref, stand_ref, values):
+    slots, width = values[0].shape
+    share = NDUAL // label_ref.shape[0]
     total = jnp.zeros((2 * share, NDUAL), F32)
-    for k in range(members):
+    for k, value in zip(sources, values):
         rows = (iota((subs * share, slots), 0) == label_ref[k:k + 1]).astype(BF)
-        moved = mm(rows, jnp.concatenate(split(values_ref[k]), axis=1)).astype(BF)
+        moved = mm(rows, jnp.concatenate(split(value[...]), axis=1)).astype(BF)
         for s in range(subs):
             i = k * subs + s
             part = moved[s * share:(s + 1) * share]
             columns = (iota((width, NDUAL), 1) == stand_ref[:, i:i + 1]).astype(BF)
             total = total + mm(jnp.concatenate([part[:, :width], part[:, width:]], axis=0), columns)
-    dual = total[:share] + total[share:]
+    return total[:share] + total[share:]
+
+
+def early_kernel(subs, sources, label_ref, stand_ref, *refs):
+    refs[-1][...] = placed(subs, sources, label_ref, stand_ref, refs[:-1])
+
+
+def finish_kernel(subs, sources, label_ref, stand_ref, high_ref, low_ref, early_ref, *refs):
+    values, (dual_ref, raw_ref, first_ref, last_ref) = refs[:-4], refs[-4:]
+    dual = early_ref[...] + placed(subs, sources, label_ref, stand_ref, values)
     dual_ref[...] = dual
     raw = mm3(split(dual), (high_ref[...], low_ref[...]))
     raw_ref[...] = raw
     first_ref[...] = raw[:IFACE]
-    last_ref[...] = raw[share - IFACE:]
+    last_ref[...] = raw[raw.shape[0] - IFACE:]
 
 
 def call(kernel, outs, args, flops, name, smem=0, grant=16):
@@ -318,11 +327,18 @@
     slots = subs * capacity
     count = members * subs
     shape = jax.ShapeDtypeStruct
+    place = lax.axis_index("member").astype(jnp.int32).reshape(1)
+
+    def across(value, distance):
+        return lax.ppermute(value, "member", [(i, i ^ distance) for i in range(members)])
+
     packed = call(pack_kernel, shape((members, share // 2 + 8 * (-(-subs // 16)), nrhs), F32), (loads, glue_index), 1_000_000, "pack", grant=58)
     own = lax.all_to_all(packed, "member", split_axis=0, concat_axis=0, tiled=True)
-    values = solve(factors, panels, sizes, glue_index, members)
-    twin = lax.ppermute(own, "member", [(i, i ^ 1) for i in range(members)])
-    place = lax.axis_index("member").astype(jnp.int32).reshape(1)
+    values = solve(place, sizes, glue_index, factors, panels, members)
+    own, *values = lax.optimization_barrier((own, *values))
+    arrivals = (0, *range(2, members, 2), *range(3, members, 2), 1)
+    arrived = [across(values[k], k) if k else values[k] for k in arrivals]
+    twin = across(own, 1)
     stand, labels, high, low = call(
         functools.partial(routes_kernel, subs),
         (
@@ -336,17 +352,24 @@
         "routes",
         smem=1,
     )
-    values = lax.all_to_all(values, "member", split_axis=0, concat_axis=0, tiled=True)
+    half = members // 2
+    early = call(
+        functools.partial(early_kernel, subs, arrivals[:half]),
+        shape((share, NDUAL), F32),
+        (labels, stand, *arrived[:half]),
+        2_000_000_000,
+        "early",
+    )
     dual_rows, raw, first, last = call(
-        functools.partial(finish_kernel, subs),
+        functools.partial(finish_kernel, subs, arrivals[half:]),
         (
             shape((share, NDUAL), F32),
             shape((share, nrhs), F32),
             shape((IFACE, nrhs), F32),
             shape((IFACE, nrhs), F32),
         ),
-        (values, labels, stand, high, low),
-        5_000_000_000,
+        (labels, stand, high, low, early, *arrived[half:]),
+        3_000_000_000,
         "finish",
     )
     peers = lax.axis_size("cluster")

time: 49.7 us -> 44.4 us (0.89)
  waiting for transfers between devices: 15.7 us -> 6.69 us
  starting transfers between devices: 13.7 us -> 16.6 us
  local copies, waits for them, and re-layouts: 0.08 us -> 0.98 us
    all_to_all x1 -> x0, waiting for transfers between devices: 12.4 us -> none  [on_device(): lax.all_to_all(values, 'member', split_axis=0, concat_axis=0, tiled=True)]
    ppermute x1 -> x8, starting transfers between devices: 0.51 us -> 7.56 us  [across(): lax.ppermute(value, 'member', [(i, i ^ distance) for i in range(members)])]
    all_to_all x1 -> x0, starting transfers between devices: 4.21 us -> none  [on_device(): lax.all_to_all(values, 'member', split_axis=0, concat_axis=0, tiled=True)]
    ppermute x1 -> x8, waiting for transfers between devices: 1.68 us -> 5.14 us  [across(): lax.ppermute(value, 'member', [(i, i ^ distance) for i in range(members)])]
    unnamed x0 -> x2, local copies, waits for them, and re-layouts: none -> 0.9 us
    pallas_call x3 -> x4, Pallas kernels: 7.3 us -> 7.38 us  [call(): pl.pallas_call(kernel, out_shape=outs, in_specs=specs, out_specs=jax.tree...]
  transfers between devices with their start and end apart: 5 -> 11, of which waited for: 3 -> 4; matrix products, arithmetic and copies ran while one was open for 0% -> 0% of each run, Pallas kernels for 24% -> 31%
where the time goes in v5:
time: 44.4 us; the launch traced here: 44.2 us
  Pallas kernels  18.5 us (42%)
  starting transfers between devices  16.6 us (37%)
  waiting for transfers between devices  6.69 us (15%)
  local copies, waits for them, and re-layouts  0.98 us (2%)
  other arithmetic  0.74 us (2%)
  between operations  0.68 us (2%)
    pallas_call x1, Pallas kernels, solve(): pl.pallas_call(functools.partial(solve_kernel, members), out_shape=[jax.S...  11.1 us
    ppermute x8, starting transfers between devices, across(): lax.ppermute(value, 'member', [(i, i ^ distance) for i in range(members)])  7.56 us
    pallas_call x4, Pallas kernels, call(): pl.pallas_call(kernel, out_shape=outs, in_specs=specs, out_specs=jax.tree...  7.38 us
    all_to_all x1, starting transfers between devices, on_device(): lax.all_to_all(packed, 'member', split_axis=0, concat_axis=0, tiled=True)  5.17 us
    ppermute x8, waiting for transfers between devices, across(): lax.ppermute(value, 'member', [(i, i ^ distance) for i in range(members)])  5.14 us
    ppermute x1, starting transfers between devices, on_device(): after = lax.ppermute(first, 'cluster', down)  2.25 us
    ppermute x1, starting transfers between devices, on_device(): before = lax.ppermute(last, 'cluster', up)  1.58 us
    ppermute x1, waiting for transfers between devices, on_device(): before = lax.ppermute(last, 'cluster', up)  1.54 us
  transfers between devices with their start and end apart: 11, of which 4 were waited for; matrix products, arithmetic and copies ran while one was open for 0% of the time, Pallas kernels for 31%

profile of v5, /device:TPU:0, one launch (start us, length us, event | category | flops | bytes accessed | tf_op | source)
XLA Modules:
  0.0 44.2 jit_solution(7556138695430505825)
XLA Ops:
  0.6 1.8 %pack.1 = f32[8,72,256]{2,1,0:T(8,128)} custom-call(f32[128,256]{1,0:T(8,128)} %loads_ref.1, s32[2,256]{1,0:T(2,128)} %glue_ref.3), custom_call_target="tpu_custom_call" | custom-call | flops 1000000 | bytes 4194304 | tf_op jit(solution)/shard_map/pack/pallas_call | solution.py:311
  2.4 5.2 %all-to-all-start = ((f32[8,72,256]{2,1,0:T(8,128)}), f32[8,72,256]{2,1,0:T(8,128)S(1)}, u32[]{:S(2)}, u32[]{:S(2)}) async-start(f32[8,72,256]{2,1,0:T(8,128)} %pack.1), calls=%async_computation | async-start | bytes 1179648 | tf_op jit(solution)/shard_map/all_to_all | solution.py:336
  7.6 11.1 %solve.1 = (f32[128,256]{1,0:T(8,128)}, f32[128,256]{1,0:T(8,128)}, f32[128,256]{1,0:T(8,128)}, f32[128,256]{1,0:T(8,128)}, f32[128,256]{1,0:T(8,128)}, /*index=...) custom-call(s32[1]{0:T(128)} %bitcast.place_ref, s32[2]{0:T(128)} %sizes_ref.1, s32[2,256]{1,0:T(2,128)} %glue_ref.3, ...), custom_call_target="tpu_custom_call" | custom-call | flops 10000000000 | bytes 8388608 | tf_op jit(solution)/shard_map/solve/pallas_call | solution.py:212
  18.7 0.0 all-to-all-done.own_ref
  18.7 0.6 %collective-permute-start = (f32[8,72,256]{2,1,0:T(8,128)S(1)}, f32[8,72,256]{2,1,0:T(8,128)S(1)}, u32[]{:S(2)}, u32[]{:S(2)}) collective-permute-start(f32[8,72,256]{2,1,0:T(8,128)S(1)} %all-to-all-done.own_ref), channel_id=1, source_target_pairs={{0,1},{1,0},{2,3},{3,2},{4,5},{5,4},{6,7},{7,6},{8,9},{9,8},{10,11... | collective-permute-start | bytes 1769480 | tf_op jit(solution)/shard_map/ppermute | solution.py:333
  19.3 1.7 %collective-permute-start.1 = (f32[128,256]{1,0:T(8,128)}, f32[128,256]{1,0:T(8,128)S(1)}, u32[]{:S(2)}, u32[]{:S(2)}) collective-permute-start(f32[128,256]{1,0:T(8,128)} %get-tuple-element.41), channel_id=1, source_target_pairs={{0,2},{1,3},{2,0},{3,1},{4,6},{5,7},{6,4},{7,5},{8,10},{9,11},{10,... | collective-permute-start | bytes 393224 | tf_op jit(solution)/shard_map/ppermute | solution.py:333
  21.0 1.5 %collective-permute-start.2 = (f32[128,256]{1,0:T(8,128)}, f32[128,256]{1,0:T(8,128)S(1)}, u32[]{:S(2)}, u32[]{:S(2)}) collective-permute-start(f32[128,256]{1,0:T(8,128)} %get-tuple-element.42), channel_id=1, source_target_pairs={{0,4},{1,5},{2,6},{3,7},{4,0},{5,1},{6,2},{7,3},{8,12},{9,13},{10,... | collective-permute-start | bytes 393224 | tf_op jit(solution)/shard_map/ppermute | solution.py:333
  22.4 0.3 collective-permute-start.3
  22.8 0.8 %collective-permute-start.4 = (f32[128,256]{1,0:T(8,128)}, f32[128,256]{1,0:T(8,128)S(1)}, u32[]{:S(2)}, u32[]{:S(2)}) collective-permute-start(f32[128,256]{1,0:T(8,128)} %get-tuple-element.44), channel_id=1, source_target_pairs={{0,3},{1,2},{2,1},{3,0},{4,7},{5,6},{6,5},{7,4},{8,11},{9,10},{10,... | collective-permute-start | bytes 393224 | tf_op jit(solution)/shard_map/ppermute | solution.py:333
  23.6 0.0 collective-permute-done.twin_ref
  23.6 2.1 %collective-permute-start.5 = (f32[128,256]{1,0:T(8,128)}, f32[128,256]{1,0:T(8,128)S(1)}, u32[]{:S(2)}, u32[]{:S(2)}) collective-permute-start(f32[128,256]{1,0:T(8,128)} %get-tuple-element.45), channel_id=1, source_target_pairs={{0,5},{1,4},{2,7},{3,6},{4,1},{5,0},{6,3},{7,2},{8,13},{9,12},{10,... | collective-permute-start | bytes 393224 | tf_op jit(solution)/shard_map/ppermute | solution.py:333
  25.6 0.7 %routes.1 = (s32[256,16]{1,0:T(8,128)S(1)}, s32[8,128]{1,0:T(8,128)S(1)}, bf16[1024,256]{1,0:T(8,128)(2,1)S(1)}, bf16[1024,256]{1,0:T(8,128)(2,1)S(1)}) custom-call(s32[1]{0:T(128)} %bitcast.place_ref, f32[8,72,256]{2,1,0:T(8,128)S(1)} %all-to-all-done.own_ref, f32[8,72,256]{2,1,0:T(8,128)S(1)} %collective-permute-done.twin_ref), custom_call_target="tpu_custom_call" | custom-call | flops 2000000000 | bytes 4194304 | tf_op jit(solution)/shard_map/routes/pallas_call | solution.py:311
  26.4 0.0 collective-permute-done.1.refs_1_
  26.4 0.6 %collective-permute-start.6 = (f32[128,256]{1,0:T(8,128)}, f32[128,256]{1,0:T(8,128)S(1)}, u32[]{:S(2)}, u32[]{:S(2)}) collective-permute-start(f32[128,256]{1,0:T(8,128)} %get-tuple-element.46), channel_id=1, source_target_pairs={{0,7},{1,6},{2,5},{3,4},{4,3},{5,2},{6,1},{7,0},{8,15},{9,14},{10,... | collective-permute-start | bytes 393224 | tf_op jit(solution)/shard_map/ppermute | solution.py:333
  27.0 2.3 %collective-permute-done.2.refs_2_ = f32[128,256]{1,0:T(8,128)S(1)} collective-permute-done((f32[128,256]{1,0:T(8,128)}, f32[128,256]{1,0:T(8,128)S(1)}, u32[]{:S(2)}, u32[]{:S(2)}) %collective-permute-start.2) | collective-permute-done | bytes 131104 | tf_op jit(solution)/shard_map/ppermute | solution.py:333
  29.3 0.0 collective-permute-start.7
  29.3 0.7 %collective-permute-done.3.refs_3_ = f32[128,256]{1,0:T(8,128)S(1)} collective-permute-done((f32[128,256]{1,0:T(8,128)}, f32[128,256]{1,0:T(8,128)S(1)}, u32[]{:S(2)}, u32[]{:S(2)}) %collective-permute-start.3) | collective-permute-done | bytes 131104 | tf_op jit(solution)/shard_map/ppermute | solution.py:333
  30.0 0.0 copy-start
  30.0 0.9 %copy-done = f32[128,256]{1,0:T(8,128)S(1)} copy-done((f32[128,256]{1,0:T(8,128)S(1)}, f32[128,256]{1,0:T(8,128)}, u32[]{:S(2)}) %copy-start) | copy-done | bytes 131096
  30.9 1.9 %early.1.early_ref = f32[128,1024]{1,0:T(8,128)S(1)} custom-call(s32[8,128]{1,0:T(8,128)S(1)} %get-tuple-element.36.label_ref, s32[256,16]{1,0:T(8,128)S(1)} %get-tuple-element.37.stand_ref, f32[128,256]{1,0:T(8,128)S(1)} %copy-done, f32[128,256]{1,0:T(8,128)S(1)} %collective-permute-done.1.refs_1_, f32[128,256]{1,0:T(8,128)S(1)} %collective-permute-done.2.refs_2_, ...), custom_call_target="tpu_custom_call" | custom-call | flops 2000000000 | bytes 4194304 | tf_op jit(solution)/shard_map/early/pallas_call | solution.py:311
  32.8 0.0 collective-permute-done.4.refs_0_
  32.8 2.1 %collective-permute-done.5.refs_1_ = f32[128,256]{1,0:T(8,128)S(1)} collective-permute-done((f32[128,256]{1,0:T(8,128)}, f32[128,256]{1,0:T(8,128)S(1)}, u32[]{:S(2)}, u32[]{:S(2)}) %collective-permute-start.5) | collective-permute-done | bytes 131104 | tf_op jit(solution)/shard_map/ppermute | solution.py:333
  35.0 0.0 collective-permute-done.6.refs_2_
  35.0 0.0 collective-permute-done.7.refs_3_
  35.0 3.0 %finish.1 = (f32[128,1024]{1,0:T(8,128)}, f32[128,256]{1,0:T(8,128)S(1)}, f32[8,256]{1,0:T(8,128)S(1)}, f32[8,256]{1,0:T(8,128)S(1)}) custom-call(s32[8,128]{1,0:T(8,128)S(1)} %get-tuple-element.36.label_ref, s32[256,16]{1,0:T(8,128)S(1)} %get-tuple-element.37.stand_ref, bf16[1024,256]{1,0:T(8,128)(2,1)S(1)} %get-tuple-element.38.high_ref, ...), custom_call_target="tpu_custom_call" | custom-call | flops 3000000000 | bytes 4194304 | tf_op jit(solution)/shard_map/finish/pallas_call | solution.py:311
  38.0 1.6 %collective-permute-start.8 = (f32[8,256]{1,0:T(8,128)S(1)}, f32[8,256]{1,0:T(8,128)S(1)}, u32[]{:S(2)}, u32[]{:S(2)}) collective-permute-start(f32[8,256]{1,0:T(8,128)S(1)} %get-tuple-element.50), channel_id=1, source_target_pairs={{0,8},{8,16},{16,24},{24,0},{1,9},{9,17},{17,25},{25,1},{2,10},{10... | collective-permute-start | bytes 24584 | tf_op jit(solution)/shard_map/ppermute | solution.py:378
  39.5 2.2 %collective-permute-start.9 = (f32[8,256]{1,0:T(8,128)S(1)}, f32[8,256]{1,0:T(8,128)S(1)}, u32[]{:S(2)}, u32[]{:S(2)}) collective-permute-start(f32[8,256]{1,0:T(8,128)S(1)} %get-tuple-element.51), channel_id=1, source_target_pairs={{8,0},{16,8},{24,16},{0,24},{9,1},{17,9},{25,17},{1,25},{10,2},{18... | collective-permute-start | bytes 24584 | tf_op jit(solution)/shard_map/ppermute | solution.py:379
  41.8 0.1 pad.1.clone
  41.9 1.5 %collective-permute-done.8 = f32[8,256]{1,0:T(8,128)S(1)} collective-permute-done((f32[8,256]{1,0:T(8,128)S(1)}, f32[8,256]{1,0:T(8,128)S(1)}, u32[]{:S(2)}, u32[]{:S(2)}) %collective-permute-start.8) | collective-permute-done | bytes 8224 | tf_op jit(solution)/shard_map/ppermute | solution.py:378
  43.4 0.0 collective-permute-done.9
  43.4 0.7 %maximum_add_fusion = f32[128,256]{1,0:T(8,128)} fusion(f32[128,256]{1,0:T(8,128)S(1)} %get-tuple-element.49, f32[8,256]{1,0:T(8,128)S(1)} %collective-permute-done.9, f32[8,256]{1,0:T(8,128)S(1)} %collective-permute-done.8, f32[128]{0:T(128)S(1)} %pad.1.clone), kind=kLoop, calls=%fused_computation | loop fusion | flops 98304 | bytes 279040 | tf_op jit(solution)/shard_map/add | solution.py:381
  (1 shorter events, 0.0 us)
Async XLA Ops:
  2.4 16.3 %all-to-all-start = ((f32[8,72,256]{2,1,0:T(8,128)}), f32[8,72,256]{2,1,0:T(8,128)S(1)}, u32[]{:S(2)}, u32[]{:S(2)}) async-start(f32[8,72,256]{2,1,0:T(8,128)} %pack.1), calls=%async_computation | async-start | bytes 1179648 | tf_op jit(solution)/shard_map/all_to_all | solution.py:336
  18.7 4.9 %collective-permute-start = (f32[8,72,256]{2,1,0:T(8,128)S(1)}, f32[8,72,256]{2,1,0:T(8,128)S(1)}, u32[]{:S(2)}, u32[]{:S(2)}) collective-permute-start(f32[8,72,256]{2,1,0:T(8,128)S(1)} %all-to-all-done.own_ref), channel_id=1, source_target_pairs={{0,1},{1,0},{2,3},{3,2},{4,5},{5,4},{6,7},{7,6},{8,9},{9,8},{10,11... | collective-permute-start | bytes 1769480 | tf_op jit(solution)/shard_map/ppermute | solution.py:333
  19.3 7.1 %collective-permute-start.1 = (f32[128,256]{1,0:T(8,128)}, f32[128,256]{1,0:T(8,128)S(1)}, u32[]{:S(2)}, u32[]{:S(2)}) collective-permute-start(f32[128,256]{1,0:T(8,128)} %get-tuple-element.41), channel_id=1, source_target_pairs={{0,2},{1,3},{2,0},{3,1},{4,6},{5,7},{6,4},{7,5},{8,10},{9,11},{10,... | collective-permute-start | bytes 393224 | tf_op jit(solution)/shard_map/ppermute | solution.py:333
  21.0 8.3 %collective-permute-start.2 = (f32[128,256]{1,0:T(8,128)}, f32[128,256]{1,0:T(8,128)S(1)}, u32[]{:S(2)}, u32[]{:S(2)}) collective-permute-start(f32[128,256]{1,0:T(8,128)} %get-tuple-element.42), channel_id=1, source_target_pairs={{0,4},{1,5},{2,6},{3,7},{4,0},{5,1},{6,2},{7,3},{8,12},{9,13},{10,... | collective-permute-start | bytes 393224 | tf_op jit(solution)/shard_map/ppermute | solution.py:333
  22.4 7.5 %collective-permute-start.3 = (f32[128,256]{1,0:T(8,128)}, f32[128,256]{1,0:T(8,128)S(1)}, u32[]{:S(2)}, u32[]{:S(2)}) collective-permute-start(f32[128,256]{1,0:T(8,128)} %get-tuple-element.43), channel_id=1, source_target_pairs={{0,6},{1,7},{2,4},{3,5},{4,2},{5,3},{6,0},{7,1},{8,14},{9,15},{10,... | collective-permute-start | bytes 393224 | tf_op jit(solution)/shard_map/ppermute | solution.py:333
  22.8 10.0 %collective-permute-start.4 = (f32[128,256]{1,0:T(8,128)}, f32[128,256]{1,0:T(8,128)S(1)}, u32[]{:S(2)}, u32[]{:S(2)}) collective-permute-start(f32[128,256]{1,0:T(8,128)} %get-tuple-element.44), channel_id=1, source_target_pairs={{0,3},{1,2},{2,1},{3,0},{4,7},{5,6},{6,5},{7,4},{8,11},{9,10},{10,... | collective-permute-start | bytes 393224 | tf_op jit(solution)/shard_map/ppermute | solution.py:333
  23.6 11.4 %collective-permute-start.5 = (f32[128,256]{1,0:T(8,128)}, f32[128,256]{1,0:T(8,128)S(1)}, u32[]{:S(2)}, u32[]{:S(2)}) collective-permute-start(f32[128,256]{1,0:T(8,128)} %get-tuple-element.45), channel_id=1, source_target_pairs={{0,5},{1,4},{2,7},{3,6},{4,1},{5,0},{6,3},{7,2},{8,13},{9,12},{10,... | collective-permute-start | bytes 393224 | tf_op jit(solution)/shard_map/ppermute | solution.py:333
  26.4 8.6 %collective-permute-start.6 = (f32[128,256]{1,0:T(8,128)}, f32[128,256]{1,0:T(8,128)S(1)}, u32[]{:S(2)}, u32[]{:S(2)}) collective-permute-start(f32[128,256]{1,0:T(8,128)} %get-tuple-element.46), channel_id=1, source_target_pairs={{0,7},{1,6},{2,5},{3,4},{4,3},{5,2},{6,1},{7,0},{8,15},{9,14},{10,... | collective-permute-start | bytes 393224 | tf_op jit(solution)/shard_map/ppermute | solution.py:333
  29.3 5.7 %collective-permute-start.7 = (f32[128,256]{1,0:T(8,128)}, f32[128,256]{1,0:T(8,128)S(1)}, u32[]{:S(2)}, u32[]{:S(2)}) collective-permute-start(f32[128,256]{1,0:T(8,128)} %get-tuple-element.47), channel_id=1, source_target_pairs={{0,1},{1,0},{2,3},{3,2},{4,5},{5,4},{6,7},{7,6},{8,9},{9,8},{10,11... | collective-permute-start | bytes 393224 | tf_op jit(solution)/shard_map/ppermute | solution.py:333
  30.0 0.9 %copy-start = (f32[128,256]{1,0:T(8,128)S(1)}, f32[128,256]{1,0:T(8,128)}, u32[]{:S(2)}) copy-start(f32[128,256]{1,0:T(8,128)} %get-tuple-element.40.refs_0_) | copy-start | bytes 393220
  38.0 5.4 %collective-permute-start.8 = (f32[8,256]{1,0:T(8,128)S(1)}, f32[8,256]{1,0:T(8,128)S(1)}, u32[]{:S(2)}, u32[]{:S(2)}) collective-permute-start(f32[8,256]{1,0:T(8,128)S(1)} %get-tuple-element.50), channel_id=1, source_target_pairs={{0,8},{8,16},{16,24},{24,0},{1,9},{9,17},{17,25},{25,1},{2,10},{10... | collective-permute-start | bytes 24584 | tf_op jit(solution)/shard_map/ppermute | solution.py:378
  39.5 3.9 %collective-permute-start.9 = (f32[8,256]{1,0:T(8,128)S(1)}, f32[8,256]{1,0:T(8,128)S(1)}, u32[]{:S(2)}, u32[]{:S(2)}) collective-permute-start(f32[8,256]{1,0:T(8,128)S(1)} %get-tuple-element.51), channel_id=1, source_target_pairs={{8,0},{16,8},{24,16},{0,24},{9,1},{17,9},{25,17},{1,25},{10,2},{18... | collective-permute-start | bytes 24584 | tf_op jit(solution)/shard_map/ppermute | solution.py:379

commit v6 on v5

--- a/solution.py
+++ b/solution.py
@@ -111,9 +111,12 @@
 BATCH = 16
 
 
-def solve_kernel(members, place_ref, sizes_ref, glue_ref, far_ref, p_ref, *refs):
+def solve_kernel(members, far_sizes_ref, far_glue_ref, far_ref, p_ref, *refs):
     out_refs = refs[:members]
-    rest, f_ref, square_sems, corner_sems, strip_sems, panel_sem = refs[members:]
+    rest, f_ref, sizes_ref, glue_ref, square_sems, corner_sems, strip_sems, panel_sem, small_sems = refs[members:]
+    sizes_copy = pltpu.make_async_copy(far_sizes_ref, sizes_ref, small_sems.at[0])
+    glue_copy = pltpu.make_async_copy(far_glue_ref, glue_ref, small_sems.at[1])
+    sizes_copy.start()
     subs, order, width = p_ref.shape
     wide = 2 * STRIDE
     square_copies, corner_copies, strip_copies = {}, {}, {}
@@ -132,9 +135,11 @@
             corner_copies[s, a] = fetch(s, pl.ds(a + STRIDE, STRIDE), pl.ds(a, STRIDE), corner_sems.at[s, step])
     panel_copy = pltpu.make_async_copy(p_ref, rest, panel_sem)
     panel_copy.start()
+    glue_copy.start()
     for step, a in enumerate(range(0, order - wide, wide)):
         for s in range(subs):
             strip_copies[s, a] = fetch(s, pl.ds(a + wide, order - a - wide), pl.ds(a, wide), strip_sems.at[s, step])
+    sizes_copy.wait()
     row = iota((STRIDE, STRIDE), 0)
     col = iota((STRIDE, STRIDE), 1)
     prow = iota((wide, width), 0)
@@ -170,6 +175,19 @@
             for u, t, l in zip(above, turned, below)
         ]
 
+    capacity = 2 * width // members
+    glue_copy.wait()
+    glue = glue_ref[...]
+    place = lax.axis_index("member")
+    before = (iota((width, width), 0) < iota((width, width), 1)).astype(BF)
+    dispatches = []
+    for s in range(subs):
+        owner = glue[s:s + 1] // (NDUAL // members)
+        owners = (iota((members, width), 0) == owner)
+        ranks = mm(owners.astype(BF), before)
+        rank = jnp.sum(jnp.where(owners, ranks, 0.0), axis=0, keepdims=True).astype(jnp.int32)
+        target = (owner ^ place) * capacity + rank
+        dispatches.append((iota((members * capacity, width), 0) == target).astype(BF))
     panel_copy.wait()
     for a in range(0, order, wide):
         solved = []
@@ -186,57 +204,87 @@
             hi, lo = solved[s]
             squares[s] = squares[s] + mm(hi, hi, dims)
             crosses[s] = crosses[s] + mm(hi, lo, dims)
-    capacity = 2 * width // members
-    glue = glue_ref[...]
-    before = (iota((width, width), 0) < iota((width, width), 1)).astype(BF)
-    dual_order = NDUAL
+    duals = [split(squares[s] + (crosses[s] + crosses[s].T)) for s in range(subs)]
     for s in range(subs):
-        dh, dl = split(squares[s] + (crosses[s] + crosses[s].T))
-        line = glue[s:s + 1]
-        owner = line // (dual_order // members)
-        owners = (iota((members, width), 0) == owner)
-        ranks = mm(owners.astype(BF), before)
-        rank = jnp.sum(jnp.where(owners, ranks, 0.0), axis=0, keepdims=True).astype(jnp.int32)
-        target = (owner ^ place_ref[0]) * capacity + rank
-        dispatch = (iota((members * capacity, width), 0) == target).astype(BF)
-        values = mm(dispatch, dh) + mm(dispatch, dl)
+        values = mm(dispatches[s], duals[s][0]) + mm(dispatches[s], duals[s][1])
         for k in range(members):
             out_refs[k][s * capacity:(s + 1) * capacity] = values[k * capacity:(k + 1) * capacity]
 
-def solve(place, sizes, glue, factors, panels, members):
+
+def solve(sizes, glue, factors, panels, members):
     subs, order, width = panels.shape
     capacity = 2 * width // members
     vm = pl.BlockSpec(memory_space=pltpu.VMEM)
-    sm = pl.BlockSpec(memory_space=pltpu.SMEM)
     far = pl.BlockSpec(memory_space=pltpu.HBM)
     return pl.pallas_call(
         functools.partial(solve_kernel, members),
         out_shape=[jax.ShapeDtypeStruct((subs * capacity, width), F32)] * members,
-        in_specs=[sm, sm, vm, far, far],
+        in_specs=[far] * 4,
         out_specs=[vm] * members,
         scratch_shapes=[
             pltpu.VMEM((subs, order, width), F32),
             pltpu.VMEM((subs, order, order), F32),
+            pltpu.SMEM((subs,), jnp.int32),
+            pltpu.VMEM((subs, width), jnp.int32),
             pltpu.SemaphoreType.DMA((subs, order // STRIDE)),
             pltpu.SemaphoreType.DMA((subs, order // (2 * STRIDE))),
             pltpu.SemaphoreType.DMA((subs, order // (2 * STRIDE))),
             pltpu.SemaphoreType.DMA,
+            pltpu.SemaphoreType.DMA((2,)),
         ],
         compiler_params=pltpu.CompilerParams(vmem_limit_bytes=54 << 20),
         cost_estimate=pl.CostEstimate(flops=10_000_000_000, bytes_accessed=8 << 20, transcendentals=0),
         name="solve",
-    )(place, sizes, glue, factors, panels)
-
-
-def pack_kernel(loads_ref, glue_ref, out_ref):
+    )(sizes, glue, factors, panels)
+
+
+def pack_kernel(loads_ref, glue_ref, out_ref, held, lines_of, tail, in_sems, load_sems, tail_sems):
     members, rows, nrhs = out_ref.shape
     half, lines = loads_ref.shape[0] // 2, glue_ref.shape[0] // 2
+    labels = pltpu.make_async_copy(glue_ref, lines_of, in_sems.at[0])
+    load = pltpu.make_async_copy(loads_ref, held, in_sems.at[1])
+    labels.start()
+    load.start()
+    labels.wait()
     blank = jnp.zeros((rows - half - lines, nrhs), F32)
+    for part in range(2):
+        line = lines_of[part * lines:(part + 1) * lines].astype(F32)
+        tail[part] = jnp.concatenate([line, blank], axis=0)
+    copies = []
     for k in range(members):
-        part = k % 2
-        out_ref[k, :half] = loads_ref[part * half:(part + 1) * half]
-        line = glue_ref[part * lines:(part + 1) * lines].astype(F32)
-        out_ref[k, half:] = jnp.concatenate([line, blank], axis=0)
+        copies.append(pltpu.make_async_copy(tail.at[k % 2], out_ref.at[k, pl.ds(half, rows - half)], tail_sems.at[k]))
+        copies[-1].start()
+    load.wait()
+    for k in range(members):
+        rows_of = held.at[pl.ds(k % 2 * half, half)]
+        copies.append(pltpu.make_async_copy(rows_of, out_ref.at[k, pl.ds(0, half)], load_sems.at[k]))
+        copies[-1].start()
+    for copy in copies:
+        copy.wait()
+
+
+def pack(loads, glue, members):
+    subs = glue.shape[0]
+    share, nrhs = loads.shape
+    rows = share // 2 + 8 * (-(-subs // 16))
+    far = pl.BlockSpec(memory_space=pltpu.HBM)
+    return pl.pallas_call(
+        pack_kernel,
+        out_shape=jax.ShapeDtypeStruct((members, rows, nrhs), F32),
+        in_specs=[far, far],
+        out_specs=far,
+        scratch_shapes=[
+            pltpu.VMEM((share, nrhs), F32),
+            pltpu.VMEM(glue.shape, jnp.int32),
+            pltpu.VMEM((2, rows - share // 2, nrhs), F32),
+            pltpu.SemaphoreType.DMA((2,)),
+            pltpu.SemaphoreType.DMA((members,)),
+            pltpu.SemaphoreType.DMA((members,)),
+        ],
+        compiler_params=pltpu.CompilerParams(vmem_limit_bytes=58 << 20),
+        cost_estimate=pl.CostEstimate(flops=1_000_000, bytes_accessed=1 << 20, transcendentals=0),
+        name="pack",
+    )(loads, glue)
 
 
 def routes_kernel(subs, place_ref, own_ref, twin_ref, stand_ref, label_ref, high_ref, low_ref):
@@ -305,7 +353,7 @@
     last_ref[...] = raw[raw.shape[0] - IFACE:]
 
 
-def call(kernel, outs, args, flops, name, smem=0, grant=16):
+def call(kernel, outs, args, flops, name, smem=0):
     vm = pl.BlockSpec(memory_space=pltpu.VMEM)
     specs = [pl.BlockSpec(memory_space=pltpu.SMEM)] * smem + [vm] * (len(args) - smem)
     return pl.pallas_call(
@@ -313,7 +361,7 @@
         out_shape=outs,
         in_specs=specs,
         out_specs=jax.tree.map(lambda _: vm, outs),
-        compiler_params=pltpu.CompilerParams(vmem_limit_bytes=grant << 20),
+        compiler_params=pltpu.CompilerParams(vmem_limit_bytes=16 << 20),
         cost_estimate=pl.CostEstimate(flops=flops, bytes_accessed=4 << 20, transcendentals=0),
         name=name,
     )(*args)
@@ -332,9 +380,9 @@
     def across(value, distance):
         return lax.ppermute(value, "member", [(i, i ^ distance) for i in range(members)])
 
-    packed = call(pack_kernel, shape((members, share // 2 + 8 * (-(-subs // 16)), nrhs), F32), (loads, glue_index), 1_000_000, "pack", grant=58)
+    packed = pack(loads, glue_index, members)
     own = lax.all_to_all(packed, "member", split_axis=0, concat_axis=0, tiled=True)
-    values = solve(place, sizes, glue_index, factors, panels, members)
+    values = solve(sizes, glue_index, factors, panels, members)
     own, *values = lax.optimization_barrier((own, *values))
     arrivals = (0, *range(2, members, 2), *range(3, members, 2), 1)
     arrived = [across(values[k], k) if k else values[k] for k in arrivals]

time: 44.4 us -> 43.9 us (0.989)
  Pallas kernels: 18.5 us -> 18 us
    pallas_call x0 -> x1, Pallas kernels: none -> 1.9 us  [pack(): pl.pallas_call(pack_kernel, out_shape=jax.ShapeDtypeStruct((members, rows...]
    pallas_call x4 -> x3, Pallas kernels: 7.38 us -> 5.62 us  [call(): pl.pallas_call(kernel, out_shape=outs, in_specs=specs, out_specs=jax.tree...]
    pallas_call x1, Pallas kernels: 11.1 us -> 10.4 us  [solve(): pl.pallas_call(functools.partial(solve_kernel, members), out_shape=[jax.S...]
  transfers between devices with their start and end apart: 11 -> 11, of which waited for: 4 -> 4; matrix products, arithmetic and copies ran while one was open for 0% -> 0% of each run, Pallas kernels for 31% -> 30%
where the time goes in v6:
time: 43.9 us; the launch traced here: 43.6 us
  Pallas kernels  18 us (41%)
  starting transfers between devices  16.6 us (38%)
  waiting for transfers between devices  6.69 us (15%)
  local copies, waits for them, and re-layouts  0.98 us (2%)
  other arithmetic  0.74 us (2%)
  between operations  0.68 us (2%)
    pallas_call x1, Pallas kernels, solve(): pl.pallas_call(functools.partial(solve_kernel, members), out_shape=[jax.S...  10.4 us
    ppermute x8, starting transfers between devices, across(): lax.ppermute(value, 'member', [(i, i ^ distance) for i in range(members)])  7.55 us
    pallas_call x3, Pallas kernels, call(): pl.pallas_call(kernel, out_shape=outs, in_specs=specs, out_specs=jax.tree...  5.62 us
    all_to_all x1, starting transfers between devices, on_device(): lax.all_to_all(packed, 'member', split_axis=0, concat_axis=0, tiled=True)  5.18 us
    ppermute x8, waiting for transfers between devices, across(): lax.ppermute(value, 'member', [(i, i ^ distance) for i in range(members)])  5.14 us
    ppermute x1, starting transfers between devices, on_device(): after = lax.ppermute(first, 'cluster', down)  2.25 us
    pallas_call x1, Pallas kernels, pack(): pl.pallas_call(pack_kernel, out_shape=jax.ShapeDtypeStruct((members, rows...  1.9 us
    ppermute x1, starting transfers between devices, on_device(): before = lax.ppermute(last, 'cluster', up)  1.58 us
  transfers between devices with their start and end apart: 11, of which 4 were waited for; matrix products, arithmetic and copies ran while one was open for 0% of the time, Pallas kernels for 30%

profile of v6, /device:TPU:0, one launch (start us, length us, event | category | flops | bytes accessed | tf_op | source)
XLA Modules:
  0.0 43.6 jit_solution(15507147028716358689)
XLA Ops:
  0.6 1.9 %pack.1 = f32[8,72,256]{2,1,0:T(8,128)} custom-call(f32[128,256]{1,0:T(8,128)} %loads_ref.1, s32[2,256]{1,0:T(2,128)} %far_glue_ref.1), custom_call_target="tpu_custom_call" | custom-call | flops 1000000 | bytes 1048576 | tf_op jit(solution)/shard_map/pack/pallas_call | solution.py:271
  2.5 5.2 %all-to-all-start = ((f32[8,72,256]{2,1,0:T(8,128)}), f32[8,72,256]{2,1,0:T(8,128)S(1)}, u32[]{:S(2)}, u32[]{:S(2)}) async-start(f32[8,72,256]{2,1,0:T(8,128)} %pack.1), calls=%async_computation | async-start | bytes 1179648 | tf_op jit(solution)/shard_map/all_to_all | solution.py:384
  7.7 10.4 %solve.1 = (f32[128,256]{1,0:T(8,128)}, f32[128,256]{1,0:T(8,128)}, f32[128,256]{1,0:T(8,128)}, f32[128,256]{1,0:T(8,128)}, f32[128,256]{1,0:T(8,128)}, /*index=...) custom-call(s32[2]{0:T(128)} %far_sizes_ref.1, s32[2,256]{1,0:T(2,128)} %far_glue_ref.1, ...), custom_call_target="tpu_custom_call" | custom-call | flops 10000000000 | bytes 8388608 | tf_op jit(solution)/shard_map/solve/pallas_call | solution.py:219
  18.2 0.0 all-to-all-done.own_ref
  18.2 0.6 %collective-permute-start = (f32[8,72,256]{2,1,0:T(8,128)S(1)}, f32[8,72,256]{2,1,0:T(8,128)S(1)}, u32[]{:S(2)}, u32[]{:S(2)}) collective-permute-start(f32[8,72,256]{2,1,0:T(8,128)S(1)} %all-to-all-done.own_ref), channel_id=1, source_target_pairs={{0,1},{1,0},{2,3},{3,2},{4,5},{5,4},{6,7},{7,6},{8,9},{9,8},{10,11... | collective-permute-start | bytes 1769480 | tf_op jit(solution)/shard_map/ppermute | solution.py:381
  18.8 1.7 %collective-permute-start.1 = (f32[128,256]{1,0:T(8,128)}, f32[128,256]{1,0:T(8,128)S(1)}, u32[]{:S(2)}, u32[]{:S(2)}) collective-permute-start(f32[128,256]{1,0:T(8,128)} %get-tuple-element.41), channel_id=1, source_target_pairs={{0,2},{1,3},{2,0},{3,1},{4,6},{5,7},{6,4},{7,5},{8,10},{9,11},{10,... | collective-permute-start | bytes 393224 | tf_op jit(solution)/shard_map/ppermute | solution.py:381
  20.4 1.5 %collective-permute-start.2 = (f32[128,256]{1,0:T(8,128)}, f32[128,256]{1,0:T(8,128)S(1)}, u32[]{:S(2)}, u32[]{:S(2)}) collective-permute-start(f32[128,256]{1,0:T(8,128)} %get-tuple-element.42), channel_id=1, source_target_pairs={{0,4},{1,5},{2,6},{3,7},{4,0},{5,1},{6,2},{7,3},{8,12},{9,13},{10,... | collective-permute-start | bytes 393224 | tf_op jit(solution)/shard_map/ppermute | solution.py:381
  21.9 0.3 collective-permute-start.3
  22.3 0.8 %collective-permute-start.4 = (f32[128,256]{1,0:T(8,128)}, f32[128,256]{1,0:T(8,128)S(1)}, u32[]{:S(2)}, u32[]{:S(2)}) collective-permute-start(f32[128,256]{1,0:T(8,128)} %get-tuple-element.44), channel_id=1, source_target_pairs={{0,3},{1,2},{2,1},{3,0},{4,7},{5,6},{6,5},{7,4},{8,11},{9,10},{10,... | collective-permute-start | bytes 393224 | tf_op jit(solution)/shard_map/ppermute | solution.py:381
  23.0 0.0 collective-permute-done.twin_ref
  23.0 2.1 %collective-permute-start.5 = (f32[128,256]{1,0:T(8,128)}, f32[128,256]{1,0:T(8,128)S(1)}, u32[]{:S(2)}, u32[]{:S(2)}) collective-permute-start(f32[128,256]{1,0:T(8,128)} %get-tuple-element.45), channel_id=1, source_target_pairs={{0,5},{1,4},{2,7},{3,6},{4,1},{5,0},{6,3},{7,2},{8,13},{9,12},{10,... | collective-permute-start | bytes 393224 | tf_op jit(solution)/shard_map/ppermute | solution.py:381
  25.1 0.7 %routes.1 = (s32[256,16]{1,0:T(8,128)S(1)}, s32[8,128]{1,0:T(8,128)S(1)}, bf16[1024,256]{1,0:T(8,128)(2,1)S(1)}, bf16[1024,256]{1,0:T(8,128)(2,1)S(1)}) custom-call(s32[1]{0:T(128)} %bitcast.place_ref, f32[8,72,256]{2,1,0:T(8,128)S(1)} %all-to-all-done.own_ref, f32[8,72,256]{2,1,0:T(8,128)S(1)} %collective-permute-done.twin_ref), custom_call_target="tpu_custom_call" | custom-call | flops 2000000000 | bytes 4194304 | tf_op jit(solution)/shard_map/routes/pallas_call | solution.py:359
  25.8 0.0 collective-permute-done.1.refs_1_
  25.8 0.6 %collective-permute-start.6 = (f32[128,256]{1,0:T(8,128)}, f32[128,256]{1,0:T(8,128)S(1)}, u32[]{:S(2)}, u32[]{:S(2)}) collective-permute-start(f32[128,256]{1,0:T(8,128)} %get-tuple-element.46), channel_id=1, source_target_pairs={{0,7},{1,6},{2,5},{3,4},{4,3},{5,2},{6,1},{7,0},{8,15},{9,14},{10,... | collective-permute-start | bytes 393224 | tf_op jit(solution)/shard_map/ppermute | solution.py:381
  26.5 2.3 %collective-permute-done.2.refs_2_ = f32[128,256]{1,0:T(8,128)S(1)} collective-permute-done((f32[128,256]{1,0:T(8,128)}, f32[128,256]{1,0:T(8,128)S(1)}, u32[]{:S(2)}, u32[]{:S(2)}) %collective-permute-start.2) | collective-permute-done | bytes 131104 | tf_op jit(solution)/shard_map/ppermute | solution.py:381
  28.8 0.0 collective-permute-start.7
  28.8 0.7 %collective-permute-done.3.refs_3_ = f32[128,256]{1,0:T(8,128)S(1)} collective-permute-done((f32[128,256]{1,0:T(8,128)}, f32[128,256]{1,0:T(8,128)S(1)}, u32[]{:S(2)}, u32[]{:S(2)}) %collective-permute-start.3) | collective-permute-done | bytes 131104 | tf_op jit(solution)/shard_map/ppermute | solution.py:381
  29.5 0.0 copy-start
  29.5 0.9 %copy-done = f32[128,256]{1,0:T(8,128)S(1)} copy-done((f32[128,256]{1,0:T(8,128)S(1)}, f32[128,256]{1,0:T(8,128)}, u32[]{:S(2)}) %copy-start) | copy-done | bytes 131096
  30.4 1.9 %early.1.early_ref = f32[128,1024]{1,0:T(8,128)S(1)} custom-call(s32[8,128]{1,0:T(8,128)S(1)} %get-tuple-element.36.label_ref, s32[256,16]{1,0:T(8,128)S(1)} %get-tuple-element.37.stand_ref, f32[128,256]{1,0:T(8,128)S(1)} %copy-done, f32[128,256]{1,0:T(8,128)S(1)} %collective-permute-done.1.refs_1_, f32[128,256]{1,0:T(8,128)S(1)} %collective-permute-done.2.refs_2_, ...), custom_call_target="tpu_custom_call" | custom-call | flops 2000000000 | bytes 4194304 | tf_op jit(solution)/shard_map/early/pallas_call | solution.py:359
  32.3 0.0 collective-permute-done.4.refs_0_
  32.3 2.1 %collective-permute-done.5.refs_1_ = f32[128,256]{1,0:T(8,128)S(1)} collective-permute-done((f32[128,256]{1,0:T(8,128)}, f32[128,256]{1,0:T(8,128)S(1)}, u32[]{:S(2)}, u32[]{:S(2)}) %collective-permute-start.5) | collective-permute-done | bytes 131104 | tf_op jit(solution)/shard_map/ppermute | solution.py:381
  34.4 0.0 collective-permute-done.6.refs_2_
  34.4 0.0 collective-permute-done.7.refs_3_
  34.4 3.0 %finish.1 = (f32[128,1024]{1,0:T(8,128)}, f32[128,256]{1,0:T(8,128)S(1)}, f32[8,256]{1,0:T(8,128)S(1)}, f32[8,256]{1,0:T(8,128)S(1)}) custom-call(s32[8,128]{1,0:T(8,128)S(1)} %get-tuple-element.36.label_ref, s32[256,16]{1,0:T(8,128)S(1)} %get-tuple-element.37.stand_ref, bf16[1024,256]{1,0:T(8,128)(2,1)S(1)} %get-tuple-element.38.high_ref, ...), custom_call_target="tpu_custom_call" | custom-call | flops 3000000000 | bytes 4194304 | tf_op jit(solution)/shard_map/finish/pallas_call | solution.py:359
  37.4 1.6 %collective-permute-start.8 = (f32[8,256]{1,0:T(8,128)S(1)}, f32[8,256]{1,0:T(8,128)S(1)}, u32[]{:S(2)}, u32[]{:S(2)}) collective-permute-start(f32[8,256]{1,0:T(8,128)S(1)} %get-tuple-element.50), channel_id=1, source_target_pairs={{0,8},{8,16},{16,24},{24,0},{1,9},{9,17},{17,25},{25,1},{2,10},{10... | collective-permute-start | bytes 24584 | tf_op jit(solution)/shard_map/ppermute | solution.py:426
  39.0 2.2 %collective-permute-start.9 = (f32[8,256]{1,0:T(8,128)S(1)}, f32[8,256]{1,0:T(8,128)S(1)}, u32[]{:S(2)}, u32[]{:S(2)}) collective-permute-start(f32[8,256]{1,0:T(8,128)S(1)} %get-tuple-element.51), channel_id=1, source_target_pairs={{8,0},{16,8},{24,16},{0,24},{9,1},{17,9},{25,17},{1,25},{10,2},{18... | collective-permute-start | bytes 24584 | tf_op jit(solution)/shard_map/ppermute | solution.py:427
  41.3 0.1 pad.1.clone
  41.3 1.5 %collective-permute-done.8 = f32[8,256]{1,0:T(8,128)S(1)} collective-permute-done((f32[8,256]{1,0:T(8,128)S(1)}, f32[8,256]{1,0:T(8,128)S(1)}, u32[]{:S(2)}, u32[]{:S(2)}) %collective-permute-start.8) | collective-permute-done | bytes 8224 | tf_op jit(solution)/shard_map/ppermute | solution.py:426
  42.9 0.0 collective-permute-done.9
  42.9 0.7 %maximum_add_fusion = f32[128,256]{1,0:T(8,128)} fusion(f32[128,256]{1,0:T(8,128)S(1)} %get-tuple-element.49, f32[8,256]{1,0:T(8,128)S(1)} %collective-permute-done.9, f32[8,256]{1,0:T(8,128)S(1)} %collective-permute-done.8, f32[128]{0:T(128)S(1)} %pad.1.clone), kind=kLoop, calls=%fused_computation | loop fusion | flops 98304 | bytes 279040 | tf_op jit(solution)/shard_map/add | solution.py:429
  (1 shorter events, 0.0 us)
Async XLA Ops:
  2.5 15.6 %all-to-all-start = ((f32[8,72,256]{2,1,0:T(8,128)}), f32[8,72,256]{2,1,0:T(8,128)S(1)}, u32[]{:S(2)}, u32[]{:S(2)}) async-start(f32[8,72,256]{2,1,0:T(8,128)} %pack.1), calls=%async_computation | async-start | bytes 1179648 | tf_op jit(solution)/shard_map/all_to_all | solution.py:384
  18.2 4.9 %collective-permute-start = (f32[8,72,256]{2,1,0:T(8,128)S(1)}, f32[8,72,256]{2,1,0:T(8,128)S(1)}, u32[]{:S(2)}, u32[]{:S(2)}) collective-permute-start(f32[8,72,256]{2,1,0:T(8,128)S(1)} %all-to-all-done.own_ref), channel_id=1, source_target_pairs={{0,1},{1,0},{2,3},{3,2},{4,5},{5,4},{6,7},{7,6},{8,9},{9,8},{10,11... | collective-permute-start | bytes 1769480 | tf_op jit(solution)/shard_map/ppermute | solution.py:381
  18.8 7.1 %collective-permute-start.1 = (f32[128,256]{1,0:T(8,128)}, f32[128,256]{1,0:T(8,128)S(1)}, u32[]{:S(2)}, u32[]{:S(2)}) collective-permute-start(f32[128,256]{1,0:T(8,128)} %get-tuple-element.41), channel_id=1, source_target_pairs={{0,2},{1,3},{2,0},{3,1},{4,6},{5,7},{6,4},{7,5},{8,10},{9,11},{10,... | collective-permute-start | bytes 393224 | tf_op jit(solution)/shard_map/ppermute | solution.py:381
  20.4 8.3 %collective-permute-start.2 = (f32[128,256]{1,0:T(8,128)}, f32[128,256]{1,0:T(8,128)S(1)}, u32[]{:S(2)}, u32[]{:S(2)}) collective-permute-start(f32[128,256]{1,0:T(8,128)} %get-tuple-element.42), channel_id=1, source_target_pairs={{0,4},{1,5},{2,6},{3,7},{4,0},{5,1},{6,2},{7,3},{8,12},{9,13},{10,... | collective-permute-start | bytes 393224 | tf_op jit(solution)/shard_map/ppermute | solution.py:381
  21.9 7.5 %collective-permute-start.3 = (f32[128,256]{1,0:T(8,128)}, f32[128,256]{1,0:T(8,128)S(1)}, u32[]{:S(2)}, u32[]{:S(2)}) collective-permute-start(f32[128,256]{1,0:T(8,128)} %get-tuple-element.43), channel_id=1, source_target_pairs={{0,6},{1,7},{2,4},{3,5},{4,2},{5,3},{6,0},{7,1},{8,14},{9,15},{10,... | collective-permute-start | bytes 393224 | tf_op jit(solution)/shard_map/ppermute | solution.py:381
  22.3 10.0 %collective-permute-start.4 = (f32[128,256]{1,0:T(8,128)}, f32[128,256]{1,0:T(8,128)S(1)}, u32[]{:S(2)}, u32[]{:S(2)}) collective-permute-start(f32[128,256]{1,0:T(8,128)} %get-tuple-element.44), channel_id=1, source_target_pairs={{0,3},{1,2},{2,1},{3,0},{4,7},{5,6},{6,5},{7,4},{8,11},{9,10},{10,... | collective-permute-start | bytes 393224 | tf_op jit(solution)/shard_map/ppermute | solution.py:381
  23.0 11.4 %collective-permute-start.5 = (f32[128,256]{1,0:T(8,128)}, f32[128,256]{1,0:T(8,128)S(1)}, u32[]{:S(2)}, u32[]{:S(2)}) collective-permute-start(f32[128,256]{1,0:T(8,128)} %get-tuple-element.45), channel_id=1, source_target_pairs={{0,5},{1,4},{2,7},{3,6},{4,1},{5,0},{6,3},{7,2},{8,13},{9,12},{10,... | collective-permute-start | bytes 393224 | tf_op jit(solution)/shard_map/ppermute | solution.py:381
  25.8 8.6 %collective-permute-start.6 = (f32[128,256]{1,0:T(8,128)}, f32[128,256]{1,0:T(8,128)S(1)}, u32[]{:S(2)}, u32[]{:S(2)}) collective-permute-start(f32[128,256]{1,0:T(8,128)} %get-tuple-element.46), channel_id=1, source_target_pairs={{0,7},{1,6},{2,5},{3,4},{4,3},{5,2},{6,1},{7,0},{8,15},{9,14},{10,... | collective-permute-start | bytes 393224 | tf_op jit(solution)/shard_map/ppermute | solution.py:381
  28.8 5.7 %collective-permute-start.7 = (f32[128,256]{1,0:T(8,128)}, f32[128,256]{1,0:T(8,128)S(1)}, u32[]{:S(2)}, u32[]{:S(2)}) collective-permute-start(f32[128,256]{1,0:T(8,128)} %get-tuple-element.47), channel_id=1, source_target_pairs={{0,1},{1,0},{2,3},{3,2},{4,5},{5,4},{6,7},{7,6},{8,9},{9,8},{10,11... | collective-permute-start | bytes 393224 | tf_op jit(solution)/shard_map/ppermute | solution.py:381
  29.5 0.9 %copy-start = (f32[128,256]{1,0:T(8,128)S(1)}, f32[128,256]{1,0:T(8,128)}, u32[]{:S(2)}) copy-start(f32[128,256]{1,0:T(8,128)} %get-tuple-element.40.refs_0_) | copy-start | bytes 393220
  37.4 5.4 %collective-permute-start.8 = (f32[8,256]{1,0:T(8,128)S(1)}, f32[8,256]{1,0:T(8,128)S(1)}, u32[]{:S(2)}, u32[]{:S(2)}) collective-permute-start(f32[8,256]{1,0:T(8,128)S(1)} %get-tuple-element.50), channel_id=1, source_target_pairs={{0,8},{8,16},{16,24},{24,0},{1,9},{9,17},{17,25},{25,1},{2,10},{10... | collective-permute-start | bytes 24584 | tf_op jit(solution)/shard_map/ppermute | solution.py:426
  39.0 3.9 %collective-permute-start.9 = (f32[8,256]{1,0:T(8,128)S(1)}, f32[8,256]{1,0:T(8,128)S(1)}, u32[]{:S(2)}, u32[]{:S(2)}) collective-permute-start(f32[8,256]{1,0:T(8,128)S(1)} %get-tuple-element.51), channel_id=1, source_target_pairs={{8,0},{16,8},{24,16},{0,24},{9,1},{17,9},{25,17},{1,25},{10,2},{18... | collective-permute-start | bytes 24584 | tf_op jit(solution)/shard_map/ppermute | solution.py:427

commit v7 on v6

--- a/solution.py
+++ b/solution.py
@@ -384,8 +384,10 @@
     own = lax.all_to_all(packed, "member", split_axis=0, concat_axis=0, tiled=True)
     values = solve(sizes, glue_index, factors, panels, members)
     own, *values = lax.optimization_barrier((own, *values))
-    arrivals = (0, *range(2, members, 2), *range(3, members, 2), 1)
-    arrived = [across(values[k], k) if k else values[k] for k in arrivals]
+    distances = [*range(2, members, 2), *range(3, members, 2), 1]
+    arrived = {0: values[0], **{k: across(values[k], k) for k in distances}}
+    last_ones = distances[-3:-1]
+    first_ones = [k for k in arrived if k not in last_ones]
     twin = across(own, 1)
     stand, labels, high, low = call(
         functools.partial(routes_kernel, subs),
@@ -400,23 +402,22 @@
         "routes",
         smem=1,
     )
-    half = members // 2
     early = call(
-        functools.partial(early_kernel, subs, arrivals[:half]),
+        functools.partial(early_kernel, subs, first_ones),
         shape((share, NDUAL), F32),
-        (labels, stand, *arrived[:half]),
+        (labels, stand, *[arrived[k] for k in first_ones]),
         2_000_000_000,
         "early",
     )
     dual_rows, raw, first, last = call(
-        functools.partial(finish_kernel, subs, arrivals[half:]),
+        functools.partial(finish_kernel, subs, last_ones),
         (
             shape((share, NDUAL), F32),
             shape((share, nrhs), F32),
             shape((IFACE, nrhs), F32),
             shape((IFACE, nrhs), F32),
         ),
-        (labels, stand, high, low, early, *arrived[half:]),
+        (labels, stand, high, low, early, *[arrived[k] for k in last_ones]),
         3_000_000_000,
         "finish",
     )

time: 43.9 us -> 43.2 us (0.984)
  starting transfers between devices: 16.6 us -> 16 us
    ppermute x8, starting transfers between devices: 7.55 us -> 6.99 us  [across(): lax.ppermute(value, 'member', [(i, i ^ distance) for i in range(members)])]
  transfers between devices with their start and end apart: 11 -> 11, of which waited for: 4 -> 5; matrix products, arithmetic and copies ran while one was open for 0% -> 0% of each run, Pallas kernels for 30% -> 32%
where the time goes in v7:
time: 43.2 us; the launch traced here: 43 us
  Pallas kernels  18 us (42%)
  starting transfers between devices  16 us (37%)
  waiting for transfers between devices  6.59 us (15%)
  local copies, waits for them, and re-layouts  0.98 us (2%)
  other arithmetic  0.74 us (2%)
  between operations  0.68 us (2%)
    pallas_call x1, Pallas kernels, solve(): pl.pallas_call(functools.partial(solve_kernel, members), out_shape=[jax.S...  10.4 us
    ppermute x8, starting transfers between devices, across(): lax.ppermute(value, 'member', [(i, i ^ distance) for i in range(members)])  6.99 us
    pallas_call x3, Pallas kernels, call(): pl.pallas_call(kernel, out_shape=outs, in_specs=specs, out_specs=jax.tree...  5.61 us
    all_to_all x1, starting transfers between devices, on_device(): lax.all_to_all(packed, 'member', split_axis=0, concat_axis=0, tiled=True)  5.18 us
    ppermute x8, waiting for transfers between devices, across(): lax.ppermute(value, 'member', [(i, i ^ distance) for i in range(members)])  5.04 us
    ppermute x1, starting transfers between devices, on_device(): after = lax.ppermute(first, 'cluster', down)  2.25 us
    pallas_call x1, Pallas kernels, pack(): pl.pallas_call(pack_kernel, out_shape=jax.ShapeDtypeStruct((members, rows...  1.9 us
    ppermute x1, starting transfers between devices, on_device(): before = lax.ppermute(last, 'cluster', up)  1.58 us
  transfers between devices with their start and end apart: 11, of which 5 were waited for; matrix products, arithmetic and copies ran while one was open for 0% of the time, Pallas kernels for 32%

profile of v7, /device:TPU:0, one launch (start us, length us, event | category | flops | bytes accessed | tf_op | source)
XLA Modules:
  0.0 43.0 jit_solution(2454377379988547997)
XLA Ops:
  0.6 1.9 %pack.1 = f32[8,72,256]{2,1,0:T(8,128)} custom-call(f32[128,256]{1,0:T(8,128)} %loads_ref.1, s32[2,256]{1,0:T(2,128)} %far_glue_ref.1), custom_call_target="tpu_custom_call" | custom-call | flops 1000000 | bytes 1048576 | tf_op jit(solution)/shard_map/pack/pallas_call | solution.py:271
  2.5 5.2 %all-to-all-start = ((f32[8,72,256]{2,1,0:T(8,128)}), f32[8,72,256]{2,1,0:T(8,128)S(1)}, u32[]{:S(2)}, u32[]{:S(2)}) async-start(f32[8,72,256]{2,1,0:T(8,128)} %pack.1), calls=%async_computation | async-start | bytes 1179648 | tf_op jit(solution)/shard_map/all_to_all | solution.py:384
  7.7 10.4 %solve.1 = (f32[128,256]{1,0:T(8,128)}, f32[128,256]{1,0:T(8,128)}, f32[128,256]{1,0:T(8,128)}, f32[128,256]{1,0:T(8,128)}, f32[128,256]{1,0:T(8,128)}, /*index=...) custom-call(s32[2]{0:T(128)} %far_sizes_ref.1, s32[2,256]{1,0:T(2,128)} %far_glue_ref.1, ...), custom_call_target="tpu_custom_call" | custom-call | flops 10000000000 | bytes 8388608 | tf_op jit(solution)/shard_map/solve/pallas_call | solution.py:219
  18.2 0.0 all-to-all-done.own_ref
  18.2 0.6 %collective-permute-start = (f32[8,72,256]{2,1,0:T(8,128)S(1)}, f32[8,72,256]{2,1,0:T(8,128)S(1)}, u32[]{:S(2)}, u32[]{:S(2)}) collective-permute-start(f32[8,72,256]{2,1,0:T(8,128)S(1)} %all-to-all-done.own_ref), channel_id=1, source_target_pairs={{0,1},{1,0},{2,3},{3,2},{4,5},{5,4},{6,7},{7,6},{8,9},{9,8},{10,11... | collective-permute-start | bytes 1769480 | tf_op jit(solution)/shard_map/ppermute | solution.py:381
  18.8 1.7 %collective-permute-start.1 = (f32[128,256]{1,0:T(8,128)}, f32[128,256]{1,0:T(8,128)S(1)}, u32[]{:S(2)}, u32[]{:S(2)}) collective-permute-start(f32[128,256]{1,0:T(8,128)} %get-tuple-element.41), channel_id=1, source_target_pairs={{0,2},{1,3},{2,0},{3,1},{4,6},{5,7},{6,4},{7,5},{8,10},{9,11},{10,... | collective-permute-start | bytes 393224 | tf_op jit(solution)/shard_map/ppermute | solution.py:381
  20.4 1.5 %collective-permute-start.2 = (f32[128,256]{1,0:T(8,128)}, f32[128,256]{1,0:T(8,128)S(1)}, u32[]{:S(2)}, u32[]{:S(2)}) collective-permute-start(f32[128,256]{1,0:T(8,128)} %get-tuple-element.42), channel_id=1, source_target_pairs={{0,4},{1,5},{2,6},{3,7},{4,0},{5,1},{6,2},{7,3},{8,12},{9,13},{10,... | collective-permute-start | bytes 393224 | tf_op jit(solution)/shard_map/ppermute | solution.py:381
  21.9 0.3 collective-permute-start.3
  22.3 0.8 %collective-permute-start.4 = (f32[128,256]{1,0:T(8,128)}, f32[128,256]{1,0:T(8,128)S(1)}, u32[]{:S(2)}, u32[]{:S(2)}) collective-permute-start(f32[128,256]{1,0:T(8,128)} %get-tuple-element.44), channel_id=1, source_target_pairs={{0,3},{1,2},{2,1},{3,0},{4,7},{5,6},{6,5},{7,4},{8,11},{9,10},{10,... | collective-permute-start | bytes 393224 | tf_op jit(solution)/shard_map/ppermute | solution.py:381
  23.0 0.0 collective-permute-done.twin_ref
  23.0 1.0 %collective-permute-start.5 = (f32[128,256]{1,0:T(8,128)}, f32[128,256]{1,0:T(8,128)S(1)}, u32[]{:S(2)}, u32[]{:S(2)}) collective-permute-start(f32[128,256]{1,0:T(8,128)} %get-tuple-element.45), channel_id=1, source_target_pairs={{0,1},{1,0},{2,3},{3,2},{4,5},{5,4},{6,7},{7,6},{8,9},{9,8},{10,11... | collective-permute-start | bytes 393224 | tf_op jit(solution)/shard_map/ppermute | solution.py:381
  24.0 0.7 %routes.1 = (s32[256,16]{1,0:T(8,128)S(1)}, s32[8,128]{1,0:T(8,128)S(1)}, bf16[1024,256]{1,0:T(8,128)(2,1)S(1)}, bf16[1024,256]{1,0:T(8,128)(2,1)S(1)}) custom-call(s32[1]{0:T(128)} %bitcast.place_ref, f32[8,72,256]{2,1,0:T(8,128)S(1)} %all-to-all-done.own_ref, f32[8,72,256]{2,1,0:T(8,128)S(1)} %collective-permute-done.twin_ref), custom_call_target="tpu_custom_call" | custom-call | flops 2000000000 | bytes 4194304 | tf_op jit(solution)/shard_map/routes/pallas_call | solution.py:359
  24.7 0.0 collective-permute-done.1.refs_1_
  24.8 1.1 %collective-permute-start.6 = (f32[128,256]{1,0:T(8,128)}, f32[128,256]{1,0:T(8,128)S(1)}, u32[]{:S(2)}, u32[]{:S(2)}) collective-permute-start(f32[128,256]{1,0:T(8,128)} %get-tuple-element.46), channel_id=1, source_target_pairs={{0,5},{1,4},{2,7},{3,6},{4,1},{5,0},{6,3},{7,2},{8,13},{9,12},{10,... | collective-permute-start | bytes 393224 | tf_op jit(solution)/shard_map/ppermute | solution.py:381
  25.9 2.7 %collective-permute-done.2.refs_2_ = f32[128,256]{1,0:T(8,128)S(1)} collective-permute-done((f32[128,256]{1,0:T(8,128)}, f32[128,256]{1,0:T(8,128)S(1)}, u32[]{:S(2)}, u32[]{:S(2)}) %collective-permute-start.2) | collective-permute-done | bytes 131104 | tf_op jit(solution)/shard_map/ppermute | solution.py:381
  28.6 0.0 collective-permute-start.7
  28.6 0.9 %collective-permute-done.3.refs_3_ = f32[128,256]{1,0:T(8,128)S(1)} collective-permute-done((f32[128,256]{1,0:T(8,128)}, f32[128,256]{1,0:T(8,128)S(1)}, u32[]{:S(2)}, u32[]{:S(2)}) %collective-permute-start.3) | collective-permute-done | bytes 131104 | tf_op jit(solution)/shard_map/ppermute | solution.py:381
  29.5 0.2 collective-permute-done.4.refs_4_
  29.7 0.0 collective-permute-done.5.refs_5_
  29.7 0.0 copy-start
  29.7 0.9 %copy-done = f32[128,256]{1,0:T(8,128)S(1)} copy-done((f32[128,256]{1,0:T(8,128)S(1)}, f32[128,256]{1,0:T(8,128)}, u32[]{:S(2)}) %copy-start) | copy-done | bytes 131096
  30.6 2.8 %early.1.early_ref = f32[128,1024]{1,0:T(8,128)S(1)} custom-call(s32[8,128]{1,0:T(8,128)S(1)} %get-tuple-element.36.label_ref, s32[256,16]{1,0:T(8,128)S(1)} %get-tuple-element.37.stand_ref, f32[128,256]{1,0:T(8,128)S(1)} %copy-done, f32[128,256]{1,0:T(8,128)S(1)} %collective-permute-done.1.refs_1_, f32[128,256]{1,0:T(8,128)S(1)} %collective-permute-done.2.refs_2_, ...), custom_call_target="tpu_custom_call" | custom-call | flops 2000000000 | bytes 4194304 | tf_op jit(solution)/shard_map/early/pallas_call | solution.py:359
  33.4 0.0 collective-permute-done.6.refs_0_
  33.4 1.2 %collective-permute-done.7.refs_1_ = f32[128,256]{1,0:T(8,128)S(1)} collective-permute-done((f32[128,256]{1,0:T(8,128)}, f32[128,256]{1,0:T(8,128)S(1)}, u32[]{:S(2)}, u32[]{:S(2)}) %collective-permute-start.7) | collective-permute-done | bytes 131104 | tf_op jit(solution)/shard_map/ppermute | solution.py:381
  34.6 2.1 %finish.1 = (f32[128,1024]{1,0:T(8,128)}, f32[128,256]{1,0:T(8,128)S(1)}, f32[8,256]{1,0:T(8,128)S(1)}, f32[8,256]{1,0:T(8,128)S(1)}) custom-call(s32[8,128]{1,0:T(8,128)S(1)} %get-tuple-element.36.label_ref, s32[256,16]{1,0:T(8,128)S(1)} %get-tuple-element.37.stand_ref, bf16[1024,256]{1,0:T(8,128)(2,1)S(1)} %get-tuple-element.38.high_ref, ...), custom_call_target="tpu_custom_call" | custom-call | flops 3000000000 | bytes 4194304 | tf_op jit(solution)/shard_map/finish/pallas_call | solution.py:359
  36.8 1.6 %collective-permute-start.8 = (f32[8,256]{1,0:T(8,128)S(1)}, f32[8,256]{1,0:T(8,128)S(1)}, u32[]{:S(2)}, u32[]{:S(2)}) collective-permute-start(f32[8,256]{1,0:T(8,128)S(1)} %get-tuple-element.50), channel_id=1, source_target_pairs={{0,8},{8,16},{16,24},{24,0},{1,9},{9,17},{17,25},{25,1},{2,10},{10... | collective-permute-start | bytes 24584 | tf_op jit(solution)/shard_map/ppermute | solution.py:427
  38.3 2.2 %collective-permute-start.9 = (f32[8,256]{1,0:T(8,128)S(1)}, f32[8,256]{1,0:T(8,128)S(1)}, u32[]{:S(2)}, u32[]{:S(2)}) collective-permute-start(f32[8,256]{1,0:T(8,128)S(1)} %get-tuple-element.51), channel_id=1, source_target_pairs={{8,0},{16,8},{24,16},{0,24},{9,1},{17,9},{25,17},{1,25},{10,2},{18... | collective-permute-start | bytes 24584 | tf_op jit(solution)/shard_map/ppermute | solution.py:428
  40.6 0.1 pad.1.clone
  40.7 1.5 %collective-permute-done.8 = f32[8,256]{1,0:T(8,128)S(1)} collective-permute-done((f32[8,256]{1,0:T(8,128)S(1)}, f32[8,256]{1,0:T(8,128)S(1)}, u32[]{:S(2)}, u32[]{:S(2)}) %collective-permute-start.8) | collective-permute-done | bytes 8224 | tf_op jit(solution)/shard_map/ppermute | solution.py:427
  42.2 0.0 collective-permute-done.9
  42.2 0.7 %maximum_add_fusion = f32[128,256]{1,0:T(8,128)} fusion(f32[128,256]{1,0:T(8,128)S(1)} %get-tuple-element.49, f32[8,256]{1,0:T(8,128)S(1)} %collective-permute-done.9, f32[8,256]{1,0:T(8,128)S(1)} %collective-permute-done.8, f32[128]{0:T(128)S(1)} %pad.1.clone), kind=kLoop, calls=%fused_computation | loop fusion | flops 98304 | bytes 279040 | tf_op jit(solution)/shard_map/add | solution.py:430
  (1 shorter events, 0.0 us)
Async XLA Ops:
  2.5 15.6 %all-to-all-start = ((f32[8,72,256]{2,1,0:T(8,128)}), f32[8,72,256]{2,1,0:T(8,128)S(1)}, u32[]{:S(2)}, u32[]{:S(2)}) async-start(f32[8,72,256]{2,1,0:T(8,128)} %pack.1), calls=%async_computation | async-start | bytes 1179648 | tf_op jit(solution)/shard_map/all_to_all | solution.py:384
  18.2 4.9 %collective-permute-start = (f32[8,72,256]{2,1,0:T(8,128)S(1)}, f32[8,72,256]{2,1,0:T(8,128)S(1)}, u32[]{:S(2)}, u32[]{:S(2)}) collective-permute-start(f32[8,72,256]{2,1,0:T(8,128)S(1)} %all-to-all-done.own_ref), channel_id=1, source_target_pairs={{0,1},{1,0},{2,3},{3,2},{4,5},{5,4},{6,7},{7,6},{8,9},{9,8},{10,11... | collective-permute-start | bytes 1769480 | tf_op jit(solution)/shard_map/ppermute | solution.py:381
  18.8 6.0 %collective-permute-start.1 = (f32[128,256]{1,0:T(8,128)}, f32[128,256]{1,0:T(8,128)S(1)}, u32[]{:S(2)}, u32[]{:S(2)}) collective-permute-start(f32[128,256]{1,0:T(8,128)} %get-tuple-element.41), channel_id=1, source_target_pairs={{0,2},{1,3},{2,0},{3,1},{4,6},{5,7},{6,4},{7,5},{8,10},{9,11},{10,... | collective-permute-start | bytes 393224 | tf_op jit(solution)/shard_map/ppermute | solution.py:381
  20.4 8.2 %collective-permute-start.2 = (f32[128,256]{1,0:T(8,128)}, f32[128,256]{1,0:T(8,128)S(1)}, u32[]{:S(2)}, u32[]{:S(2)}) collective-permute-start(f32[128,256]{1,0:T(8,128)} %get-tuple-element.42), channel_id=1, source_target_pairs={{0,4},{1,5},{2,6},{3,7},{4,0},{5,1},{6,2},{7,3},{8,12},{9,13},{10,... | collective-permute-start | bytes 393224 | tf_op jit(solution)/shard_map/ppermute | solution.py:381
  21.9 7.5 %collective-permute-start.3 = (f32[128,256]{1,0:T(8,128)}, f32[128,256]{1,0:T(8,128)S(1)}, u32[]{:S(2)}, u32[]{:S(2)}) collective-permute-start(f32[128,256]{1,0:T(8,128)} %get-tuple-element.43), channel_id=1, source_target_pairs={{0,6},{1,7},{2,4},{3,5},{4,2},{5,3},{6,0},{7,1},{8,14},{9,15},{10,... | collective-permute-start | bytes 393224 | tf_op jit(solution)/shard_map/ppermute | solution.py:381
  22.3 7.4 %collective-permute-start.4 = (f32[128,256]{1,0:T(8,128)}, f32[128,256]{1,0:T(8,128)S(1)}, u32[]{:S(2)}, u32[]{:S(2)}) collective-permute-start(f32[128,256]{1,0:T(8,128)} %get-tuple-element.44), channel_id=1, source_target_pairs={{0,3},{1,2},{2,1},{3,0},{4,7},{5,6},{6,5},{7,4},{8,11},{9,10},{10,... | collective-permute-start | bytes 393224 | tf_op jit(solution)/shard_map/ppermute | solution.py:381
  23.0 6.6 %collective-permute-start.5 = (f32[128,256]{1,0:T(8,128)}, f32[128,256]{1,0:T(8,128)S(1)}, u32[]{:S(2)}, u32[]{:S(2)}) collective-permute-start(f32[128,256]{1,0:T(8,128)} %get-tuple-element.45), channel_id=1, source_target_pairs={{0,1},{1,0},{2,3},{3,2},{4,5},{5,4},{6,7},{7,6},{8,9},{9,8},{10,11... | collective-permute-start | bytes 393224 | tf_op jit(solution)/shard_map/ppermute | solution.py:381
  24.8 8.6 %collective-permute-start.6 = (f32[128,256]{1,0:T(8,128)}, f32[128,256]{1,0:T(8,128)S(1)}, u32[]{:S(2)}, u32[]{:S(2)}) collective-permute-start(f32[128,256]{1,0:T(8,128)} %get-tuple-element.46), channel_id=1, source_target_pairs={{0,5},{1,4},{2,7},{3,6},{4,1},{5,0},{6,3},{7,2},{8,13},{9,12},{10,... | collective-permute-start | bytes 393224 | tf_op jit(solution)/shard_map/ppermute | solution.py:381
  28.6 6.0 %collective-permute-start.7 = (f32[128,256]{1,0:T(8,128)}, f32[128,256]{1,0:T(8,128)S(1)}, u32[]{:S(2)}, u32[]{:S(2)}) collective-permute-start(f32[128,256]{1,0:T(8,128)} %get-tuple-element.47), channel_id=1, source_target_pairs={{0,7},{1,6},{2,5},{3,4},{4,3},{5,2},{6,1},{7,0},{8,15},{9,14},{10,... | collective-permute-start | bytes 393224 | tf_op jit(solution)/shard_map/ppermute | solution.py:381
  29.7 0.9 %copy-start = (f32[128,256]{1,0:T(8,128)S(1)}, f32[128,256]{1,0:T(8,128)}, u32[]{:S(2)}) copy-start(f32[128,256]{1,0:T(8,128)} %get-tuple-element.40.refs_0_) | copy-start | bytes 393220
  36.8 5.4 %collective-permute-start.8 = (f32[8,256]{1,0:T(8,128)S(1)}, f32[8,256]{1,0:T(8,128)S(1)}, u32[]{:S(2)}, u32[]{:S(2)}) collective-permute-start(f32[8,256]{1,0:T(8,128)S(1)} %get-tuple-element.50), channel_id=1, source_target_pairs={{0,8},{8,16},{16,24},{24,0},{1,9},{9,17},{17,25},{25,1},{2,10},{10... | collective-permute-start | bytes 24584 | tf_op jit(solution)/shard_map/ppermute | solution.py:427
  38.3 3.9 %collective-permute-start.9 = (f32[8,256]{1,0:T(8,128)S(1)}, f32[8,256]{1,0:T(8,128)S(1)}, u32[]{:S(2)}, u32[]{:S(2)}) collective-permute-start(f32[8,256]{1,0:T(8,128)S(1)} %get-tuple-element.51), channel_id=1, source_target_pairs={{8,0},{16,8},{24,16},{0,24},{9,1},{17,9},{25,17},{1,25},{10,2},{18... | collective-permute-start | bytes 24584 | tf_op jit(solution)/shard_map/ppermute | solution.py:428

commit v8 on v7

--- a/solution.py
+++ b/solution.py
@@ -232,7 +232,7 @@
             pltpu.SemaphoreType.DMA,
             pltpu.SemaphoreType.DMA((2,)),
         ],
-        compiler_params=pltpu.CompilerParams(vmem_limit_bytes=54 << 20),
+        compiler_params=pltpu.CompilerParams(vmem_limit_bytes=52 << 20),
         cost_estimate=pl.CostEstimate(flops=10_000_000_000, bytes_accessed=8 << 20, transcendentals=0),
         name="solve",
     )(sizes, glue, factors, panels)

time: 43.2 us -> 43.4 us (level)
  Pallas kernels: 18 us -> 17.1 us
  waiting for transfers between devices: 6.59 us -> 7.17 us
    pallas_call x1, Pallas kernels: 10.4 us -> 9.62 us  [solve(): pl.pallas_call(functools.partial(solve_kernel, members), out_shape=[jax.S...]
    ppermute x8, waiting for transfers between devices: 5.04 us -> 5.62 us  [across(): lax.ppermute(value, 'member', [(i, i ^ distance) for i in range(members)])]
    unnamed x2 -> x4, local copies, waits for them, and re-layouts: 0.9 us -> 1.33 us
  transfers between devices with their start and end apart: 11 -> 11, of which waited for: 5 -> 5; matrix products, arithmetic and copies ran while one was open for 0% -> 0% of each run, Pallas kernels for 32% -> 30%
where the time goes in v8:
time: 43.4 us; the launch traced here: 43.1 us
  Pallas kernels  17.1 us (39%)
  starting transfers between devices  16 us (37%)
  waiting for transfers between devices  7.17 us (17%)
  local copies, waits for them, and re-layouts  1.41 us (3%)
  other arithmetic  0.74 us (2%)
  between operations  0.69 us (2%)
    pallas_call x1, Pallas kernels, solve(): pl.pallas_call(functools.partial(solve_kernel, members), out_shape=[jax.S...  9.62 us
    ppermute x8, starting transfers between devices, across(): lax.ppermute(value, 'member', [(i, i ^ distance) for i in range(members)])  6.99 us
    ppermute x8, waiting for transfers between devices, across(): lax.ppermute(value, 'member', [(i, i ^ distance) for i in range(members)])  5.62 us
    pallas_call x3, Pallas kernels, call(): pl.pallas_call(kernel, out_shape=outs, in_specs=specs, out_specs=jax.tree...  5.6 us
    all_to_all x1, starting transfers between devices, on_device(): lax.all_to_all(packed, 'member', split_axis=0, concat_axis=0, tiled=True)  5.18 us
    ppermute x1, starting transfers between devices, on_device(): after = lax.ppermute(first, 'cluster', down)  2.24 us
    pallas_call x1, Pallas kernels, pack(): pl.pallas_call(pack_kernel, out_shape=jax.ShapeDtypeStruct((members, rows...  1.9 us
    ppermute x1, starting transfers between devices, on_device(): before = lax.ppermute(last, 'cluster', up)  1.59 us
  transfers between devices with their start and end apart: 11, of which 5 were waited for; matrix products, arithmetic and copies ran while one was open for 0% of the time, Pallas kernels for 30%

profile of v8, /device:TPU:0, one launch (start us, length us, event | category | flops | bytes accessed | tf_op | source)
XLA Modules:
  0.0 43.1 jit_solution(13338406062144131043)
XLA Ops:
  0.6 1.9 %pack.1 = f32[8,72,256]{2,1,0:T(8,128)} custom-call(f32[128,256]{1,0:T(8,128)} %loads_ref.1, s32[2,256]{1,0:T(2,128)} %far_glue_ref.1), custom_call_target="tpu_custom_call" | custom-call | flops 1000000 | bytes 1048576 | tf_op jit(solution)/shard_map/pack/pallas_call | solution.py:271
  2.5 5.2 %all-to-all-start = ((f32[8,72,256]{2,1,0:T(8,128)}), f32[8,72,256]{2,1,0:T(8,128)S(1)}, u32[]{:S(2)}, u32[]{:S(2)}) async-start(f32[8,72,256]{2,1,0:T(8,128)} %pack.1), calls=%async_computation | async-start | bytes 1179648 | tf_op jit(solution)/shard_map/all_to_all | solution.py:384
  7.7 0.0 copy-start
  7.7 0.7 %copy-done = s32[2,256]{1,0:T(2,128)S(1)} copy-done((s32[2,256]{1,0:T(2,128)S(1)}, s32[2,256]{1,0:T(2,128)}, u32[]{:S(2)}) %copy-start) | copy-done | bytes 2072
  8.4 0.7 %copy-done.1 = s32[2]{0:T(128)S(1)} copy-done((s32[2]{0:T(128)S(1)}, s32[2]{0:T(128)}, u32[]{:S(2)}) %copy-start.1) | copy-done | bytes 32
  9.1 9.6 %solve.1 = (f32[128,256]{1,0:T(8,128)S(1)}, f32[128,256]{1,0:T(8,128)S(1)}, f32[128,256]{1,0:T(8,128)S(1)}, f32[128,256]{1,0:T(8,128)S(1)}, f32[128,256]{1,0:T(8...) custom-call(s32[2]{0:T(128)S(1)} %copy-done.1, s32[2,256]{1,0:T(2,128)S(1)} %copy-done, ...), custom_call_target="tpu_custom_call" | custom-call | flops 10000000000 | bytes 8388608 | tf_op jit(solution)/shard_map/solve/pallas_call | solution.py:219
  18.7 0.0 all-to-all-done.own_ref
  18.7 0.6 %collective-permute-start = (f32[8,72,256]{2,1,0:T(8,128)S(1)}, f32[8,72,256]{2,1,0:T(8,128)S(1)}, u32[]{:S(2)}, u32[]{:S(2)}) collective-permute-start(f32[8,72,256]{2,1,0:T(8,128)S(1)} %all-to-all-done.own_ref), channel_id=1, source_target_pairs={{0,1},{1,0},{2,3},{3,2},{4,5},{5,4},{6,7},{7,6},{8,9},{9,8},{10,11... | collective-permute-start | bytes 1769480 | tf_op jit(solution)/shard_map/ppermute | solution.py:381
  19.3 1.7 %collective-permute-start.1 = (f32[128,256]{1,0:T(8,128)S(1)}, f32[128,256]{1,0:T(8,128)S(1)}, u32[]{:S(2)}, u32[]{:S(2)}) collective-permute-start(f32[128,256]{1,0:T(8,128)S(1)} %get-tuple-element.41), channel_id=1, source_target_pairs={{0,2},{1,3},{2,0},{3,1},{4,6},{5,7},{6,4},{7,5},{8,10},{9,11},{10,... | collective-permute-start | bytes 393224 | tf_op jit(solution)/shard_map/ppermute | solution.py:381
  20.9 1.5 %collective-permute-start.2 = (f32[128,256]{1,0:T(8,128)S(1)}, f32[128,256]{1,0:T(8,128)S(1)}, u32[]{:S(2)}, u32[]{:S(2)}) collective-permute-start(f32[128,256]{1,0:T(8,128)S(1)} %get-tuple-element.42), channel_id=1, source_target_pairs={{0,4},{1,5},{2,6},{3,7},{4,0},{5,1},{6,2},{7,3},{8,12},{9,13},{10,... | collective-permute-start | bytes 393224 | tf_op jit(solution)/shard_map/ppermute | solution.py:381
  22.4 0.3 collective-permute-start.3
  22.8 0.8 %collective-permute-start.4 = (f32[128,256]{1,0:T(8,128)S(1)}, f32[128,256]{1,0:T(8,128)S(1)}, u32[]{:S(2)}, u32[]{:S(2)}) collective-permute-start(f32[128,256]{1,0:T(8,128)S(1)} %get-tuple-element.44), channel_id=1, source_target_pairs={{0,3},{1,2},{2,1},{3,0},{4,7},{5,6},{6,5},{7,4},{8,11},{9,10},{10,... | collective-permute-start | bytes 393224 | tf_op jit(solution)/shard_map/ppermute | solution.py:381
  23.6 0.0 collective-permute-done.twin_ref
  23.6 1.0 %collective-permute-start.5 = (f32[128,256]{1,0:T(8,128)S(1)}, f32[128,256]{1,0:T(8,128)S(1)}, u32[]{:S(2)}, u32[]{:S(2)}) collective-permute-start(f32[128,256]{1,0:T(8,128)S(1)} %get-tuple-element.45), channel_id=1, source_target_pairs={{0,1},{1,0},{2,3},{3,2},{4,5},{5,4},{6,7},{7,6},{8,9},{9,8},{10,11... | collective-permute-start | bytes 393224 | tf_op jit(solution)/shard_map/ppermute | solution.py:381
  24.6 0.7 %routes.1 = (s32[256,16]{1,0:T(8,128)S(1)}, s32[8,128]{1,0:T(8,128)S(1)}, bf16[1024,256]{1,0:T(8,128)(2,1)S(1)}, bf16[1024,256]{1,0:T(8,128)(2,1)S(1)}) custom-call(s32[1]{0:T(128)} %bitcast.place_ref, f32[8,72,256]{2,1,0:T(8,128)S(1)} %all-to-all-done.own_ref, f32[8,72,256]{2,1,0:T(8,128)S(1)} %collective-permute-done.twin_ref), custom_call_target="tpu_custom_call" | custom-call | flops 2000000000 | bytes 4194304 | tf_op jit(solution)/shard_map/routes/pallas_call | solution.py:359
  25.3 0.0 collective-permute-done.1.refs_1_
  25.3 1.1 %collective-permute-start.6 = (f32[128,256]{1,0:T(8,128)S(1)}, f32[128,256]{1,0:T(8,128)S(1)}, u32[]{:S(2)}, u32[]{:S(2)}) collective-permute-start(f32[128,256]{1,0:T(8,128)S(1)} %get-tuple-element.46), channel_id=1, source_target_pairs={{0,5},{1,4},{2,7},{3,6},{4,1},{5,0},{6,3},{7,2},{8,13},{9,12},{10,... | collective-permute-start | bytes 393224 | tf_op jit(solution)/shard_map/ppermute | solution.py:381
  26.4 2.5 %collective-permute-done.2.refs_2_ = f32[128,256]{1,0:T(8,128)S(1)} collective-permute-done((f32[128,256]{1,0:T(8,128)S(1)}, f32[128,256]{1,0:T(8,128)S(1)}, u32[]{:S(2)}, u32[]{:S(2)}) %collective-permute-start.2) | collective-permute-done | bytes 131104 | tf_op jit(solution)/shard_map/ppermute | solution.py:381
  28.9 0.0 collective-permute-start.7
  28.9 0.8 %collective-permute-done.3.refs_3_ = f32[128,256]{1,0:T(8,128)S(1)} collective-permute-done((f32[128,256]{1,0:T(8,128)S(1)}, f32[128,256]{1,0:T(8,128)S(1)}, u32[]{:S(2)}, u32[]{:S(2)}) %collective-permute-start.3) | collective-permute-done | bytes 131104 | tf_op jit(solution)/shard_map/ppermute | solution.py:381
  29.7 0.1 collective-permute-done.4.refs_4_
  29.9 0.0 collective-permute-done.5.refs_5_
  29.9 2.8 %early.1.early_ref = f32[128,1024]{1,0:T(8,128)S(1)} custom-call(s32[8,128]{1,0:T(8,128)S(1)} %get-tuple-element.36.label_ref, s32[256,16]{1,0:T(8,128)S(1)} %get-tuple-element.37.stand_ref, f32[128,256]{1,0:T(8,128)S(1)} %get-tuple-element.40.refs_0_, f32[128,256]{1,0:T(8,128)S(1)} %collective-permute-done.1.refs_1_, ...), custom_call_target="tpu_custom_call" | custom-call | flops 2000000000 | bytes 4194304 | tf_op jit(solution)/shard_map/early/pallas_call | solution.py:359
  32.7 0.0 collective-permute-done.6.refs_0_
  32.7 2.1 %collective-permute-done.7.refs_1_ = f32[128,256]{1,0:T(8,128)S(1)} collective-permute-done((f32[128,256]{1,0:T(8,128)S(1)}, f32[128,256]{1,0:T(8,128)S(1)}, u32[]{:S(2)}, u32[]{:S(2)}) %collective-permute-start.7) | collective-permute-done | bytes 131104 | tf_op jit(solution)/shard_map/ppermute | solution.py:381
  34.8 2.1 %finish.1 = (f32[128,1024]{1,0:T(8,128)}, f32[128,256]{1,0:T(8,128)S(1)}, f32[8,256]{1,0:T(8,128)S(1)}, f32[8,256]{1,0:T(8,128)S(1)}) custom-call(s32[8,128]{1,0:T(8,128)S(1)} %get-tuple-element.36.label_ref, s32[256,16]{1,0:T(8,128)S(1)} %get-tuple-element.37.stand_ref, bf16[1024,256]{1,0:T(8,128)(2,1)S(1)} %get-tuple-element.38.high_ref, ...), custom_call_target="tpu_custom_call" | custom-call | flops 3000000000 | bytes 4194304 | tf_op jit(solution)/shard_map/finish/pallas_call | solution.py:359
  36.9 1.6 %collective-permute-start.8 = (f32[8,256]{1,0:T(8,128)S(1)}, f32[8,256]{1,0:T(8,128)S(1)}, u32[]{:S(2)}, u32[]{:S(2)}) collective-permute-start(f32[8,256]{1,0:T(8,128)S(1)} %get-tuple-element.50), channel_id=1, source_target_pairs={{0,8},{8,16},{16,24},{24,0},{1,9},{9,17},{17,25},{25,1},{2,10},{10... | collective-permute-start | bytes 24584 | tf_op jit(solution)/shard_map/ppermute | solution.py:427
  38.5 2.2 %collective-permute-start.9 = (f32[8,256]{1,0:T(8,128)S(1)}, f32[8,256]{1,0:T(8,128)S(1)}, u32[]{:S(2)}, u32[]{:S(2)}) collective-permute-start(f32[8,256]{1,0:T(8,128)S(1)} %get-tuple-element.51), channel_id=1, source_target_pairs={{8,0},{16,8},{24,16},{0,24},{9,1},{17,9},{25,17},{1,25},{10,2},{18... | collective-permute-start | bytes 24584 | tf_op jit(solution)/shard_map/ppermute | solution.py:428
  40.8 0.1 pad.1.clone
  40.8 1.5 %collective-permute-done.8 = f32[8,256]{1,0:T(8,128)S(1)} collective-permute-done((f32[8,256]{1,0:T(8,128)S(1)}, f32[8,256]{1,0:T(8,128)S(1)}, u32[]{:S(2)}, u32[]{:S(2)}) %collective-permute-start.8) | collective-permute-done | bytes 8224 | tf_op jit(solution)/shard_map/ppermute | solution.py:427
  42.4 0.0 collective-permute-done.9
  42.4 0.7 %maximum_add_fusion = f32[128,256]{1,0:T(8,128)} fusion(f32[128,256]{1,0:T(8,128)S(1)} %get-tuple-element.49, f32[8,256]{1,0:T(8,128)S(1)} %collective-permute-done.9, f32[8,256]{1,0:T(8,128)S(1)} %collective-permute-done.8, f32[128]{0:T(128)S(1)} %pad.1.clone), kind=kLoop, calls=%fused_computation | loop fusion | flops 98304 | bytes 279040 | tf_op jit(solution)/shard_map/add | solution.py:430
  (2 shorter events, 0.0 us)
Async XLA Ops:
  2.5 16.2 %all-to-all-start = ((f32[8,72,256]{2,1,0:T(8,128)}), f32[8,72,256]{2,1,0:T(8,128)S(1)}, u32[]{:S(2)}, u32[]{:S(2)}) async-start(f32[8,72,256]{2,1,0:T(8,128)} %pack.1), calls=%async_computation | async-start | bytes 1179648 | tf_op jit(solution)/shard_map/all_to_all | solution.py:384
  7.7 0.7 %copy-start = (s32[2,256]{1,0:T(2,128)S(1)}, s32[2,256]{1,0:T(2,128)}, u32[]{:S(2)}) copy-start(s32[2,256]{1,0:T(2,128)} %far_glue_ref.1) | copy-start | bytes 6148
  8.4 0.7 %copy-start.1 = (s32[2]{0:T(128)S(1)}, s32[2]{0:T(128)}, u32[]{:S(2)}) copy-start(s32[2]{0:T(128)} %far_sizes_ref.1) | copy-start | bytes 28
  18.7 4.9 %collective-permute-start = (f32[8,72,256]{2,1,0:T(8,128)S(1)}, f32[8,72,256]{2,1,0:T(8,128)S(1)}, u32[]{:S(2)}, u32[]{:S(2)}) collective-permute-start(f32[8,72,256]{2,1,0:T(8,128)S(1)} %all-to-all-done.own_ref), channel_id=1, source_target_pairs={{0,1},{1,0},{2,3},{3,2},{4,5},{5,4},{6,7},{7,6},{8,9},{9,8},{10,11... | collective-permute-start | bytes 1769480 | tf_op jit(solution)/shard_map/ppermute | solution.py:381
  19.3 6.0 %collective-permute-start.1 = (f32[128,256]{1,0:T(8,128)S(1)}, f32[128,256]{1,0:T(8,128)S(1)}, u32[]{:S(2)}, u32[]{:S(2)}) collective-permute-start(f32[128,256]{1,0:T(8,128)S(1)} %get-tuple-element.41), channel_id=1, source_target_pairs={{0,2},{1,3},{2,0},{3,1},{4,6},{5,7},{6,4},{7,5},{8,10},{9,11},{10,... | collective-permute-start | bytes 393224 | tf_op jit(solution)/shard_map/ppermute | solution.py:381
  20.9 8.0 %collective-permute-start.2 = (f32[128,256]{1,0:T(8,128)S(1)}, f32[128,256]{1,0:T(8,128)S(1)}, u32[]{:S(2)}, u32[]{:S(2)}) collective-permute-start(f32[128,256]{1,0:T(8,128)S(1)} %get-tuple-element.42), channel_id=1, source_target_pairs={{0,4},{1,5},{2,6},{3,7},{4,0},{5,1},{6,2},{7,3},{8,12},{9,13},{10,... | collective-permute-start | bytes 393224 | tf_op jit(solution)/shard_map/ppermute | solution.py:381
  22.4 7.3 %collective-permute-start.3 = (f32[128,256]{1,0:T(8,128)S(1)}, f32[128,256]{1,0:T(8,128)S(1)}, u32[]{:S(2)}, u32[]{:S(2)}) collective-permute-start(f32[128,256]{1,0:T(8,128)S(1)} %get-tuple-element.43), channel_id=1, source_target_pairs={{0,6},{1,7},{2,4},{3,5},{4,2},{5,3},{6,0},{7,1},{8,14},{9,15},{10,... | collective-permute-start | bytes 393224 | tf_op jit(solution)/shard_map/ppermute | solution.py:381
  22.8 7.1 %collective-permute-start.4 = (f32[128,256]{1,0:T(8,128)S(1)}, f32[128,256]{1,0:T(8,128)S(1)}, u32[]{:S(2)}, u32[]{:S(2)}) collective-permute-start(f32[128,256]{1,0:T(8,128)S(1)} %get-tuple-element.44), channel_id=1, source_target_pairs={{0,3},{1,2},{2,1},{3,0},{4,7},{5,6},{6,5},{7,4},{8,11},{9,10},{10,... | collective-permute-start | bytes 393224 | tf_op jit(solution)/shard_map/ppermute | solution.py:381
  23.6 6.3 %collective-permute-start.5 = (f32[128,256]{1,0:T(8,128)S(1)}, f32[128,256]{1,0:T(8,128)S(1)}, u32[]{:S(2)}, u32[]{:S(2)}) collective-permute-start(f32[128,256]{1,0:T(8,128)S(1)} %get-tuple-element.45), channel_id=1, source_target_pairs={{0,1},{1,0},{2,3},{3,2},{4,5},{5,4},{6,7},{7,6},{8,9},{9,8},{10,11... | collective-permute-start | bytes 393224 | tf_op jit(solution)/shard_map/ppermute | solution.py:381
  25.3 7.4 %collective-permute-start.6 = (f32[128,256]{1,0:T(8,128)S(1)}, f32[128,256]{1,0:T(8,128)S(1)}, u32[]{:S(2)}, u32[]{:S(2)}) collective-permute-start(f32[128,256]{1,0:T(8,128)S(1)} %get-tuple-element.46), channel_id=1, source_target_pairs={{0,5},{1,4},{2,7},{3,6},{4,1},{5,0},{6,3},{7,2},{8,13},{9,12},{10,... | collective-permute-start | bytes 393224 | tf_op jit(solution)/shard_map/ppermute | solution.py:381
  28.9 5.9 %collective-permute-start.7 = (f32[128,256]{1,0:T(8,128)S(1)}, f32[128,256]{1,0:T(8,128)S(1)}, u32[]{:S(2)}, u32[]{:S(2)}) collective-permute-start(f32[128,256]{1,0:T(8,128)S(1)} %get-tuple-element.47), channel_id=1, source_target_pairs={{0,7},{1,6},{2,5},{3,4},{4,3},{5,2},{6,1},{7,0},{8,15},{9,14},{10,... | collective-permute-start | bytes 393224 | tf_op jit(solution)/shard_map/ppermute | solution.py:381
  36.9 5.4 %collective-permute-start.8 = (f32[8,256]{1,0:T(8,128)S(1)}, f32[8,256]{1,0:T(8,128)S(1)}, u32[]{:S(2)}, u32[]{:S(2)}) collective-permute-start(f32[8,256]{1,0:T(8,128)S(1)} %get-tuple-element.50), channel_id=1, source_target_pairs={{0,8},{8,16},{16,24},{24,0},{1,9},{9,17},{17,25},{25,1},{2,10},{10... | collective-permute-start | bytes 24584 | tf_op jit(solution)/shard_map/ppermute | solution.py:427
  38.5 3.9 %collective-permute-start.9 = (f32[8,256]{1,0:T(8,128)S(1)}, f32[8,256]{1,0:T(8,128)S(1)}, u32[]{:S(2)}, u32[]{:S(2)}) collective-permute-start(f32[8,256]{1,0:T(8,128)S(1)} %get-tuple-element.51), channel_id=1, source_target_pairs={{8,0},{16,8},{24,16},{0,24},{9,1},{17,9},{25,17},{1,25},{10,2},{18... | collective-permute-start | bytes 24584 | tf_op jit(solution)/shard_map/ppermute | solution.py:428

commit v9 on v8

--- a/solution.py
+++ b/solution.py
@@ -111,12 +111,13 @@
 BATCH = 16
 
 
-def solve_kernel(members, far_sizes_ref, far_glue_ref, far_ref, p_ref, *refs):
+def solve_kernel(members, packed_ref, far_ref, p_ref, *refs):
     out_refs = refs[:members]
-    rest, f_ref, sizes_ref, glue_ref, square_sems, corner_sems, strip_sems, panel_sem, small_sems = refs[members:]
-    sizes_copy = pltpu.make_async_copy(far_sizes_ref, sizes_ref, small_sems.at[0])
-    glue_copy = pltpu.make_async_copy(far_glue_ref, glue_ref, small_sems.at[1])
-    sizes_copy.start()
+    rest, f_ref, tails, square_sems, corner_sems, strip_sems, panel_sem, small_sem = refs[members:]
+    extra = tails.shape[1]
+    ends = packed_ref.at[pl.ds(0, 2), pl.ds(packed_ref.shape[1] - extra, extra)]
+    small_copy = pltpu.make_async_copy(ends, tails, small_sem)
+    small_copy.start()
     subs, order, width = p_ref.shape
     wide = 2 * STRIDE
     square_copies, corner_copies, strip_copies = {}, {}, {}
@@ -135,11 +136,12 @@
             corner_copies[s, a] = fetch(s, pl.ds(a + STRIDE, STRIDE), pl.ds(a, STRIDE), corner_sems.at[s, step])
     panel_copy = pltpu.make_async_copy(p_ref, rest, panel_sem)
     panel_copy.start()
-    glue_copy.start()
     for step, a in enumerate(range(0, order - wide, wide)):
         for s in range(subs):
             strip_copies[s, a] = fetch(s, pl.ds(a + wide, order - a - wide), pl.ds(a, wide), strip_sems.at[s, step])
-    sizes_copy.wait()
+    small_copy.wait()
+    lines = subs // 2
+    lives = [tails[0, lines + s:lines + s + 1].astype(jnp.int32) for s in range(subs)]
     row = iota((STRIDE, STRIDE), 0)
     col = iota((STRIDE, STRIDE), 1)
     prow = iota((wide, width), 0)
@@ -154,7 +156,7 @@
         for s, a in batch:
             square_copies[s, a].wait()
             d = f_ref[s, a:a + STRIDE, a:a + STRIDE]
-            keep = (row + a < sizes_ref[s]) & (col <= row)
+            keep = (row + a < lives[s][:, :STRIDE]) & (col <= row)
             blocks.append(jnp.where(keep, d, (row == col).astype(F32)))
         for place, inverse in zip(batch, invert_blocks(blocks)):
             small[place] = split(inverse)
@@ -163,7 +165,7 @@
     for s, a in heads:
         b = a + STRIDE
         corner_copies[s, a].wait()
-        corner = jnp.where(row + b < sizes_ref[s], f_ref[s, b:b + STRIDE, a:b], 0.0)
+        corner = jnp.where(row + b < lives[s][:, :STRIDE], f_ref[s, b:b + STRIDE, a:b], 0.0)
         corners.append(split(mmk(split(corner), small[s, a])))
     inverses = {}
     for (s, a), corner in zip(heads, corners):
@@ -176,8 +178,7 @@
         ]
 
     capacity = 2 * width // members
-    glue_copy.wait()
-    glue = glue_ref[...]
+    glue = jnp.concatenate([tails[0, :lines], tails[1, :lines]], axis=0).astype(jnp.int32)
     place = lax.axis_index("member")
     before = (iota((width, width), 0) < iota((width, width), 1)).astype(BF)
     dispatches = []
@@ -192,7 +193,7 @@
     for a in range(0, order, wide):
         solved = []
         for s in range(subs):
-            now = jnp.where(prow + a < sizes_ref[s], rest[s, a:a + wide], 0.0)
+            now = jnp.where(prow + a < lives[s], rest[s, a:a + wide], 0.0)
             solved.append(split(mm3(inverses[s, a], split(now))))
         if a + wide < order:
             for s in range(subs):
@@ -211,7 +212,7 @@
             out_refs[k][s * capacity:(s + 1) * capacity] = values[k * capacity:(k + 1) * capacity]
 
 
-def solve(sizes, glue, factors, panels, members):
+def solve(packed, factors, panels, members):
     subs, order, width = panels.shape
     capacity = 2 * width // members
     vm = pl.BlockSpec(memory_space=pltpu.VMEM)
@@ -219,37 +220,45 @@
     return pl.pallas_call(
         functools.partial(solve_kernel, members),
         out_shape=[jax.ShapeDtypeStruct((subs * capacity, width), F32)] * members,
-        in_specs=[far] * 4,
+        in_specs=[far] * 3,
         out_specs=[vm] * members,
         scratch_shapes=[
             pltpu.VMEM((subs, order, width), F32),
             pltpu.VMEM((subs, order, order), F32),
-            pltpu.SMEM((subs,), jnp.int32),
-            pltpu.VMEM((subs, width), jnp.int32),
+            pltpu.VMEM((2, tail_rows(subs), width), F32),
             pltpu.SemaphoreType.DMA((subs, order // STRIDE)),
             pltpu.SemaphoreType.DMA((subs, order // (2 * STRIDE))),
             pltpu.SemaphoreType.DMA((subs, order // (2 * STRIDE))),
             pltpu.SemaphoreType.DMA,
-            pltpu.SemaphoreType.DMA((2,)),
+            pltpu.SemaphoreType.DMA,
         ],
         compiler_params=pltpu.CompilerParams(vmem_limit_bytes=52 << 20),
         cost_estimate=pl.CostEstimate(flops=10_000_000_000, bytes_accessed=8 << 20, transcendentals=0),
         name="solve",
-    )(sizes, glue, factors, panels)
-
-
-def pack_kernel(loads_ref, glue_ref, out_ref, held, lines_of, tail, in_sems, load_sems, tail_sems):
+    )(packed, factors, panels)
+
+
+def tail_rows(subs):
+    return 8 * (-(-(subs // 2 + subs) // 8))
+
+
+def pack_kernel(loads_ref, glue_ref, sizes_ref, out_ref, held, lines_of, sizes_of, tail, in_sems, load_sems, tail_sems):
     members, rows, nrhs = out_ref.shape
-    half, lines = loads_ref.shape[0] // 2, glue_ref.shape[0] // 2
+    subs = glue_ref.shape[0]
+    half, lines = loads_ref.shape[0] // 2, subs // 2
     labels = pltpu.make_async_copy(glue_ref, lines_of, in_sems.at[0])
     load = pltpu.make_async_copy(loads_ref, held, in_sems.at[1])
+    sizes = pltpu.make_async_copy(sizes_ref, sizes_of, in_sems.at[2])
     labels.start()
+    sizes.start()
     load.start()
     labels.wait()
-    blank = jnp.zeros((rows - half - lines, nrhs), F32)
+    sizes.wait()
+    lives = [jnp.full((1, nrhs), sizes_of[s], jnp.int32).astype(F32) for s in range(subs)]
+    blank = [jnp.zeros((rows - half - lines - subs, nrhs), F32)]
     for part in range(2):
         line = lines_of[part * lines:(part + 1) * lines].astype(F32)
-        tail[part] = jnp.concatenate([line, blank], axis=0)
+        tail[part] = jnp.concatenate([line, *lives, *blank], axis=0)
     copies = []
     for k in range(members):
         copies.append(pltpu.make_async_copy(tail.at[k % 2], out_ref.at[k, pl.ds(half, rows - half)], tail_sems.at[k]))
@@ -263,28 +272,29 @@
         copy.wait()
 
 
-def pack(loads, glue, members):
+def pack(loads, glue, sizes, members):
     subs = glue.shape[0]
     share, nrhs = loads.shape
-    rows = share // 2 + 8 * (-(-subs // 16))
+    rows = share // 2 + tail_rows(subs)
     far = pl.BlockSpec(memory_space=pltpu.HBM)
     return pl.pallas_call(
         pack_kernel,
         out_shape=jax.ShapeDtypeStruct((members, rows, nrhs), F32),
-        in_specs=[far, far],
+        in_specs=[far] * 3,
         out_specs=far,
         scratch_shapes=[
             pltpu.VMEM((share, nrhs), F32),
             pltpu.VMEM(glue.shape, jnp.int32),
+            pltpu.SMEM(sizes.shape, jnp.int32),
             pltpu.VMEM((2, rows - share // 2, nrhs), F32),
-            pltpu.SemaphoreType.DMA((2,)),
+            pltpu.SemaphoreType.DMA((3,)),
             pltpu.SemaphoreType.DMA((members,)),
             pltpu.SemaphoreType.DMA((members,)),
         ],
         compiler_params=pltpu.CompilerParams(vmem_limit_bytes=58 << 20),
         cost_estimate=pl.CostEstimate(flops=1_000_000, bytes_accessed=1 << 20, transcendentals=0),
         name="pack",
-    )(loads, glue)
+    )(loads, glue, sizes)
 
 
 def routes_kernel(subs, place_ref, own_ref, twin_ref, stand_ref, label_ref, high_ref, low_ref):
@@ -380,9 +390,9 @@
     def across(value, distance):
         return lax.ppermute(value, "member", [(i, i ^ distance) for i in range(members)])
 
-    packed = pack(loads, glue_index, members)
+    packed = pack(loads, glue_index, sizes, members)
     own = lax.all_to_all(packed, "member", split_axis=0, concat_axis=0, tiled=True)
-    values = solve(sizes, glue_index, factors, panels, members)
+    values = solve(packed, factors, panels, members)
     own, *values = lax.optimization_barrier((own, *values))
     distances = [*range(2, members, 2), *range(3, members, 2), 1]
     arrived = {0: values[0], **{k: across(values[k], k) for k in distances}}

time: 43.4 us -> 43.1 us (level)
    unnamed x4 -> x2, local copies, waits for them, and re-layouts: 1.33 us -> 1.09 us
where the time goes in v9:
time: 43.1 us; the launch traced here: 42.8 us
  Pallas kernels  17 us (39%)
  starting transfers between devices  16 us (37%)
  waiting for transfers between devices  7.18 us (17%)
  local copies, waits for them, and re-layouts  1.17 us (3%)
  other arithmetic  0.74 us (2%)
  between operations  0.69 us (2%)
    pallas_call x1, Pallas kernels, solve(): pl.pallas_call(functools.partial(solve_kernel, members), out_shape=[jax.S...  9.51 us
    ppermute x8, starting transfers between devices, across(): lax.ppermute(value, 'member', [(i, i ^ distance) for i in range(members)])  6.99 us
    ppermute x8, waiting for transfers between devices, across(): lax.ppermute(value, 'member', [(i, i ^ distance) for i in range(members)])  5.63 us
    pallas_call x3, Pallas kernels, call(): pl.pallas_call(kernel, out_shape=outs, in_specs=specs, out_specs=jax.tree...  5.61 us
    all_to_all x1, starting transfers between devices, on_device(): lax.all_to_all(packed, 'member', split_axis=0, concat_axis=0, tiled=True)  5.18 us
    ppermute x1, starting transfers between devices, on_device(): after = lax.ppermute(first, 'cluster', down)  2.25 us
    pallas_call x1, Pallas kernels, pack(): pl.pallas_call(pack_kernel, out_shape=jax.ShapeDtypeStruct((members, rows...  1.91 us
    ppermute x1, starting transfers between devices, on_device(): before = lax.ppermute(last, 'cluster', up)  1.58 us
  transfers between devices with their start and end apart: 11, of which 5 were waited for; matrix products, arithmetic and copies ran while one was open for 0% of the time, Pallas kernels for 30%

profile of v9, /device:TPU:0, one launch (start us, length us, event | category | flops | bytes accessed | tf_op | source)
XLA Modules:
  0.0 42.8 jit_solution(6095181465623946832)
XLA Ops:
  0.6 1.9 %pack.1.packed_ref = f32[8,72,256]{2,1,0:T(8,128)} custom-call(f32[128,256]{1,0:T(8,128)} %loads_ref.1, s32[2,256]{1,0:T(2,128)} %glue_ref.1, s32[2]{0:T(128)} %sizes_ref.1), custom_call_target="tpu_custom_call" | custom-call | flops 1000000 | bytes 1048576 | tf_op jit(solution)/shard_map/pack/pallas_call | solution.py:280
  2.5 5.2 %all-to-all-start = ((f32[8,72,256]{2,1,0:T(8,128)}), f32[8,72,256]{2,1,0:T(8,128)S(1)}, u32[]{:S(2)}, u32[]{:S(2)}) async-start(f32[8,72,256]{2,1,0:T(8,128)} %pack.1.packed_ref), calls=%async_computation | async-start | bytes 1179648 | tf_op jit(solution)/shard_map/all_to_all | solution.py:394
  7.7 0.0 copy-start
  7.7 1.1 %copy-done = f32[8,72,256]{2,1,0:T(8,128)S(1)} copy-done((f32[8,72,256]{2,1,0:T(8,128)S(1)}, f32[8,72,256]{2,1,0:T(8,128)}, u32[]{:S(2)}) %copy-start) | copy-done | bytes 589848
  8.8 9.5 %solve.1 = (f32[128,256]{1,0:T(8,128)S(1)}, f32[128,256]{1,0:T(8,128)S(1)}, f32[128,256]{1,0:T(8,128)S(1)}, f32[128,256]{1,0:T(8,128)S(1)}, f32[128,256]{1,0:T(8...) custom-call(f32[8,72,256]{2,1,0:T(8,128)S(1)} %copy-done, ...), custom_call_target="tpu_custom_call" | custom-call | flops 10000000000 | bytes 8388608 | tf_op jit(solution)/shard_map/solve/pallas_call | solution.py:220
  18.3 0.0 all-to-all-done.own_ref
  18.4 0.6 %collective-permute-start = (f32[8,72,256]{2,1,0:T(8,128)S(1)}, f32[8,72,256]{2,1,0:T(8,128)S(1)}, u32[]{:S(2)}, u32[]{:S(2)}) collective-permute-start(f32[8,72,256]{2,1,0:T(8,128)S(1)} %all-to-all-done.own_ref), channel_id=1, source_target_pairs={{0,1},{1,0},{2,3},{3,2},{4,5},{5,4},{6,7},{7,6},{8,9},{9,8},{10,11... | collective-permute-start | bytes 1769480 | tf_op jit(solution)/shard_map/ppermute | solution.py:391
  18.9 1.7 %collective-permute-start.1 = (f32[128,256]{1,0:T(8,128)S(1)}, f32[128,256]{1,0:T(8,128)S(1)}, u32[]{:S(2)}, u32[]{:S(2)}) collective-permute-start(f32[128,256]{1,0:T(8,128)S(1)} %get-tuple-element.41), channel_id=1, source_target_pairs={{0,2},{1,3},{2,0},{3,1},{4,6},{5,7},{6,4},{7,5},{8,10},{9,11},{10,... | collective-permute-start | bytes 393224 | tf_op jit(solution)/shard_map/ppermute | solution.py:391
  20.6 1.5 %collective-permute-start.2 = (f32[128,256]{1,0:T(8,128)S(1)}, f32[128,256]{1,0:T(8,128)S(1)}, u32[]{:S(2)}, u32[]{:S(2)}) collective-permute-start(f32[128,256]{1,0:T(8,128)S(1)} %get-tuple-element.42), channel_id=1, source_target_pairs={{0,4},{1,5},{2,6},{3,7},{4,0},{5,1},{6,2},{7,3},{8,12},{9,13},{10,... | collective-permute-start | bytes 393224 | tf_op jit(solution)/shard_map/ppermute | solution.py:391
  22.1 0.3 collective-permute-start.3
  22.4 0.8 %collective-permute-start.4 = (f32[128,256]{1,0:T(8,128)S(1)}, f32[128,256]{1,0:T(8,128)S(1)}, u32[]{:S(2)}, u32[]{:S(2)}) collective-permute-start(f32[128,256]{1,0:T(8,128)S(1)} %get-tuple-element.44), channel_id=1, source_target_pairs={{0,3},{1,2},{2,1},{3,0},{4,7},{5,6},{6,5},{7,4},{8,11},{9,10},{10,... | collective-permute-start | bytes 393224 | tf_op jit(solution)/shard_map/ppermute | solution.py:391
  23.2 0.0 collective-permute-done.twin_ref
  23.2 1.0 %collective-permute-start.5 = (f32[128,256]{1,0:T(8,128)S(1)}, f32[128,256]{1,0:T(8,128)S(1)}, u32[]{:S(2)}, u32[]{:S(2)}) collective-permute-start(f32[128,256]{1,0:T(8,128)S(1)} %get-tuple-element.45), channel_id=1, source_target_pairs={{0,1},{1,0},{2,3},{3,2},{4,5},{5,4},{6,7},{7,6},{8,9},{9,8},{10,11... | collective-permute-start | bytes 393224 | tf_op jit(solution)/shard_map/ppermute | solution.py:391
  24.2 0.7 %routes.1 = (s32[256,16]{1,0:T(8,128)S(1)}, s32[8,128]{1,0:T(8,128)S(1)}, bf16[1024,256]{1,0:T(8,128)(2,1)S(1)}, bf16[1024,256]{1,0:T(8,128)(2,1)S(1)}) custom-call(s32[1]{0:T(128)} %bitcast.place_ref, f32[8,72,256]{2,1,0:T(8,128)S(1)} %all-to-all-done.own_ref, f32[8,72,256]{2,1,0:T(8,128)S(1)} %collective-permute-done.twin_ref), custom_call_target="tpu_custom_call" | custom-call | flops 2000000000 | bytes 4194304 | tf_op jit(solution)/shard_map/routes/pallas_call | solution.py:369
  24.9 0.0 collective-permute-done.1.refs_1_
  24.9 1.1 %collective-permute-start.6 = (f32[128,256]{1,0:T(8,128)S(1)}, f32[128,256]{1,0:T(8,128)S(1)}, u32[]{:S(2)}, u32[]{:S(2)}) collective-permute-start(f32[128,256]{1,0:T(8,128)S(1)} %get-tuple-element.46), channel_id=1, source_target_pairs={{0,5},{1,4},{2,7},{3,6},{4,1},{5,0},{6,3},{7,2},{8,13},{9,12},{10,... | collective-permute-start | bytes 393224 | tf_op jit(solution)/shard_map/ppermute | solution.py:391
  26.1 2.5 %collective-permute-done.2.refs_2_ = f32[128,256]{1,0:T(8,128)S(1)} collective-permute-done((f32[128,256]{1,0:T(8,128)S(1)}, f32[128,256]{1,0:T(8,128)S(1)}, u32[]{:S(2)}, u32[]{:S(2)}) %collective-permute-start.2) | collective-permute-done | bytes 131104 | tf_op jit(solution)/shard_map/ppermute | solution.py:391
  28.5 0.0 collective-permute-start.7
  28.5 0.9 %collective-permute-done.3.refs_3_ = f32[128,256]{1,0:T(8,128)S(1)} collective-permute-done((f32[128,256]{1,0:T(8,128)S(1)}, f32[128,256]{1,0:T(8,128)S(1)}, u32[]{:S(2)}, u32[]{:S(2)}) %collective-permute-start.3) | collective-permute-done | bytes 131104 | tf_op jit(solution)/shard_map/ppermute | solution.py:391
  29.4 0.1 collective-permute-done.4.refs_4_
  29.5 0.0 collective-permute-done.5.refs_5_
  29.5 2.8 %early.1.early_ref = f32[128,1024]{1,0:T(8,128)S(1)} custom-call(s32[8,128]{1,0:T(8,128)S(1)} %get-tuple-element.36.label_ref, s32[256,16]{1,0:T(8,128)S(1)} %get-tuple-element.37.stand_ref, f32[128,256]{1,0:T(8,128)S(1)} %get-tuple-element.40.refs_0_, f32[128,256]{1,0:T(8,128)S(1)} %collective-permute-done.1.refs_1_, ...), custom_call_target="tpu_custom_call" | custom-call | flops 2000000000 | bytes 4194304 | tf_op jit(solution)/shard_map/early/pallas_call | solution.py:369
  32.3 0.0 collective-permute-done.6.refs_0_
  32.3 2.1 %collective-permute-done.7.refs_1_ = f32[128,256]{1,0:T(8,128)S(1)} collective-permute-done((f32[128,256]{1,0:T(8,128)S(1)}, f32[128,256]{1,0:T(8,128)S(1)}, u32[]{:S(2)}, u32[]{:S(2)}) %collective-permute-start.7) | collective-permute-done | bytes 131104 | tf_op jit(solution)/shard_map/ppermute | solution.py:391
  34.5 2.1 %finish.1 = (f32[128,1024]{1,0:T(8,128)}, f32[128,256]{1,0:T(8,128)S(1)}, f32[8,256]{1,0:T(8,128)S(1)}, f32[8,256]{1,0:T(8,128)S(1)}) custom-call(s32[8,128]{1,0:T(8,128)S(1)} %get-tuple-element.36.label_ref, s32[256,16]{1,0:T(8,128)S(1)} %get-tuple-element.37.stand_ref, bf16[1024,256]{1,0:T(8,128)(2,1)S(1)} %get-tuple-element.38.high_ref, ...), custom_call_target="tpu_custom_call" | custom-call | flops 3000000000 | bytes 4194304 | tf_op jit(solution)/shard_map/finish/pallas_call | solution.py:369
  36.6 1.6 %collective-permute-start.8 = (f32[8,256]{1,0:T(8,128)S(1)}, f32[8,256]{1,0:T(8,128)S(1)}, u32[]{:S(2)}, u32[]{:S(2)}) collective-permute-start(f32[8,256]{1,0:T(8,128)S(1)} %get-tuple-element.50), channel_id=1, source_target_pairs={{0,8},{8,16},{16,24},{24,0},{1,9},{9,17},{17,25},{25,1},{2,10},{10... | collective-permute-start | bytes 24584 | tf_op jit(solution)/shard_map/ppermute | solution.py:437
  38.2 2.2 %collective-permute-start.9 = (f32[8,256]{1,0:T(8,128)S(1)}, f32[8,256]{1,0:T(8,128)S(1)}, u32[]{:S(2)}, u32[]{:S(2)}) collective-permute-start(f32[8,256]{1,0:T(8,128)S(1)} %get-tuple-element.51), channel_id=1, source_target_pairs={{8,0},{16,8},{24,16},{0,24},{9,1},{17,9},{25,17},{1,25},{10,2},{18... | collective-permute-start | bytes 24584 | tf_op jit(solution)/shard_map/ppermute | solution.py:438
  40.4 0.1 pad.1.clone
  40.5 1.5 %collective-permute-done.8 = f32[8,256]{1,0:T(8,128)S(1)} collective-permute-done((f32[8,256]{1,0:T(8,128)S(1)}, f32[8,256]{1,0:T(8,128)S(1)}, u32[]{:S(2)}, u32[]{:S(2)}) %collective-permute-start.8) | collective-permute-done | bytes 8224 | tf_op jit(solution)/shard_map/ppermute | solution.py:437
  42.1 0.0 collective-permute-done.9
  42.1 0.7 %maximum_add_fusion = f32[128,256]{1,0:T(8,128)} fusion(f32[128,256]{1,0:T(8,128)S(1)} %get-tuple-element.49, f32[8,256]{1,0:T(8,128)S(1)} %collective-permute-done.9, f32[8,256]{1,0:T(8,128)S(1)} %collective-permute-done.8, f32[128]{0:T(128)S(1)} %pad.1.clone), kind=kLoop, calls=%fused_computation | loop fusion | flops 98304 | bytes 279040 | tf_op jit(solution)/shard_map/add | solution.py:440
  (1 shorter events, 0.0 us)
Async XLA Ops:
  2.5 15.8 %all-to-all-start = ((f32[8,72,256]{2,1,0:T(8,128)}), f32[8,72,256]{2,1,0:T(8,128)S(1)}, u32[]{:S(2)}, u32[]{:S(2)}) async-start(f32[8,72,256]{2,1,0:T(8,128)} %pack.1.packed_ref), calls=%async_computation | async-start | bytes 1179648 | tf_op jit(solution)/shard_map/all_to_all | solution.py:394
  7.7 1.1 %copy-start = (f32[8,72,256]{2,1,0:T(8,128)S(1)}, f32[8,72,256]{2,1,0:T(8,128)}, u32[]{:S(2)}) copy-start(f32[8,72,256]{2,1,0:T(8,128)} %pack.1.packed_ref) | copy-start | bytes 1769476
  18.4 4.8 %collective-permute-start = (f32[8,72,256]{2,1,0:T(8,128)S(1)}, f32[8,72,256]{2,1,0:T(8,128)S(1)}, u32[]{:S(2)}, u32[]{:S(2)}) collective-permute-start(f32[8,72,256]{2,1,0:T(8,128)S(1)} %all-to-all-done.own_ref), channel_id=1, source_target_pairs={{0,1},{1,0},{2,3},{3,2},{4,5},{5,4},{6,7},{7,6},{8,9},{9,8},{10,11... | collective-permute-start | bytes 1769480 | tf_op jit(solution)/shard_map/ppermute | solution.py:391
  18.9 6.0 %collective-permute-start.1 = (f32[128,256]{1,0:T(8,128)S(1)}, f32[128,256]{1,0:T(8,128)S(1)}, u32[]{:S(2)}, u32[]{:S(2)}) collective-permute-start(f32[128,256]{1,0:T(8,128)S(1)} %get-tuple-element.41), channel_id=1, source_target_pairs={{0,2},{1,3},{2,0},{3,1},{4,6},{5,7},{6,4},{7,5},{8,10},{9,11},{10,... | collective-permute-start | bytes 393224 | tf_op jit(solution)/shard_map/ppermute | solution.py:391
  20.6 7.9 %collective-permute-start.2 = (f32[128,256]{1,0:T(8,128)S(1)}, f32[128,256]{1,0:T(8,128)S(1)}, u32[]{:S(2)}, u32[]{:S(2)}) collective-permute-start(f32[128,256]{1,0:T(8,128)S(1)} %get-tuple-element.42), channel_id=1, source_target_pairs={{0,4},{1,5},{2,6},{3,7},{4,0},{5,1},{6,2},{7,3},{8,12},{9,13},{10,... | collective-permute-start | bytes 393224 | tf_op jit(solution)/shard_map/ppermute | solution.py:391
  22.1 7.3 %collective-permute-start.3 = (f32[128,256]{1,0:T(8,128)S(1)}, f32[128,256]{1,0:T(8,128)S(1)}, u32[]{:S(2)}, u32[]{:S(2)}) collective-permute-start(f32[128,256]{1,0:T(8,128)S(1)} %get-tuple-element.43), channel_id=1, source_target_pairs={{0,6},{1,7},{2,4},{3,5},{4,2},{5,3},{6,0},{7,1},{8,14},{9,15},{10,... | collective-permute-start | bytes 393224 | tf_op jit(solution)/shard_map/ppermute | solution.py:391
  22.4 7.1 %collective-permute-start.4 = (f32[128,256]{1,0:T(8,128)S(1)}, f32[128,256]{1,0:T(8,128)S(1)}, u32[]{:S(2)}, u32[]{:S(2)}) collective-permute-start(f32[128,256]{1,0:T(8,128)S(1)} %get-tuple-element.44), channel_id=1, source_target_pairs={{0,3},{1,2},{2,1},{3,0},{4,7},{5,6},{6,5},{7,4},{8,11},{9,10},{10,... | collective-permute-start | bytes 393224 | tf_op jit(solution)/shard_map/ppermute | solution.py:391
  23.2 6.3 %collective-permute-start.5 = (f32[128,256]{1,0:T(8,128)S(1)}, f32[128,256]{1,0:T(8,128)S(1)}, u32[]{:S(2)}, u32[]{:S(2)}) collective-permute-start(f32[128,256]{1,0:T(8,128)S(1)} %get-tuple-element.45), channel_id=1, source_target_pairs={{0,1},{1,0},{2,3},{3,2},{4,5},{5,4},{6,7},{7,6},{8,9},{9,8},{10,11... | collective-permute-start | bytes 393224 | tf_op jit(solution)/shard_map/ppermute | solution.py:391
  24.9 7.4 %collective-permute-start.6 = (f32[128,256]{1,0:T(8,128)S(1)}, f32[128,256]{1,0:T(8,128)S(1)}, u32[]{:S(2)}, u32[]{:S(2)}) collective-permute-start(f32[128,256]{1,0:T(8,128)S(1)} %get-tuple-element.46), channel_id=1, source_target_pairs={{0,5},{1,4},{2,7},{3,6},{4,1},{5,0},{6,3},{7,2},{8,13},{9,12},{10,... | collective-permute-start | bytes 393224 | tf_op jit(solution)/shard_map/ppermute | solution.py:391
  28.5 6.0 %collective-permute-start.7 = (f32[128,256]{1,0:T(8,128)S(1)}, f32[128,256]{1,0:T(8,128)S(1)}, u32[]{:S(2)}, u32[]{:S(2)}) collective-permute-start(f32[128,256]{1,0:T(8,128)S(1)} %get-tuple-element.47), channel_id=1, source_target_pairs={{0,7},{1,6},{2,5},{3,4},{4,3},{5,2},{6,1},{7,0},{8,15},{9,14},{10,... | collective-permute-start | bytes 393224 | tf_op jit(solution)/shard_map/ppermute | solution.py:391
  36.6 5.4 %collective-permute-start.8 = (f32[8,256]{1,0:T(8,128)S(1)}, f32[8,256]{1,0:T(8,128)S(1)}, u32[]{:S(2)}, u32[]{:S(2)}) collective-permute-start(f32[8,256]{1,0:T(8,128)S(1)} %get-tuple-element.50), channel_id=1, source_target_pairs={{0,8},{8,16},{16,24},{24,0},{1,9},{9,17},{17,25},{25,1},{2,10},{10... | collective-permute-start | bytes 24584 | tf_op jit(solution)/shard_map/ppermute | solution.py:437
  38.2 3.9 %collective-permute-start.9 = (f32[8,256]{1,0:T(8,128)S(1)}, f32[8,256]{1,0:T(8,128)S(1)}, u32[]{:S(2)}, u32[]{:S(2)}) collective-permute-start(f32[8,256]{1,0:T(8,128)S(1)} %get-tuple-element.51), channel_id=1, source_target_pairs={{8,0},{16,8},{24,16},{0,24},{9,1},{17,9},{25,17},{1,25},{10,2},{18... | collective-permute-start | bytes 24584 | tf_op jit(solution)/shard_map/ppermute | solution.py:438

commit v10 on v9

--- a/solution.py
+++ b/solution.py
@@ -232,7 +232,7 @@
             pltpu.SemaphoreType.DMA,
             pltpu.SemaphoreType.DMA,
         ],
-        compiler_params=pltpu.CompilerParams(vmem_limit_bytes=52 << 20),
+        compiler_params=pltpu.CompilerParams(vmem_limit_bytes=53760 << 10),
         cost_estimate=pl.CostEstimate(flops=10_000_000_000, bytes_accessed=8 << 20, transcendentals=0),
         name="solve",
     )(packed, factors, panels)

time: 43.1 us -> 43 us (level)
  Pallas kernels: 17 us -> 18.2 us
  local copies, waits for them, and re-layouts: 1.17 us -> 0.08 us
    pallas_call x1, Pallas kernels: 9.51 us -> 10.7 us  [solve(): pl.pallas_call(functools.partial(solve_kernel, members), out_shape=[jax.S...]
    unnamed x2 -> x0, local copies, waits for them, and re-layouts: 1.09 us -> none
  transfers between devices with their start and end apart: 11 -> 11, of which waited for: 5 -> 5; matrix products, arithmetic and copies ran while one was open for 0% -> 0% of each run, Pallas kernels for 30% -> 33%
where the time goes in v10:
time: 43 us; the launch traced here: 42.8 us
  Pallas kernels  18.2 us (42%)
  starting transfers between devices  16 us (37%)
  waiting for transfers between devices  7.17 us (17%)
  other arithmetic  0.74 us (2%)
  between operations  0.68 us (2%)
    pallas_call x1, Pallas kernels, solve(): pl.pallas_call(functools.partial(solve_kernel, members), out_shape=[jax.S...  10.7 us
    ppermute x8, starting transfers between devices, across(): lax.ppermute(value, 'member', [(i, i ^ distance) for i in range(members)])  6.99 us
    ppermute x8, waiting for transfers between devices, across(): lax.ppermute(value, 'member', [(i, i ^ distance) for i in range(members)])  5.62 us
    pallas_call x3, Pallas kernels, call(): pl.pallas_call(kernel, out_shape=outs, in_specs=specs, out_specs=jax.tree...  5.61 us
    all_to_all x1, starting transfers between devices, on_device(): lax.all_to_all(packed, 'member', split_axis=0, concat_axis=0, tiled=True)  5.18 us
    ppermute x1, starting transfers between devices, on_device(): after = lax.ppermute(first, 'cluster', down)  2.26 us
    pallas_call x1, Pallas kernels, pack(): pl.pallas_call(pack_kernel, out_shape=jax.ShapeDtypeStruct((members, rows...  1.88 us
    ppermute x1, starting transfers between devices, on_device(): before = lax.ppermute(last, 'cluster', up)  1.56 us
  transfers between devices with their start and end apart: 11, of which 5 were waited for; matrix products, arithmetic and copies ran while one was open for 0% of the time, Pallas kernels for 33%

profile of v10, /device:TPU:0, one launch (start us, length us, event | category | flops | bytes accessed | tf_op | source)
XLA Modules:
  0.0 42.8 jit_solution(8014008520205717037)
XLA Ops:
  0.6 1.9 %pack.1.packed_ref = f32[8,72,256]{2,1,0:T(8,128)} custom-call(f32[128,256]{1,0:T(8,128)} %loads_ref.1, s32[2,256]{1,0:T(2,128)} %glue_ref.1, s32[2]{0:T(128)} %sizes_ref.1), custom_call_target="tpu_custom_call" | custom-call | flops 1000000 | bytes 1048576 | tf_op jit(solution)/shard_map/pack/pallas_call | solution.py:280
  2.5 5.2 %all-to-all-start = ((f32[8,72,256]{2,1,0:T(8,128)}), f32[8,72,256]{2,1,0:T(8,128)S(1)}, u32[]{:S(2)}, u32[]{:S(2)}) async-start(f32[8,72,256]{2,1,0:T(8,128)} %pack.1.packed_ref), calls=%async_computation | async-start | bytes 1179648 | tf_op jit(solution)/shard_map/all_to_all | solution.py:394
  7.7 10.7 %solve.1 = (f32[128,256]{1,0:T(8,128)S(1)}, f32[128,256]{1,0:T(8,128)S(1)}, f32[128,256]{1,0:T(8,128)S(1)}, f32[128,256]{1,0:T(8,128)S(1)}, f32[128,256]{1,0:T(8...) custom-call(f32[8,72,256]{2,1,0:T(8,128)} %pack.1.packed_ref, ...), custom_call_target="tpu_custom_call" | custom-call | flops 10000000000 | bytes 8388608 | tf_op jit(solution)/shard_map/solve/pallas_call | solution.py:220
  18.4 0.0 all-to-all-done.own_ref
  18.4 0.6 %collective-permute-start = (f32[8,72,256]{2,1,0:T(8,128)S(1)}, f32[8,72,256]{2,1,0:T(8,128)S(1)}, u32[]{:S(2)}, u32[]{:S(2)}) collective-permute-start(f32[8,72,256]{2,1,0:T(8,128)S(1)} %all-to-all-done.own_ref), channel_id=1, source_target_pairs={{0,1},{1,0},{2,3},{3,2},{4,5},{5,4},{6,7},{7,6},{8,9},{9,8},{10,11... | collective-permute-start | bytes 1769480 | tf_op jit(solution)/shard_map/ppermute | solution.py:391
  19.0 1.7 %collective-permute-start.1 = (f32[128,256]{1,0:T(8,128)S(1)}, f32[128,256]{1,0:T(8,128)S(1)}, u32[]{:S(2)}, u32[]{:S(2)}) collective-permute-start(f32[128,256]{1,0:T(8,128)S(1)} %get-tuple-element.41), channel_id=1, source_target_pairs={{0,2},{1,3},{2,0},{3,1},{4,6},{5,7},{6,4},{7,5},{8,10},{9,11},{10,... | collective-permute-start | bytes 393224 | tf_op jit(solution)/shard_map/ppermute | solution.py:391
  20.6 1.5 %collective-permute-start.2 = (f32[128,256]{1,0:T(8,128)S(1)}, f32[128,256]{1,0:T(8,128)S(1)}, u32[]{:S(2)}, u32[]{:S(2)}) collective-permute-start(f32[128,256]{1,0:T(8,128)S(1)} %get-tuple-element.42), channel_id=1, source_target_pairs={{0,4},{1,5},{2,6},{3,7},{4,0},{5,1},{6,2},{7,3},{8,12},{9,13},{10,... | collective-permute-start | bytes 393224 | tf_op jit(solution)/shard_map/ppermute | solution.py:391
  22.1 0.4 collective-permute-start.3
  22.5 0.8 %collective-permute-start.4 = (f32[128,256]{1,0:T(8,128)S(1)}, f32[128,256]{1,0:T(8,128)S(1)}, u32[]{:S(2)}, u32[]{:S(2)}) collective-permute-start(f32[128,256]{1,0:T(8,128)S(1)} %get-tuple-element.44), channel_id=1, source_target_pairs={{0,3},{1,2},{2,1},{3,0},{4,7},{5,6},{6,5},{7,4},{8,11},{9,10},{10,... | collective-permute-start | bytes 393224 | tf_op jit(solution)/shard_map/ppermute | solution.py:391
  23.2 0.0 collective-permute-done.twin_ref
  23.2 1.0 %collective-permute-start.5 = (f32[128,256]{1,0:T(8,128)S(1)}, f32[128,256]{1,0:T(8,128)S(1)}, u32[]{:S(2)}, u32[]{:S(2)}) collective-permute-start(f32[128,256]{1,0:T(8,128)S(1)} %get-tuple-element.45), channel_id=1, source_target_pairs={{0,1},{1,0},{2,3},{3,2},{4,5},{5,4},{6,7},{7,6},{8,9},{9,8},{10,11... | collective-permute-start | bytes 393224 | tf_op jit(solution)/shard_map/ppermute | solution.py:391
  24.2 0.7 %routes.1 = (s32[256,16]{1,0:T(8,128)S(1)}, s32[8,128]{1,0:T(8,128)S(1)}, bf16[1024,256]{1,0:T(8,128)(2,1)S(1)}, bf16[1024,256]{1,0:T(8,128)(2,1)S(1)}) custom-call(s32[1]{0:T(128)} %bitcast.place_ref, f32[8,72,256]{2,1,0:T(8,128)S(1)} %all-to-all-done.own_ref, f32[8,72,256]{2,1,0:T(8,128)S(1)} %collective-permute-done.twin_ref), custom_call_target="tpu_custom_call" | custom-call | flops 2000000000 | bytes 4194304 | tf_op jit(solution)/shard_map/routes/pallas_call | solution.py:369
  24.9 0.0 collective-permute-done.1.refs_1_
  24.9 1.1 %collective-permute-start.6 = (f32[128,256]{1,0:T(8,128)S(1)}, f32[128,256]{1,0:T(8,128)S(1)}, u32[]{:S(2)}, u32[]{:S(2)}) collective-permute-start(f32[128,256]{1,0:T(8,128)S(1)} %get-tuple-element.46), channel_id=1, source_target_pairs={{0,5},{1,4},{2,7},{3,6},{4,1},{5,0},{6,3},{7,2},{8,13},{9,12},{10,... | collective-permute-start | bytes 393224 | tf_op jit(solution)/shard_map/ppermute | solution.py:391
  26.1 2.5 %collective-permute-done.2.refs_2_ = f32[128,256]{1,0:T(8,128)S(1)} collective-permute-done((f32[128,256]{1,0:T(8,128)S(1)}, f32[128,256]{1,0:T(8,128)S(1)}, u32[]{:S(2)}, u32[]{:S(2)}) %collective-permute-start.2) | collective-permute-done | bytes 131104 | tf_op jit(solution)/shard_map/ppermute | solution.py:391
  28.6 0.0 collective-permute-start.7
  28.6 0.9 %collective-permute-done.3.refs_3_ = f32[128,256]{1,0:T(8,128)S(1)} collective-permute-done((f32[128,256]{1,0:T(8,128)S(1)}, f32[128,256]{1,0:T(8,128)S(1)}, u32[]{:S(2)}, u32[]{:S(2)}) %collective-permute-start.3) | collective-permute-done | bytes 131104 | tf_op jit(solution)/shard_map/ppermute | solution.py:391
  29.4 0.1 collective-permute-done.4.refs_4_
  29.6 0.0 collective-permute-done.5.refs_5_
  29.6 2.8 %early.1.early_ref = f32[128,1024]{1,0:T(8,128)S(1)} custom-call(s32[8,128]{1,0:T(8,128)S(1)} %get-tuple-element.36.label_ref, s32[256,16]{1,0:T(8,128)S(1)} %get-tuple-element.37.stand_ref, f32[128,256]{1,0:T(8,128)S(1)} %get-tuple-element.40.refs_0_, f32[128,256]{1,0:T(8,128)S(1)} %collective-permute-done.1.refs_1_, ...), custom_call_target="tpu_custom_call" | custom-call | flops 2000000000 | bytes 4194304 | tf_op jit(solution)/shard_map/early/pallas_call | solution.py:369
  32.4 0.0 collective-permute-done.6.refs_0_
  32.4 2.1 %collective-permute-done.7.refs_1_ = f32[128,256]{1,0:T(8,128)S(1)} collective-permute-done((f32[128,256]{1,0:T(8,128)S(1)}, f32[128,256]{1,0:T(8,128)S(1)}, u32[]{:S(2)}, u32[]{:S(2)}) %collective-permute-start.7) | collective-permute-done | bytes 131104 | tf_op jit(solution)/shard_map/ppermute | solution.py:391
  34.5 2.1 %finish.1 = (f32[128,1024]{1,0:T(8,128)}, f32[128,256]{1,0:T(8,128)S(1)}, f32[8,256]{1,0:T(8,128)S(1)}, f32[8,256]{1,0:T(8,128)S(1)}) custom-call(s32[8,128]{1,0:T(8,128)S(1)} %get-tuple-element.36.label_ref, s32[256,16]{1,0:T(8,128)S(1)} %get-tuple-element.37.stand_ref, bf16[1024,256]{1,0:T(8,128)(2,1)S(1)} %get-tuple-element.38.high_ref, ...), custom_call_target="tpu_custom_call" | custom-call | flops 3000000000 | bytes 4194304 | tf_op jit(solution)/shard_map/finish/pallas_call | solution.py:369
  36.6 1.6 %collective-permute-start.8 = (f32[8,256]{1,0:T(8,128)S(1)}, f32[8,256]{1,0:T(8,128)S(1)}, u32[]{:S(2)}, u32[]{:S(2)}) collective-permute-start(f32[8,256]{1,0:T(8,128)S(1)} %get-tuple-element.50), channel_id=1, source_target_pairs={{0,8},{8,16},{16,24},{24,0},{1,9},{9,17},{17,25},{25,1},{2,10},{10... | collective-permute-start | bytes 24584 | tf_op jit(solution)/shard_map/ppermute | solution.py:437
  38.2 2.3 %collective-permute-start.9 = (f32[8,256]{1,0:T(8,128)S(1)}, f32[8,256]{1,0:T(8,128)S(1)}, u32[]{:S(2)}, u32[]{:S(2)}) collective-permute-start(f32[8,256]{1,0:T(8,128)S(1)} %get-tuple-element.51), channel_id=1, source_target_pairs={{8,0},{16,8},{24,16},{0,24},{9,1},{17,9},{25,17},{1,25},{10,2},{18... | collective-permute-start | bytes 24584 | tf_op jit(solution)/shard_map/ppermute | solution.py:438
  40.4 0.1 pad.1.clone
  40.5 1.5 %collective-permute-done.8 = f32[8,256]{1,0:T(8,128)S(1)} collective-permute-done((f32[8,256]{1,0:T(8,128)S(1)}, f32[8,256]{1,0:T(8,128)S(1)}, u32[]{:S(2)}, u32[]{:S(2)}) %collective-permute-start.8) | collective-permute-done | bytes 8224 | tf_op jit(solution)/shard_map/ppermute | solution.py:437
  42.1 0.0 collective-permute-done.9
  42.1 0.7 %maximum_add_fusion = f32[128,256]{1,0:T(8,128)} fusion(f32[128,256]{1,0:T(8,128)S(1)} %get-tuple-element.49, f32[8,256]{1,0:T(8,128)S(1)} %collective-permute-done.9, f32[8,256]{1,0:T(8,128)S(1)} %collective-permute-done.8, f32[128]{0:T(128)S(1)} %pad.1.clone), kind=kLoop, calls=%fused_computation | loop fusion | flops 98304 | bytes 279040 | tf_op jit(solution)/shard_map/add | solution.py:440
  (1 shorter events, 0.0 us)
Async XLA Ops:
  2.5 15.9 %all-to-all-start = ((f32[8,72,256]{2,1,0:T(8,128)}), f32[8,72,256]{2,1,0:T(8,128)S(1)}, u32[]{:S(2)}, u32[]{:S(2)}) async-start(f32[8,72,256]{2,1,0:T(8,128)} %pack.1.packed_ref), calls=%async_computation | async-start | bytes 1179648 | tf_op jit(solution)/shard_map/all_to_all | solution.py:394
  18.4 4.9 %collective-permute-start = (f32[8,72,256]{2,1,0:T(8,128)S(1)}, f32[8,72,256]{2,1,0:T(8,128)S(1)}, u32[]{:S(2)}, u32[]{:S(2)}) collective-permute-start(f32[8,72,256]{2,1,0:T(8,128)S(1)} %all-to-all-done.own_ref), channel_id=1, source_target_pairs={{0,1},{1,0},{2,3},{3,2},{4,5},{5,4},{6,7},{7,6},{8,9},{9,8},{10,11... | collective-permute-start | bytes 1769480 | tf_op jit(solution)/shard_map/ppermute | solution.py:391
  19.0 6.0 %collective-permute-start.1 = (f32[128,256]{1,0:T(8,128)S(1)}, f32[128,256]{1,0:T(8,128)S(1)}, u32[]{:S(2)}, u32[]{:S(2)}) collective-permute-start(f32[128,256]{1,0:T(8,128)S(1)} %get-tuple-element.41), channel_id=1, source_target_pairs={{0,2},{1,3},{2,0},{3,1},{4,6},{5,7},{6,4},{7,5},{8,10},{9,11},{10,... | collective-permute-start | bytes 393224 | tf_op jit(solution)/shard_map/ppermute | solution.py:391
  20.6 7.9 %collective-permute-start.2 = (f32[128,256]{1,0:T(8,128)S(1)}, f32[128,256]{1,0:T(8,128)S(1)}, u32[]{:S(2)}, u32[]{:S(2)}) collective-permute-start(f32[128,256]{1,0:T(8,128)S(1)} %get-tuple-element.42), channel_id=1, source_target_pairs={{0,4},{1,5},{2,6},{3,7},{4,0},{5,1},{6,2},{7,3},{8,12},{9,13},{10,... | collective-permute-start | bytes 393224 | tf_op jit(solution)/shard_map/ppermute | solution.py:391
  22.1 7.3 %collective-permute-start.3 = (f32[128,256]{1,0:T(8,128)S(1)}, f32[128,256]{1,0:T(8,128)S(1)}, u32[]{:S(2)}, u32[]{:S(2)}) collective-permute-start(f32[128,256]{1,0:T(8,128)S(1)} %get-tuple-element.43), channel_id=1, source_target_pairs={{0,6},{1,7},{2,4},{3,5},{4,2},{5,3},{6,0},{7,1},{8,14},{9,15},{10,... | collective-permute-start | bytes 393224 | tf_op jit(solution)/shard_map/ppermute | solution.py:391
  22.5 7.1 %collective-permute-start.4 = (f32[128,256]{1,0:T(8,128)S(1)}, f32[128,256]{1,0:T(8,128)S(1)}, u32[]{:S(2)}, u32[]{:S(2)}) collective-permute-start(f32[128,256]{1,0:T(8,128)S(1)} %get-tuple-element.44), channel_id=1, source_target_pairs={{0,3},{1,2},{2,1},{3,0},{4,7},{5,6},{6,5},{7,4},{8,11},{9,10},{10,... | collective-permute-start | bytes 393224 | tf_op jit(solution)/shard_map/ppermute | solution.py:391
  23.2 6.3 %collective-permute-start.5 = (f32[128,256]{1,0:T(8,128)S(1)}, f32[128,256]{1,0:T(8,128)S(1)}, u32[]{:S(2)}, u32[]{:S(2)}) collective-permute-start(f32[128,256]{1,0:T(8,128)S(1)} %get-tuple-element.45), channel_id=1, source_target_pairs={{0,1},{1,0},{2,3},{3,2},{4,5},{5,4},{6,7},{7,6},{8,9},{9,8},{10,11... | collective-permute-start | bytes 393224 | tf_op jit(solution)/shard_map/ppermute | solution.py:391
  24.9 7.4 %collective-permute-start.6 = (f32[128,256]{1,0:T(8,128)S(1)}, f32[128,256]{1,0:T(8,128)S(1)}, u32[]{:S(2)}, u32[]{:S(2)}) collective-permute-start(f32[128,256]{1,0:T(8,128)S(1)} %get-tuple-element.46), channel_id=1, source_target_pairs={{0,5},{1,4},{2,7},{3,6},{4,1},{5,0},{6,3},{7,2},{8,13},{9,12},{10,... | collective-permute-start | bytes 393224 | tf_op jit(solution)/shard_map/ppermute | solution.py:391
  28.6 5.9 %collective-permute-start.7 = (f32[128,256]{1,0:T(8,128)S(1)}, f32[128,256]{1,0:T(8,128)S(1)}, u32[]{:S(2)}, u32[]{:S(2)}) collective-permute-start(f32[128,256]{1,0:T(8,128)S(1)} %get-tuple-element.47), channel_id=1, source_target_pairs={{0,7},{1,6},{2,5},{3,4},{4,3},{5,2},{6,1},{7,0},{8,15},{9,14},{10,... | collective-permute-start | bytes 393224 | tf_op jit(solution)/shard_map/ppermute | solution.py:391
  36.6 5.4 %collective-permute-start.8 = (f32[8,256]{1,0:T(8,128)S(1)}, f32[8,256]{1,0:T(8,128)S(1)}, u32[]{:S(2)}, u32[]{:S(2)}) collective-permute-start(f32[8,256]{1,0:T(8,128)S(1)} %get-tuple-element.50), channel_id=1, source_target_pairs={{0,8},{8,16},{16,24},{24,0},{1,9},{9,17},{17,25},{25,1},{2,10},{10... | collective-permute-start | bytes 24584 | tf_op jit(solution)/shard_map/ppermute | solution.py:437
  38.2 3.9 %collective-permute-start.9 = (f32[8,256]{1,0:T(8,128)S(1)}, f32[8,256]{1,0:T(8,128)S(1)}, u32[]{:S(2)}, u32[]{:S(2)}) collective-permute-start(f32[8,256]{1,0:T(8,128)S(1)} %get-tuple-element.51), channel_id=1, source_target_pairs={{8,0},{16,8},{24,16},{0,24},{9,1},{17,9},{25,17},{1,25},{10,2},{18... | collective-permute-start | bytes 24584 | tf_op jit(solution)/shard_map/ppermute | solution.py:438

commit v11 on v10

--- a/solution.py
+++ b/solution.py
@@ -117,7 +117,6 @@
     extra = tails.shape[1]
     ends = packed_ref.at[pl.ds(0, 2), pl.ds(packed_ref.shape[1] - extra, extra)]
     small_copy = pltpu.make_async_copy(ends, tails, small_sem)
-    small_copy.start()
     subs, order, width = p_ref.shape
     wide = 2 * STRIDE
     square_copies, corner_copies, strip_copies = {}, {}, {}
@@ -131,6 +130,7 @@
     for step, a in enumerate(range(0, order, STRIDE)):
         for s in range(subs):
             square_copies[s, a] = fetch(s, pl.ds(a, STRIDE), pl.ds(a, STRIDE), square_sems.at[s, step])
+    small_copy.start()
     for step, a in enumerate(range(0, order, wide)):
         for s in range(subs):
             corner_copies[s, a] = fetch(s, pl.ds(a + STRIDE, STRIDE), pl.ds(a, STRIDE), corner_sems.at[s, step])

time: 43 us -> 43 us (level)
  no operation moved by 1% of the time
where the time goes in v11:
time: 43 us; the launch traced here: 42.8 us
  Pallas kernels  18.2 us (42%)
  starting transfers between devices  16 us (37%)
  waiting for transfers between devices  7.17 us (17%)
  other arithmetic  0.74 us (2%)
  between operations  0.68 us (2%)
    pallas_call x1, Pallas kernels, solve(): pl.pallas_call(functools.partial(solve_kernel, members), out_shape=[jax.S...  10.7 us
    ppermute x8, starting transfers between devices, across(): lax.ppermute(value, 'member', [(i, i ^ distance) for i in range(members)])  6.99 us
    ppermute x8, waiting for transfers between devices, across(): lax.ppermute(value, 'member', [(i, i ^ distance) for i in range(members)])  5.62 us
    pallas_call x3, Pallas kernels, call(): pl.pallas_call(kernel, out_shape=outs, in_specs=specs, out_specs=jax.tree...  5.61 us
    all_to_all x1, starting transfers between devices, on_device(): lax.all_to_all(packed, 'member', split_axis=0, concat_axis=0, tiled=True)  5.18 us
    ppermute x1, starting transfers between devices, on_device(): after = lax.ppermute(first, 'cluster', down)  2.26 us
    pallas_call x1, Pallas kernels, pack(): pl.pallas_call(pack_kernel, out_shape=jax.ShapeDtypeStruct((members, rows...  1.88 us
    ppermute x1, starting transfers between devices, on_device(): before = lax.ppermute(last, 'cluster', up)  1.56 us
  transfers between devices with their start and end apart: 11, of which 5 were waited for; matrix products, arithmetic and copies ran while one was open for 0% of the time, Pallas kernels for 33%

profile of v11, /device:TPU:0, one launch (start us, length us, event | category | flops | bytes accessed | tf_op | source)
XLA Modules:
  0.0 42.8 jit_solution(8014008520205717037)
XLA Ops:
  0.6 1.9 %pack.1.packed_ref = f32[8,72,256]{2,1,0:T(8,128)} custom-call(f32[128,256]{1,0:T(8,128)} %loads_ref.1, s32[2,256]{1,0:T(2,128)} %glue_ref.1, s32[2]{0:T(128)} %sizes_ref.1), custom_call_target="tpu_custom_call" | custom-call | flops 1000000 | bytes 1048576 | tf_op jit(solution)/shard_map/pack/pallas_call | solution.py:280
  2.5 5.2 %all-to-all-start = ((f32[8,72,256]{2,1,0:T(8,128)}), f32[8,72,256]{2,1,0:T(8,128)S(1)}, u32[]{:S(2)}, u32[]{:S(2)}) async-start(f32[8,72,256]{2,1,0:T(8,128)} %pack.1.packed_ref), calls=%async_computation | async-start | bytes 1179648 | tf_op jit(solution)/shard_map/all_to_all | solution.py:394
  7.7 10.7 %solve.1 = (f32[128,256]{1,0:T(8,128)S(1)}, f32[128,256]{1,0:T(8,128)S(1)}, f32[128,256]{1,0:T(8,128)S(1)}, f32[128,256]{1,0:T(8,128)S(1)}, f32[128,256]{1,0:T(8...) custom-call(f32[8,72,256]{2,1,0:T(8,128)} %pack.1.packed_ref, ...), custom_call_target="tpu_custom_call" | custom-call | flops 10000000000 | bytes 8388608 | tf_op jit(solution)/shard_map/solve/pallas_call | solution.py:220
  18.4 0.0 all-to-all-done.own_ref
  18.4 0.6 %collective-permute-start = (f32[8,72,256]{2,1,0:T(8,128)S(1)}, f32[8,72,256]{2,1,0:T(8,128)S(1)}, u32[]{:S(2)}, u32[]{:S(2)}) collective-permute-start(f32[8,72,256]{2,1,0:T(8,128)S(1)} %all-to-all-done.own_ref), channel_id=1, source_target_pairs={{0,1},{1,0},{2,3},{3,2},{4,5},{5,4},{6,7},{7,6},{8,9},{9,8},{10,11... | collective-permute-start | bytes 1769480 | tf_op jit(solution)/shard_map/ppermute | solution.py:391
  19.0 1.7 %collective-permute-start.1 = (f32[128,256]{1,0:T(8,128)S(1)}, f32[128,256]{1,0:T(8,128)S(1)}, u32[]{:S(2)}, u32[]{:S(2)}) collective-permute-start(f32[128,256]{1,0:T(8,128)S(1)} %get-tuple-element.41), channel_id=1, source_target_pairs={{0,2},{1,3},{2,0},{3,1},{4,6},{5,7},{6,4},{7,5},{8,10},{9,11},{10,... | collective-permute-start | bytes 393224 | tf_op jit(solution)/shard_map/ppermute | solution.py:391
  20.6 1.5 %collective-permute-start.2 = (f32[128,256]{1,0:T(8,128)S(1)}, f32[128,256]{1,0:T(8,128)S(1)}, u32[]{:S(2)}, u32[]{:S(2)}) collective-permute-start(f32[128,256]{1,0:T(8,128)S(1)} %get-tuple-element.42), channel_id=1, source_target_pairs={{0,4},{1,5},{2,6},{3,7},{4,0},{5,1},{6,2},{7,3},{8,12},{9,13},{10,... | collective-permute-start | bytes 393224 | tf_op jit(solution)/shard_map/ppermute | solution.py:391
  22.1 0.4 collective-permute-start.3
  22.5 0.8 %collective-permute-start.4 = (f32[128,256]{1,0:T(8,128)S(1)}, f32[128,256]{1,0:T(8,128)S(1)}, u32[]{:S(2)}, u32[]{:S(2)}) collective-permute-start(f32[128,256]{1,0:T(8,128)S(1)} %get-tuple-element.44), channel_id=1, source_target_pairs={{0,3},{1,2},{2,1},{3,0},{4,7},{5,6},{6,5},{7,4},{8,11},{9,10},{10,... | collective-permute-start | bytes 393224 | tf_op jit(solution)/shard_map/ppermute | solution.py:391
  23.2 0.0 collective-permute-done.twin_ref
  23.2 1.0 %collective-permute-start.5 = (f32[128,256]{1,0:T(8,128)S(1)}, f32[128,256]{1,0:T(8,128)S(1)}, u32[]{:S(2)}, u32[]{:S(2)}) collective-permute-start(f32[128,256]{1,0:T(8,128)S(1)} %get-tuple-element.45), channel_id=1, source_target_pairs={{0,1},{1,0},{2,3},{3,2},{4,5},{5,4},{6,7},{7,6},{8,9},{9,8},{10,11... | collective-permute-start | bytes 393224 | tf_op jit(solution)/shard_map/ppermute | solution.py:391
  24.2 0.7 %routes.1 = (s32[256,16]{1,0:T(8,128)S(1)}, s32[8,128]{1,0:T(8,128)S(1)}, bf16[1024,256]{1,0:T(8,128)(2,1)S(1)}, bf16[1024,256]{1,0:T(8,128)(2,1)S(1)}) custom-call(s32[1]{0:T(128)} %bitcast.place_ref, f32[8,72,256]{2,1,0:T(8,128)S(1)} %all-to-all-done.own_ref, f32[8,72,256]{2,1,0:T(8,128)S(1)} %collective-permute-done.twin_ref), custom_call_target="tpu_custom_call" | custom-call | flops 2000000000 | bytes 4194304 | tf_op jit(solution)/shard_map/routes/pallas_call | solution.py:369
  24.9 0.0 collective-permute-done.1.refs_1_
  24.9 1.1 %collective-permute-start.6 = (f32[128,256]{1,0:T(8,128)S(1)}, f32[128,256]{1,0:T(8,128)S(1)}, u32[]{:S(2)}, u32[]{:S(2)}) collective-permute-start(f32[128,256]{1,0:T(8,128)S(1)} %get-tuple-element.46), channel_id=1, source_target_pairs={{0,5},{1,4},{2,7},{3,6},{4,1},{5,0},{6,3},{7,2},{8,13},{9,12},{10,... | collective-permute-start | bytes 393224 | tf_op jit(solution)/shard_map/ppermute | solution.py:391
  26.1 2.5 %collective-permute-done.2.refs_2_ = f32[128,256]{1,0:T(8,128)S(1)} collective-permute-done((f32[128,256]{1,0:T(8,128)S(1)}, f32[128,256]{1,0:T(8,128)S(1)}, u32[]{:S(2)}, u32[]{:S(2)}) %collective-permute-start.2) | collective-permute-done | bytes 131104 | tf_op jit(solution)/shard_map/ppermute | solution.py:391
  28.6 0.0 collective-permute-start.7
  28.6 0.9 %collective-permute-done.3.refs_3_ = f32[128,256]{1,0:T(8,128)S(1)} collective-permute-done((f32[128,256]{1,0:T(8,128)S(1)}, f32[128,256]{1,0:T(8,128)S(1)}, u32[]{:S(2)}, u32[]{:S(2)}) %collective-permute-start.3) | collective-permute-done | bytes 131104 | tf_op jit(solution)/shard_map/ppermute | solution.py:391
  29.4 0.1 collective-permute-done.4.refs_4_
  29.6 0.0 collective-permute-done.5.refs_5_
  29.6 2.8 %early.1.early_ref = f32[128,1024]{1,0:T(8,128)S(1)} custom-call(s32[8,128]{1,0:T(8,128)S(1)} %get-tuple-element.36.label_ref, s32[256,16]{1,0:T(8,128)S(1)} %get-tuple-element.37.stand_ref, f32[128,256]{1,0:T(8,128)S(1)} %get-tuple-element.40.refs_0_, f32[128,256]{1,0:T(8,128)S(1)} %collective-permute-done.1.refs_1_, ...), custom_call_target="tpu_custom_call" | custom-call | flops 2000000000 | bytes 4194304 | tf_op jit(solution)/shard_map/early/pallas_call | solution.py:369
  32.4 0.0 collective-permute-done.6.refs_0_
  32.4 2.1 %collective-permute-done.7.refs_1_ = f32[128,256]{1,0:T(8,128)S(1)} collective-permute-done((f32[128,256]{1,0:T(8,128)S(1)}, f32[128,256]{1,0:T(8,128)S(1)}, u32[]{:S(2)}, u32[]{:S(2)}) %collective-permute-start.7) | collective-permute-done | bytes 131104 | tf_op jit(solution)/shard_map/ppermute | solution.py:391
  34.5 2.1 %finish.1 = (f32[128,1024]{1,0:T(8,128)}, f32[128,256]{1,0:T(8,128)S(1)}, f32[8,256]{1,0:T(8,128)S(1)}, f32[8,256]{1,0:T(8,128)S(1)}) custom-call(s32[8,128]{1,0:T(8,128)S(1)} %get-tuple-element.36.label_ref, s32[256,16]{1,0:T(8,128)S(1)} %get-tuple-element.37.stand_ref, bf16[1024,256]{1,0:T(8,128)(2,1)S(1)} %get-tuple-element.38.high_ref, ...), custom_call_target="tpu_custom_call" | custom-call | flops 3000000000 | bytes 4194304 | tf_op jit(solution)/shard_map/finish/pallas_call | solution.py:369
  36.6 1.6 %collective-permute-start.8 = (f32[8,256]{1,0:T(8,128)S(1)}, f32[8,256]{1,0:T(8,128)S(1)}, u32[]{:S(2)}, u32[]{:S(2)}) collective-permute-start(f32[8,256]{1,0:T(8,128)S(1)} %get-tuple-element.50), channel_id=1, source_target_pairs={{0,8},{8,16},{16,24},{24,0},{1,9},{9,17},{17,25},{25,1},{2,10},{10... | collective-permute-start | bytes 24584 | tf_op jit(solution)/shard_map/ppermute | solution.py:437
  38.2 2.3 %collective-permute-start.9 = (f32[8,256]{1,0:T(8,128)S(1)}, f32[8,256]{1,0:T(8,128)S(1)}, u32[]{:S(2)}, u32[]{:S(2)}) collective-permute-start(f32[8,256]{1,0:T(8,128)S(1)} %get-tuple-element.51), channel_id=1, source_target_pairs={{8,0},{16,8},{24,16},{0,24},{9,1},{17,9},{25,17},{1,25},{10,2},{18... | collective-permute-start | bytes 24584 | tf_op jit(solution)/shard_map/ppermute | solution.py:438
  40.4 0.1 pad.1.clone
  40.5 1.5 %collective-permute-done.8 = f32[8,256]{1,0:T(8,128)S(1)} collective-permute-done((f32[8,256]{1,0:T(8,128)S(1)}, f32[8,256]{1,0:T(8,128)S(1)}, u32[]{:S(2)}, u32[]{:S(2)}) %collective-permute-start.8) | collective-permute-done | bytes 8224 | tf_op jit(solution)/shard_map/ppermute | solution.py:437
  42.1 0.0 collective-permute-done.9
  42.1 0.7 %maximum_add_fusion = f32[128,256]{1,0:T(8,128)} fusion(f32[128,256]{1,0:T(8,128)S(1)} %get-tuple-element.49, f32[8,256]{1,0:T(8,128)S(1)} %collective-permute-done.9, f32[8,256]{1,0:T(8,128)S(1)} %collective-permute-done.8, f32[128]{0:T(128)S(1)} %pad.1.clone), kind=kLoop, calls=%fused_computation | loop fusion | flops 98304 | bytes 279040 | tf_op jit(solution)/shard_map/add | solution.py:440
  (1 shorter events, 0.0 us)
Async XLA Ops:
  2.5 15.9 %all-to-all-start = ((f32[8,72,256]{2,1,0:T(8,128)}), f32[8,72,256]{2,1,0:T(8,128)S(1)}, u32[]{:S(2)}, u32[]{:S(2)}) async-start(f32[8,72,256]{2,1,0:T(8,128)} %pack.1.packed_ref), calls=%async_computation | async-start | bytes 1179648 | tf_op jit(solution)/shard_map/all_to_all | solution.py:394
  18.4 4.9 %collective-permute-start = (f32[8,72,256]{2,1,0:T(8,128)S(1)}, f32[8,72,256]{2,1,0:T(8,128)S(1)}, u32[]{:S(2)}, u32[]{:S(2)}) collective-permute-start(f32[8,72,256]{2,1,0:T(8,128)S(1)} %all-to-all-done.own_ref), channel_id=1, source_target_pairs={{0,1},{1,0},{2,3},{3,2},{4,5},{5,4},{6,7},{7,6},{8,9},{9,8},{10,11... | collective-permute-start | bytes 1769480 | tf_op jit(solution)/shard_map/ppermute | solution.py:391
  19.0 6.0 %collective-permute-start.1 = (f32[128,256]{1,0:T(8,128)S(1)}, f32[128,256]{1,0:T(8,128)S(1)}, u32[]{:S(2)}, u32[]{:S(2)}) collective-permute-start(f32[128,256]{1,0:T(8,128)S(1)} %get-tuple-element.41), channel_id=1, source_target_pairs={{0,2},{1,3},{2,0},{3,1},{4,6},{5,7},{6,4},{7,5},{8,10},{9,11},{10,... | collective-permute-start | bytes 393224 | tf_op jit(solution)/shard_map/ppermute | solution.py:391
  20.6 7.9 %collective-permute-start.2 = (f32[128,256]{1,0:T(8,128)S(1)}, f32[128,256]{1,0:T(8,128)S(1)}, u32[]{:S(2)}, u32[]{:S(2)}) collective-permute-start(f32[128,256]{1,0:T(8,128)S(1)} %get-tuple-element.42), channel_id=1, source_target_pairs={{0,4},{1,5},{2,6},{3,7},{4,0},{5,1},{6,2},{7,3},{8,12},{9,13},{10,... | collective-permute-start | bytes 393224 | tf_op jit(solution)/shard_map/ppermute | solution.py:391
  22.1 7.3 %collective-permute-start.3 = (f32[128,256]{1,0:T(8,128)S(1)}, f32[128,256]{1,0:T(8,128)S(1)}, u32[]{:S(2)}, u32[]{:S(2)}) collective-permute-start(f32[128,256]{1,0:T(8,128)S(1)} %get-tuple-element.43), channel_id=1, source_target_pairs={{0,6},{1,7},{2,4},{3,5},{4,2},{5,3},{6,0},{7,1},{8,14},{9,15},{10,... | collective-permute-start | bytes 393224 | tf_op jit(solution)/shard_map/ppermute | solution.py:391
  22.5 7.1 %collective-permute-start.4 = (f32[128,256]{1,0:T(8,128)S(1)}, f32[128,256]{1,0:T(8,128)S(1)}, u32[]{:S(2)}, u32[]{:S(2)}) collective-permute-start(f32[128,256]{1,0:T(8,128)S(1)} %get-tuple-element.44), channel_id=1, source_target_pairs={{0,3},{1,2},{2,1},{3,0},{4,7},{5,6},{6,5},{7,4},{8,11},{9,10},{10,... | collective-permute-start | bytes 393224 | tf_op jit(solution)/shard_map/ppermute | solution.py:391
  23.2 6.3 %collective-permute-start.5 = (f32[128,256]{1,0:T(8,128)S(1)}, f32[128,256]{1,0:T(8,128)S(1)}, u32[]{:S(2)}, u32[]{:S(2)}) collective-permute-start(f32[128,256]{1,0:T(8,128)S(1)} %get-tuple-element.45), channel_id=1, source_target_pairs={{0,1},{1,0},{2,3},{3,2},{4,5},{5,4},{6,7},{7,6},{8,9},{9,8},{10,11... | collective-permute-start | bytes 393224 | tf_op jit(solution)/shard_map/ppermute | solution.py:391
  24.9 7.4 %collective-permute-start.6 = (f32[128,256]{1,0:T(8,128)S(1)}, f32[128,256]{1,0:T(8,128)S(1)}, u32[]{:S(2)}, u32[]{:S(2)}) collective-permute-start(f32[128,256]{1,0:T(8,128)S(1)} %get-tuple-element.46), channel_id=1, source_target_pairs={{0,5},{1,4},{2,7},{3,6},{4,1},{5,0},{6,3},{7,2},{8,13},{9,12},{10,... | collective-permute-start | bytes 393224 | tf_op jit(solution)/shard_map/ppermute | solution.py:391
  28.6 5.9 %collective-permute-start.7 = (f32[128,256]{1,0:T(8,128)S(1)}, f32[128,256]{1,0:T(8,128)S(1)}, u32[]{:S(2)}, u32[]{:S(2)}) collective-permute-start(f32[128,256]{1,0:T(8,128)S(1)} %get-tuple-element.47), channel_id=1, source_target_pairs={{0,7},{1,6},{2,5},{3,4},{4,3},{5,2},{6,1},{7,0},{8,15},{9,14},{10,... | collective-permute-start | bytes 393224 | tf_op jit(solution)/shard_map/ppermute | solution.py:391
  36.6 5.4 %collective-permute-start.8 = (f32[8,256]{1,0:T(8,128)S(1)}, f32[8,256]{1,0:T(8,128)S(1)}, u32[]{:S(2)}, u32[]{:S(2)}) collective-permute-start(f32[8,256]{1,0:T(8,128)S(1)} %get-tuple-element.50), channel_id=1, source_target_pairs={{0,8},{8,16},{16,24},{24,0},{1,9},{9,17},{17,25},{25,1},{2,10},{10... | collective-permute-start | bytes 24584 | tf_op jit(solution)/shard_map/ppermute | solution.py:437
  38.2 3.9 %collective-permute-start.9 = (f32[8,256]{1,0:T(8,128)S(1)}, f32[8,256]{1,0:T(8,128)S(1)}, u32[]{:S(2)}, u32[]{:S(2)}) collective-permute-start(f32[8,256]{1,0:T(8,128)S(1)} %get-tuple-element.51), channel_id=1, source_target_pairs={{8,0},{16,8},{24,16},{0,24},{9,1},{17,9},{25,17},{1,25},{10,2},{18... | collective-permute-start | bytes 24584 | tf_op jit(solution)/shard_map/ppermute | solution.py:438

commit v12 on v9

--- a/solution.py
+++ b/solution.py
@@ -394,7 +394,7 @@
     own = lax.all_to_all(packed, "member", split_axis=0, concat_axis=0, tiled=True)
     values = solve(packed, factors, panels, members)
     own, *values = lax.optimization_barrier((own, *values))
-    distances = [*range(2, members, 2), *range(3, members, 2), 1]
+    distances = [*range(2, members, 2), members - 1, *range(3, members - 1, 2), 1]
     arrived = {0: values[0], **{k: across(values[k], k) for k in distances}}
     last_ones = distances[-3:-1]
     first_ones = [k for k in arrived if k not in last_ones]

time: 43.1 us -> 45 us (1.044)
  waiting for transfers between devices: 7.18 us -> 8.69 us
    ppermute x8, waiting for transfers between devices: 5.63 us -> 7.14 us  [across(): lax.ppermute(value, 'member', [(i, i ^ distance) for i in range(members)])]
  transfers between devices with their start and end apart: 11 -> 11, of which waited for: 5 -> 3; matrix products, arithmetic and copies ran while one was open for 0% -> 0% of each run, Pallas kernels for 30% -> 29%
where the time goes in v12:
time: 45 us; the launch traced here: 44.7 us
  Pallas kernels  17 us (38%)
  starting transfers between devices  16.4 us (36%)
  waiting for transfers between devices  8.69 us (19%)
  local copies, waits for them, and re-layouts  1.17 us (3%)
  other arithmetic  0.74 us (2%)
  between operations  0.69 us (2%)
    pallas_call x1, Pallas kernels, solve(): pl.pallas_call(functools.partial(solve_kernel, members), out_shape=[jax.S...  9.51 us
    ppermute x8, starting transfers between devices, across(): lax.ppermute(value, 'member', [(i, i ^ distance) for i in range(members)])  7.41 us
    ppermute x8, waiting for transfers between devices, across(): lax.ppermute(value, 'member', [(i, i ^ distance) for i in range(members)])  7.14 us
    pallas_call x3, Pallas kernels, call(): pl.pallas_call(kernel, out_shape=outs, in_specs=specs, out_specs=jax.tree...  5.62 us
    all_to_all x1, starting transfers between devices, on_device(): lax.all_to_all(packed, 'member', split_axis=0, concat_axis=0, tiled=True)  5.18 us
    ppermute x1, starting transfers between devices, on_device(): after = lax.ppermute(first, 'cluster', down)  2.28 us
    pallas_call x1, Pallas kernels, pack(): pl.pallas_call(pack_kernel, out_shape=jax.ShapeDtypeStruct((members, rows...  1.91 us
    ppermute x1, waiting for transfers between devices, on_device(): before = lax.ppermute(last, 'cluster', up)  1.54 us
  transfers between devices with their start and end apart: 11, of which 3 were waited for; matrix products, arithmetic and copies ran while one was open for 0% of the time, Pallas kernels for 29%

profile of v12, /device:TPU:0, one launch (start us, length us, event | category | flops | bytes accessed | tf_op | source)
XLA Modules:
  0.0 44.7 jit_solution(13816548049451443357)
XLA Ops:
  0.6 1.9 %pack.1.packed_ref = f32[8,72,256]{2,1,0:T(8,128)} custom-call(f32[128,256]{1,0:T(8,128)} %loads_ref.1, s32[2,256]{1,0:T(2,128)} %glue_ref.1, s32[2]{0:T(128)} %sizes_ref.1), custom_call_target="tpu_custom_call" | custom-call | flops 1000000 | bytes 1048576 | tf_op jit(solution)/shard_map/pack/pallas_call | solution.py:280
  2.5 5.2 %all-to-all-start = ((f32[8,72,256]{2,1,0:T(8,128)}), f32[8,72,256]{2,1,0:T(8,128)S(1)}, u32[]{:S(2)}, u32[]{:S(2)}) async-start(f32[8,72,256]{2,1,0:T(8,128)} %pack.1.packed_ref), calls=%async_computation | async-start | bytes 1179648 | tf_op jit(solution)/shard_map/all_to_all | solution.py:394
  7.7 0.0 copy-start
  7.7 1.1 %copy-done = f32[8,72,256]{2,1,0:T(8,128)S(1)} copy-done((f32[8,72,256]{2,1,0:T(8,128)S(1)}, f32[8,72,256]{2,1,0:T(8,128)}, u32[]{:S(2)}) %copy-start) | copy-done | bytes 589848
  8.8 9.5 %solve.1 = (f32[128,256]{1,0:T(8,128)S(1)}, f32[128,256]{1,0:T(8,128)S(1)}, f32[128,256]{1,0:T(8,128)S(1)}, f32[128,256]{1,0:T(8,128)S(1)}, f32[128,256]{1,0:T(8...) custom-call(f32[8,72,256]{2,1,0:T(8,128)S(1)} %copy-done, ...), custom_call_target="tpu_custom_call" | custom-call | flops 10000000000 | bytes 8388608 | tf_op jit(solution)/shard_map/solve/pallas_call | solution.py:220
  18.3 0.0 all-to-all-done.own_ref
  18.4 0.6 %collective-permute-start = (f32[8,72,256]{2,1,0:T(8,128)S(1)}, f32[8,72,256]{2,1,0:T(8,128)S(1)}, u32[]{:S(2)}, u32[]{:S(2)}) collective-permute-start(f32[8,72,256]{2,1,0:T(8,128)S(1)} %all-to-all-done.own_ref), channel_id=1, source_target_pairs={{0,1},{1,0},{2,3},{3,2},{4,5},{5,4},{6,7},{7,6},{8,9},{9,8},{10,11... | collective-permute-start | bytes 1769480 | tf_op jit(solution)/shard_map/ppermute | solution.py:391
  18.9 1.7 %collective-permute-start.1 = (f32[128,256]{1,0:T(8,128)S(1)}, f32[128,256]{1,0:T(8,128)S(1)}, u32[]{:S(2)}, u32[]{:S(2)}) collective-permute-start(f32[128,256]{1,0:T(8,128)S(1)} %get-tuple-element.41), channel_id=1, source_target_pairs={{0,2},{1,3},{2,0},{3,1},{4,6},{5,7},{6,4},{7,5},{8,10},{9,11},{10,... | collective-permute-start | bytes 393224 | tf_op jit(solution)/shard_map/ppermute | solution.py:391
  20.6 1.5 %collective-permute-start.2 = (f32[128,256]{1,0:T(8,128)S(1)}, f32[128,256]{1,0:T(8,128)S(1)}, u32[]{:S(2)}, u32[]{:S(2)}) collective-permute-start(f32[128,256]{1,0:T(8,128)S(1)} %get-tuple-element.42), channel_id=1, source_target_pairs={{0,4},{1,5},{2,6},{3,7},{4,0},{5,1},{6,2},{7,3},{8,12},{9,13},{10,... | collective-permute-start | bytes 393224 | tf_op jit(solution)/shard_map/ppermute | solution.py:391
  22.1 0.3 collective-permute-start.3
  22.4 1.7 %collective-permute-start.4 = (f32[128,256]{1,0:T(8,128)S(1)}, f32[128,256]{1,0:T(8,128)S(1)}, u32[]{:S(2)}, u32[]{:S(2)}) collective-permute-start(f32[128,256]{1,0:T(8,128)S(1)} %get-tuple-element.44), channel_id=1, source_target_pairs={{0,7},{1,6},{2,5},{3,4},{4,3},{5,2},{6,1},{7,0},{8,15},{9,14},{10,... | collective-permute-start | bytes 393224 | tf_op jit(solution)/shard_map/ppermute | solution.py:391
  24.1 0.0 collective-permute-done.twin_ref
  24.1 1.0 %collective-permute-start.5 = (f32[128,256]{1,0:T(8,128)S(1)}, f32[128,256]{1,0:T(8,128)S(1)}, u32[]{:S(2)}, u32[]{:S(2)}) collective-permute-start(f32[128,256]{1,0:T(8,128)S(1)} %get-tuple-element.45), channel_id=1, source_target_pairs={{0,1},{1,0},{2,3},{3,2},{4,5},{5,4},{6,7},{7,6},{8,9},{9,8},{10,11... | collective-permute-start | bytes 393224 | tf_op jit(solution)/shard_map/ppermute | solution.py:391
  25.1 0.7 %routes.1 = (s32[256,16]{1,0:T(8,128)S(1)}, s32[8,128]{1,0:T(8,128)S(1)}, bf16[1024,256]{1,0:T(8,128)(2,1)S(1)}, bf16[1024,256]{1,0:T(8,128)(2,1)S(1)}) custom-call(s32[1]{0:T(128)} %bitcast.place_ref, f32[8,72,256]{2,1,0:T(8,128)S(1)} %all-to-all-done.own_ref, f32[8,72,256]{2,1,0:T(8,128)S(1)} %collective-permute-done.twin_ref), custom_call_target="tpu_custom_call" | custom-call | flops 2000000000 | bytes 4194304 | tf_op jit(solution)/shard_map/routes/pallas_call | solution.py:369
  25.8 0.0 collective-permute-done.1.refs_1_
  25.8 0.2 collective-permute-start.6
  26.1 5.1 %collective-permute-done.2.refs_2_ = f32[128,256]{1,0:T(8,128)S(1)} collective-permute-done((f32[128,256]{1,0:T(8,128)S(1)}, f32[128,256]{1,0:T(8,128)S(1)}, u32[]{:S(2)}, u32[]{:S(2)}) %collective-permute-start.2) | collective-permute-done | bytes 131104 | tf_op jit(solution)/shard_map/ppermute | solution.py:391
  31.1 0.4 collective-permute-start.7
  31.6 0.0 collective-permute-done.3.refs_3_
  31.6 0.0 collective-permute-done.4.refs_4_
  31.6 0.0 collective-permute-done.5.refs_5_
  31.6 2.8 %early.1.early_ref = f32[128,1024]{1,0:T(8,128)S(1)} custom-call(s32[8,128]{1,0:T(8,128)S(1)} %get-tuple-element.36.label_ref, s32[256,16]{1,0:T(8,128)S(1)} %get-tuple-element.37.stand_ref, f32[128,256]{1,0:T(8,128)S(1)} %get-tuple-element.40.refs_0_, f32[128,256]{1,0:T(8,128)S(1)} %collective-permute-done.1.refs_1_, ...), custom_call_target="tpu_custom_call" | custom-call | flops 2000000000 | bytes 4194304 | tf_op jit(solution)/shard_map/early/pallas_call | solution.py:369
  34.4 0.0 collective-permute-done.6.refs_0_
  34.4 2.0 %collective-permute-done.7.refs_1_ = f32[128,256]{1,0:T(8,128)S(1)} collective-permute-done((f32[128,256]{1,0:T(8,128)S(1)}, f32[128,256]{1,0:T(8,128)S(1)}, u32[]{:S(2)}, u32[]{:S(2)}) %collective-permute-start.7) | collective-permute-done | bytes 131104 | tf_op jit(solution)/shard_map/ppermute | solution.py:391
  36.4 2.1 %finish.1 = (f32[128,1024]{1,0:T(8,128)}, f32[128,256]{1,0:T(8,128)S(1)}, f32[8,256]{1,0:T(8,128)S(1)}, f32[8,256]{1,0:T(8,128)S(1)}) custom-call(s32[8,128]{1,0:T(8,128)S(1)} %get-tuple-element.36.label_ref, s32[256,16]{1,0:T(8,128)S(1)} %get-tuple-element.37.stand_ref, bf16[1024,256]{1,0:T(8,128)(2,1)S(1)} %get-tuple-element.38.high_ref, ...), custom_call_target="tpu_custom_call" | custom-call | flops 3000000000 | bytes 4194304 | tf_op jit(solution)/shard_map/finish/pallas_call | solution.py:369
  38.5 1.5 %collective-permute-start.8 = (f32[8,256]{1,0:T(8,128)S(1)}, f32[8,256]{1,0:T(8,128)S(1)}, u32[]{:S(2)}, u32[]{:S(2)}) collective-permute-start(f32[8,256]{1,0:T(8,128)S(1)} %get-tuple-element.50), channel_id=1, source_target_pairs={{0,8},{8,16},{16,24},{24,0},{1,9},{9,17},{17,25},{25,1},{2,10},{10... | collective-permute-start | bytes 24584 | tf_op jit(solution)/shard_map/ppermute | solution.py:437
  40.1 2.3 %collective-permute-start.9 = (f32[8,256]{1,0:T(8,128)S(1)}, f32[8,256]{1,0:T(8,128)S(1)}, u32[]{:S(2)}, u32[]{:S(2)}) collective-permute-start(f32[8,256]{1,0:T(8,128)S(1)} %get-tuple-element.51), channel_id=1, source_target_pairs={{8,0},{16,8},{24,16},{0,24},{9,1},{17,9},{25,17},{1,25},{10,2},{18... | collective-permute-start | bytes 24584 | tf_op jit(solution)/shard_map/ppermute | solution.py:438
  42.4 0.1 pad.1.clone
  42.5 1.5 %collective-permute-done.8 = f32[8,256]{1,0:T(8,128)S(1)} collective-permute-done((f32[8,256]{1,0:T(8,128)S(1)}, f32[8,256]{1,0:T(8,128)S(1)}, u32[]{:S(2)}, u32[]{:S(2)}) %collective-permute-start.8) | collective-permute-done | bytes 8224 | tf_op jit(solution)/shard_map/ppermute | solution.py:437
  44.0 0.0 collective-permute-done.9
  44.0 0.7 %maximum_add_fusion = f32[128,256]{1,0:T(8,128)} fusion(f32[128,256]{1,0:T(8,128)S(1)} %get-tuple-element.49, f32[8,256]{1,0:T(8,128)S(1)} %collective-permute-done.9, f32[8,256]{1,0:T(8,128)S(1)} %collective-permute-done.8, f32[128]{0:T(128)S(1)} %pad.1.clone), kind=kLoop, calls=%fused_computation | loop fusion | flops 98304 | bytes 279040 | tf_op jit(solution)/shard_map/add | solution.py:440
  (1 shorter events, 0.0 us)
Async XLA Ops:
  2.5 15.8 %all-to-all-start = ((f32[8,72,256]{2,1,0:T(8,128)}), f32[8,72,256]{2,1,0:T(8,128)S(1)}, u32[]{:S(2)}, u32[]{:S(2)}) async-start(f32[8,72,256]{2,1,0:T(8,128)} %pack.1.packed_ref), calls=%async_computation | async-start | bytes 1179648 | tf_op jit(solution)/shard_map/all_to_all | solution.py:394
  7.7 1.1 %copy-start = (f32[8,72,256]{2,1,0:T(8,128)S(1)}, f32[8,72,256]{2,1,0:T(8,128)}, u32[]{:S(2)}) copy-start(f32[8,72,256]{2,1,0:T(8,128)} %pack.1.packed_ref) | copy-start | bytes 1769476
  18.4 5.8 %collective-permute-start = (f32[8,72,256]{2,1,0:T(8,128)S(1)}, f32[8,72,256]{2,1,0:T(8,128)S(1)}, u32[]{:S(2)}, u32[]{:S(2)}) collective-permute-start(f32[8,72,256]{2,1,0:T(8,128)S(1)} %all-to-all-done.own_ref), channel_id=1, source_target_pairs={{0,1},{1,0},{2,3},{3,2},{4,5},{5,4},{6,7},{7,6},{8,9},{9,8},{10,11... | collective-permute-start | bytes 1769480 | tf_op jit(solution)/shard_map/ppermute | solution.py:391
  18.9 6.9 %collective-permute-start.1 = (f32[128,256]{1,0:T(8,128)S(1)}, f32[128,256]{1,0:T(8,128)S(1)}, u32[]{:S(2)}, u32[]{:S(2)}) collective-permute-start(f32[128,256]{1,0:T(8,128)S(1)} %get-tuple-element.41), channel_id=1, source_target_pairs={{0,2},{1,3},{2,0},{3,1},{4,6},{5,7},{6,4},{7,5},{8,10},{9,11},{10,... | collective-permute-start | bytes 393224 | tf_op jit(solution)/shard_map/ppermute | solution.py:391
  20.6 10.5 %collective-permute-start.2 = (f32[128,256]{1,0:T(8,128)S(1)}, f32[128,256]{1,0:T(8,128)S(1)}, u32[]{:S(2)}, u32[]{:S(2)}) collective-permute-start(f32[128,256]{1,0:T(8,128)S(1)} %get-tuple-element.42), channel_id=1, source_target_pairs={{0,4},{1,5},{2,6},{3,7},{4,0},{5,1},{6,2},{7,3},{8,12},{9,13},{10,... | collective-permute-start | bytes 393224 | tf_op jit(solution)/shard_map/ppermute | solution.py:391
  22.1 9.5 %collective-permute-start.3 = (f32[128,256]{1,0:T(8,128)S(1)}, f32[128,256]{1,0:T(8,128)S(1)}, u32[]{:S(2)}, u32[]{:S(2)}) collective-permute-start(f32[128,256]{1,0:T(8,128)S(1)} %get-tuple-element.43), channel_id=1, source_target_pairs={{0,6},{1,7},{2,4},{3,5},{4,2},{5,3},{6,0},{7,1},{8,14},{9,15},{10,... | collective-permute-start | bytes 393224 | tf_op jit(solution)/shard_map/ppermute | solution.py:391
  22.4 9.2 %collective-permute-start.4 = (f32[128,256]{1,0:T(8,128)S(1)}, f32[128,256]{1,0:T(8,128)S(1)}, u32[]{:S(2)}, u32[]{:S(2)}) collective-permute-start(f32[128,256]{1,0:T(8,128)S(1)} %get-tuple-element.44), channel_id=1, source_target_pairs={{0,7},{1,6},{2,5},{3,4},{4,3},{5,2},{6,1},{7,0},{8,15},{9,14},{10,... | collective-permute-start | bytes 393224 | tf_op jit(solution)/shard_map/ppermute | solution.py:391
  24.1 7.5 %collective-permute-start.5 = (f32[128,256]{1,0:T(8,128)S(1)}, f32[128,256]{1,0:T(8,128)S(1)}, u32[]{:S(2)}, u32[]{:S(2)}) collective-permute-start(f32[128,256]{1,0:T(8,128)S(1)} %get-tuple-element.45), channel_id=1, source_target_pairs={{0,1},{1,0},{2,3},{3,2},{4,5},{5,4},{6,7},{7,6},{8,9},{9,8},{10,11... | collective-permute-start | bytes 393224 | tf_op jit(solution)/shard_map/ppermute | solution.py:391
  25.8 8.6 %collective-permute-start.6 = (f32[128,256]{1,0:T(8,128)S(1)}, f32[128,256]{1,0:T(8,128)S(1)}, u32[]{:S(2)}, u32[]{:S(2)}) collective-permute-start(f32[128,256]{1,0:T(8,128)S(1)} %get-tuple-element.46), channel_id=1, source_target_pairs={{0,3},{1,2},{2,1},{3,0},{4,7},{5,6},{6,5},{7,4},{8,11},{9,10},{10,... | collective-permute-start | bytes 393224 | tf_op jit(solution)/shard_map/ppermute | solution.py:391
  31.1 5.3 %collective-permute-start.7 = (f32[128,256]{1,0:T(8,128)S(1)}, f32[128,256]{1,0:T(8,128)S(1)}, u32[]{:S(2)}, u32[]{:S(2)}) collective-permute-start(f32[128,256]{1,0:T(8,128)S(1)} %get-tuple-element.47), channel_id=1, source_target_pairs={{0,5},{1,4},{2,7},{3,6},{4,1},{5,0},{6,3},{7,2},{8,13},{9,12},{10,... | collective-permute-start | bytes 393224 | tf_op jit(solution)/shard_map/ppermute | solution.py:391
  38.5 5.4 %collective-permute-start.8 = (f32[8,256]{1,0:T(8,128)S(1)}, f32[8,256]{1,0:T(8,128)S(1)}, u32[]{:S(2)}, u32[]{:S(2)}) collective-permute-start(f32[8,256]{1,0:T(8,128)S(1)} %get-tuple-element.50), channel_id=1, source_target_pairs={{0,8},{8,16},{16,24},{24,0},{1,9},{9,17},{17,25},{25,1},{2,10},{10... | collective-permute-start | bytes 24584 | tf_op jit(solution)/shard_map/ppermute | solution.py:437
  40.1 3.9 %collective-permute-start.9 = (f32[8,256]{1,0:T(8,128)S(1)}, f32[8,256]{1,0:T(8,128)S(1)}, u32[]{:S(2)}, u32[]{:S(2)}) collective-permute-start(f32[8,256]{1,0:T(8,128)S(1)} %get-tuple-element.51), channel_id=1, source_target_pairs={{8,0},{16,8},{24,16},{0,24},{9,1},{17,9},{25,17},{1,25},{10,2},{18... | collective-permute-start | bytes 24584 | tf_op jit(solution)/shard_map/ppermute | solution.py:438

commit v13 on v9

--- a/solution.py
+++ b/solution.py
@@ -396,7 +396,7 @@
     own, *values = lax.optimization_barrier((own, *values))
     distances = [*range(2, members, 2), *range(3, members, 2), 1]
     arrived = {0: values[0], **{k: across(values[k], k) for k in distances}}
-    last_ones = distances[-3:-1]
+    last_ones = distances[-2:-1]
     first_ones = [k for k in arrived if k not in last_ones]
     twin = across(own, 1)
     stand, labels, high, low = call(

time: 43.1 us -> 43 us (level)
  waiting for transfers between devices: 7.18 us -> 6.74 us
    ppermute x8, waiting for transfers between devices: 5.63 us -> 5.19 us  [across(): lax.ppermute(value, 'member', [(i, i ^ distance) for i in range(members)])]
  transfers between devices with their start and end apart: 11 -> 11, of which waited for: 5 -> 6; matrix products, arithmetic and copies ran while one was open for 0% -> 0% of each run, Pallas kernels for 30% -> 31%
where the time goes in v13:
time: 43 us; the launch traced here: 42.7 us
  Pallas kernels  17.1 us (40%)
  starting transfers between devices  16.3 us (38%)
  waiting for transfers between devices  6.74 us (16%)
  local copies, waits for them, and re-layouts  1.17 us (3%)
  other arithmetic  0.74 us (2%)
  between operations  0.69 us (2%)
    pallas_call x1, Pallas kernels, solve(): pl.pallas_call(functools.partial(solve_kernel, members), out_shape=[jax.S...  9.51 us
    ppermute x8, starting transfers between devices, across(): lax.ppermute(value, 'member', [(i, i ^ distance) for i in range(members)])  7.32 us
    pallas_call x3, Pallas kernels, call(): pl.pallas_call(kernel, out_shape=outs, in_specs=specs, out_specs=jax.tree...  5.66 us
    ppermute x8, waiting for transfers between devices, across(): lax.ppermute(value, 'member', [(i, i ^ distance) for i in range(members)])  5.19 us
    all_to_all x1, starting transfers between devices, on_device(): lax.all_to_all(packed, 'member', split_axis=0, concat_axis=0, tiled=True)  5.18 us
    ppermute x1, starting transfers between devices, on_device(): after = lax.ppermute(first, 'cluster', down)  2.25 us
    pallas_call x1, Pallas kernels, pack(): pl.pallas_call(pack_kernel, out_shape=jax.ShapeDtypeStruct((members, rows...  1.91 us
    ppermute x1, starting transfers between devices, on_device(): before = lax.ppermute(last, 'cluster', up)  1.57 us
  transfers between devices with their start and end apart: 11, of which 6 were waited for; matrix products, arithmetic and copies ran while one was open for 0% of the time, Pallas kernels for 31%

profile of v13, /device:TPU:0, one launch (start us, length us, event | category | flops | bytes accessed | tf_op | source)
XLA Modules:
  0.0 42.7 jit_solution(15738107420907347712)
XLA Ops:
  0.6 1.9 %pack.1.packed_ref = f32[8,72,256]{2,1,0:T(8,128)} custom-call(f32[128,256]{1,0:T(8,128)} %loads_ref.1, s32[2,256]{1,0:T(2,128)} %glue_ref.1, s32[2]{0:T(128)} %sizes_ref.1), custom_call_target="tpu_custom_call" | custom-call | flops 1000000 | bytes 1048576 | tf_op jit(solution)/shard_map/pack/pallas_call | solution.py:280
  2.5 5.2 %all-to-all-start = ((f32[8,72,256]{2,1,0:T(8,128)}), f32[8,72,256]{2,1,0:T(8,128)S(1)}, u32[]{:S(2)}, u32[]{:S(2)}) async-start(f32[8,72,256]{2,1,0:T(8,128)} %pack.1.packed_ref), calls=%async_computation | async-start | bytes 1179648 | tf_op jit(solution)/shard_map/all_to_all | solution.py:394
  7.7 0.0 copy-start
  7.7 1.1 %copy-done = f32[8,72,256]{2,1,0:T(8,128)S(1)} copy-done((f32[8,72,256]{2,1,0:T(8,128)S(1)}, f32[8,72,256]{2,1,0:T(8,128)}, u32[]{:S(2)}) %copy-start) | copy-done | bytes 589848
  8.8 9.5 %solve.1 = (f32[128,256]{1,0:T(8,128)S(1)}, f32[128,256]{1,0:T(8,128)S(1)}, f32[128,256]{1,0:T(8,128)S(1)}, f32[128,256]{1,0:T(8,128)S(1)}, f32[128,256]{1,0:T(8...) custom-call(f32[8,72,256]{2,1,0:T(8,128)S(1)} %copy-done, ...), custom_call_target="tpu_custom_call" | custom-call | flops 10000000000 | bytes 8388608 | tf_op jit(solution)/shard_map/solve/pallas_call | solution.py:220
  18.3 0.0 all-to-all-done.own_ref
  18.4 0.6 %collective-permute-start = (f32[8,72,256]{2,1,0:T(8,128)S(1)}, f32[8,72,256]{2,1,0:T(8,128)S(1)}, u32[]{:S(2)}, u32[]{:S(2)}) collective-permute-start(f32[8,72,256]{2,1,0:T(8,128)S(1)} %all-to-all-done.own_ref), channel_id=1, source_target_pairs={{0,1},{1,0},{2,3},{3,2},{4,5},{5,4},{6,7},{7,6},{8,9},{9,8},{10,11... | collective-permute-start | bytes 1769480 | tf_op jit(solution)/shard_map/ppermute | solution.py:391
  18.9 1.7 %collective-permute-start.1 = (f32[128,256]{1,0:T(8,128)S(1)}, f32[128,256]{1,0:T(8,128)S(1)}, u32[]{:S(2)}, u32[]{:S(2)}) collective-permute-start(f32[128,256]{1,0:T(8,128)S(1)} %get-tuple-element.41), channel_id=1, source_target_pairs={{0,2},{1,3},{2,0},{3,1},{4,6},{5,7},{6,4},{7,5},{8,10},{9,11},{10,... | collective-permute-start | bytes 393224 | tf_op jit(solution)/shard_map/ppermute | solution.py:391
  20.6 1.5 %collective-permute-start.2 = (f32[128,256]{1,0:T(8,128)S(1)}, f32[128,256]{1,0:T(8,128)S(1)}, u32[]{:S(2)}, u32[]{:S(2)}) collective-permute-start(f32[128,256]{1,0:T(8,128)S(1)} %get-tuple-element.42), channel_id=1, source_target_pairs={{0,4},{1,5},{2,6},{3,7},{4,0},{5,1},{6,2},{7,3},{8,12},{9,13},{10,... | collective-permute-start | bytes 393224 | tf_op jit(solution)/shard_map/ppermute | solution.py:391
  22.1 0.3 collective-permute-start.3
  22.4 0.8 %collective-permute-start.4 = (f32[128,256]{1,0:T(8,128)S(1)}, f32[128,256]{1,0:T(8,128)S(1)}, u32[]{:S(2)}, u32[]{:S(2)}) collective-permute-start(f32[128,256]{1,0:T(8,128)S(1)} %get-tuple-element.44), channel_id=1, source_target_pairs={{0,3},{1,2},{2,1},{3,0},{4,7},{5,6},{6,5},{7,4},{8,11},{9,10},{10,... | collective-permute-start | bytes 393224 | tf_op jit(solution)/shard_map/ppermute | solution.py:391
  23.2 1.5 %collective-permute-done.1.refs_1_ = f32[128,256]{1,0:T(8,128)S(1)} collective-permute-done((f32[128,256]{1,0:T(8,128)S(1)}, f32[128,256]{1,0:T(8,128)S(1)}, u32[]{:S(2)}, u32[]{:S(2)}) %collective-permute-start.1) | collective-permute-done | bytes 131104 | tf_op jit(solution)/shard_map/ppermute | solution.py:391
  24.7 0.8 %collective-permute-start.5 = (f32[128,256]{1,0:T(8,128)S(1)}, f32[128,256]{1,0:T(8,128)S(1)}, u32[]{:S(2)}, u32[]{:S(2)}) collective-permute-start(f32[128,256]{1,0:T(8,128)S(1)} %get-tuple-element.45), channel_id=1, source_target_pairs={{0,5},{1,4},{2,7},{3,6},{4,1},{5,0},{6,3},{7,2},{8,13},{9,12},{10,... | collective-permute-start | bytes 393224 | tf_op jit(solution)/shard_map/ppermute | solution.py:391
  25.5 0.0 collective-permute-done.twin_ref
  25.5 1.3 %collective-permute-start.6 = (f32[128,256]{1,0:T(8,128)S(1)}, f32[128,256]{1,0:T(8,128)S(1)}, u32[]{:S(2)}, u32[]{:S(2)}) collective-permute-start(f32[128,256]{1,0:T(8,128)S(1)} %get-tuple-element.46), channel_id=1, source_target_pairs={{0,1},{1,0},{2,3},{3,2},{4,5},{5,4},{6,7},{7,6},{8,9},{9,8},{10,11... | collective-permute-start | bytes 393224 | tf_op jit(solution)/shard_map/ppermute | solution.py:391
  26.8 0.7 %routes.1 = (s32[256,16]{1,0:T(8,128)S(1)}, s32[8,128]{1,0:T(8,128)S(1)}, bf16[1024,256]{1,0:T(8,128)(2,1)S(1)}, bf16[1024,256]{1,0:T(8,128)(2,1)S(1)}) custom-call(s32[1]{0:T(128)} %bitcast.place_ref, f32[8,72,256]{2,1,0:T(8,128)S(1)} %all-to-all-done.own_ref, f32[8,72,256]{2,1,0:T(8,128)S(1)} %collective-permute-done.twin_ref), custom_call_target="tpu_custom_call" | custom-call | flops 2000000000 | bytes 4194304 | tf_op jit(solution)/shard_map/routes/pallas_call | solution.py:369
  27.6 1.0 %collective-permute-done.2.refs_2_ = f32[128,256]{1,0:T(8,128)S(1)} collective-permute-done((f32[128,256]{1,0:T(8,128)S(1)}, f32[128,256]{1,0:T(8,128)S(1)}, u32[]{:S(2)}, u32[]{:S(2)}) %collective-permute-start.2) | collective-permute-done | bytes 131104 | tf_op jit(solution)/shard_map/ppermute | solution.py:391
  28.5 0.3 collective-permute-start.7
  28.9 0.5 %collective-permute-done.3.refs_3_ = f32[128,256]{1,0:T(8,128)S(1)} collective-permute-done((f32[128,256]{1,0:T(8,128)S(1)}, f32[128,256]{1,0:T(8,128)S(1)}, u32[]{:S(2)}, u32[]{:S(2)}) %collective-permute-start.3) | collective-permute-done | bytes 131104 | tf_op jit(solution)/shard_map/ppermute | solution.py:391
  29.4 0.1 collective-permute-done.4.refs_4_
  29.5 2.0 %collective-permute-done.5.refs_5_ = f32[128,256]{1,0:T(8,128)S(1)} collective-permute-done((f32[128,256]{1,0:T(8,128)S(1)}, f32[128,256]{1,0:T(8,128)S(1)}, u32[]{:S(2)}, u32[]{:S(2)}) %collective-permute-start.5) | collective-permute-done | bytes 131104 | tf_op jit(solution)/shard_map/ppermute | solution.py:391
  31.6 0.0 collective-permute-done.6.refs_6_
  31.6 3.2 %early.1.early_ref = f32[128,1024]{1,0:T(8,128)S(1)} custom-call(s32[8,128]{1,0:T(8,128)S(1)} %get-tuple-element.36.label_ref, s32[256,16]{1,0:T(8,128)S(1)} %get-tuple-element.37.stand_ref, f32[128,256]{1,0:T(8,128)S(1)} %get-tuple-element.40.refs_0_, f32[128,256]{1,0:T(8,128)S(1)} %collective-permute-done.1.refs_1_, ...), custom_call_target="tpu_custom_call" | custom-call | flops 2000000000 | bytes 4194304 | tf_op jit(solution)/shard_map/early/pallas_call | solution.py:369
  34.8 0.0 collective-permute-done.7.refs_0_
  34.8 1.7 %finish.1 = (f32[128,1024]{1,0:T(8,128)}, f32[128,256]{1,0:T(8,128)S(1)}, f32[8,256]{1,0:T(8,128)S(1)}, f32[8,256]{1,0:T(8,128)S(1)}) custom-call(s32[8,128]{1,0:T(8,128)S(1)} %get-tuple-element.36.label_ref, s32[256,16]{1,0:T(8,128)S(1)} %get-tuple-element.37.stand_ref, bf16[1024,256]{1,0:T(8,128)(2,1)S(1)} %get-tuple-element.38.high_ref, ...), custom_call_target="tpu_custom_call" | custom-call | flops 3000000000 | bytes 4194304 | tf_op jit(solution)/shard_map/finish/pallas_call | solution.py:369
  36.5 1.6 %collective-permute-start.8 = (f32[8,256]{1,0:T(8,128)S(1)}, f32[8,256]{1,0:T(8,128)S(1)}, u32[]{:S(2)}, u32[]{:S(2)}) collective-permute-start(f32[8,256]{1,0:T(8,128)S(1)} %get-tuple-element.50), channel_id=1, source_target_pairs={{0,8},{8,16},{16,24},{24,0},{1,9},{9,17},{17,25},{25,1},{2,10},{10... | collective-permute-start | bytes 24584 | tf_op jit(solution)/shard_map/ppermute | solution.py:437
  38.1 2.3 %collective-permute-start.9 = (f32[8,256]{1,0:T(8,128)S(1)}, f32[8,256]{1,0:T(8,128)S(1)}, u32[]{:S(2)}, u32[]{:S(2)}) collective-permute-start(f32[8,256]{1,0:T(8,128)S(1)} %get-tuple-element.51), channel_id=1, source_target_pairs={{8,0},{16,8},{24,16},{0,24},{9,1},{17,9},{25,17},{1,25},{10,2},{18... | collective-permute-start | bytes 24584 | tf_op jit(solution)/shard_map/ppermute | solution.py:438
  40.4 0.1 pad.1.clone
  40.4 1.5 %collective-permute-done.8 = f32[8,256]{1,0:T(8,128)S(1)} collective-permute-done((f32[8,256]{1,0:T(8,128)S(1)}, f32[8,256]{1,0:T(8,128)S(1)}, u32[]{:S(2)}, u32[]{:S(2)}) %collective-permute-start.8) | collective-permute-done | bytes 8224 | tf_op jit(solution)/shard_map/ppermute | solution.py:437
  42.0 0.0 collective-permute-done.9
  42.0 0.7 %maximum_add_fusion = f32[128,256]{1,0:T(8,128)} fusion(f32[128,256]{1,0:T(8,128)S(1)} %get-tuple-element.49, f32[8,256]{1,0:T(8,128)S(1)} %collective-permute-done.9, f32[8,256]{1,0:T(8,128)S(1)} %collective-permute-done.8, f32[128]{0:T(128)S(1)} %pad.1.clone), kind=kLoop, calls=%fused_computation | loop fusion | flops 98304 | bytes 279040 | tf_op jit(solution)/shard_map/add | solution.py:440
  (1 shorter events, 0.0 us)
Async XLA Ops:
  2.5 15.8 %all-to-all-start = ((f32[8,72,256]{2,1,0:T(8,128)}), f32[8,72,256]{2,1,0:T(8,128)S(1)}, u32[]{:S(2)}, u32[]{:S(2)}) async-start(f32[8,72,256]{2,1,0:T(8,128)} %pack.1.packed_ref), calls=%async_computation | async-start | bytes 1179648 | tf_op jit(solution)/shard_map/all_to_all | solution.py:394
  7.7 1.1 %copy-start = (f32[8,72,256]{2,1,0:T(8,128)S(1)}, f32[8,72,256]{2,1,0:T(8,128)}, u32[]{:S(2)}) copy-start(f32[8,72,256]{2,1,0:T(8,128)} %pack.1.packed_ref) | copy-start | bytes 1769476
  18.4 7.2 %collective-permute-start = (f32[8,72,256]{2,1,0:T(8,128)S(1)}, f32[8,72,256]{2,1,0:T(8,128)S(1)}, u32[]{:S(2)}, u32[]{:S(2)}) collective-permute-start(f32[8,72,256]{2,1,0:T(8,128)S(1)} %all-to-all-done.own_ref), channel_id=1, source_target_pairs={{0,1},{1,0},{2,3},{3,2},{4,5},{5,4},{6,7},{7,6},{8,9},{9,8},{10,11... | collective-permute-start | bytes 1769480 | tf_op jit(solution)/shard_map/ppermute | solution.py:391
  18.9 5.8 %collective-permute-start.1 = (f32[128,256]{1,0:T(8,128)S(1)}, f32[128,256]{1,0:T(8,128)S(1)}, u32[]{:S(2)}, u32[]{:S(2)}) collective-permute-start(f32[128,256]{1,0:T(8,128)S(1)} %get-tuple-element.41), channel_id=1, source_target_pairs={{0,2},{1,3},{2,0},{3,1},{4,6},{5,7},{6,4},{7,5},{8,10},{9,11},{10,... | collective-permute-start | bytes 393224 | tf_op jit(solution)/shard_map/ppermute | solution.py:391
  20.6 7.9 %collective-permute-start.2 = (f32[128,256]{1,0:T(8,128)S(1)}, f32[128,256]{1,0:T(8,128)S(1)}, u32[]{:S(2)}, u32[]{:S(2)}) collective-permute-start(f32[128,256]{1,0:T(8,128)S(1)} %get-tuple-element.42), channel_id=1, source_target_pairs={{0,4},{1,5},{2,6},{3,7},{4,0},{5,1},{6,2},{7,3},{8,12},{9,13},{10,... | collective-permute-start | bytes 393224 | tf_op jit(solution)/shard_map/ppermute | solution.py:391
  22.1 7.3 %collective-permute-start.3 = (f32[128,256]{1,0:T(8,128)S(1)}, f32[128,256]{1,0:T(8,128)S(1)}, u32[]{:S(2)}, u32[]{:S(2)}) collective-permute-start(f32[128,256]{1,0:T(8,128)S(1)} %get-tuple-element.43), channel_id=1, source_target_pairs={{0,6},{1,7},{2,4},{3,5},{4,2},{5,3},{6,0},{7,1},{8,14},{9,15},{10,... | collective-permute-start | bytes 393224 | tf_op jit(solution)/shard_map/ppermute | solution.py:391
  22.4 7.1 %collective-permute-start.4 = (f32[128,256]{1,0:T(8,128)S(1)}, f32[128,256]{1,0:T(8,128)S(1)}, u32[]{:S(2)}, u32[]{:S(2)}) collective-permute-start(f32[128,256]{1,0:T(8,128)S(1)} %get-tuple-element.44), channel_id=1, source_target_pairs={{0,3},{1,2},{2,1},{3,0},{4,7},{5,6},{6,5},{7,4},{8,11},{9,10},{10,... | collective-permute-start | bytes 393224 | tf_op jit(solution)/shard_map/ppermute | solution.py:391
  24.7 6.9 %collective-permute-start.5 = (f32[128,256]{1,0:T(8,128)S(1)}, f32[128,256]{1,0:T(8,128)S(1)}, u32[]{:S(2)}, u32[]{:S(2)}) collective-permute-start(f32[128,256]{1,0:T(8,128)S(1)} %get-tuple-element.45), channel_id=1, source_target_pairs={{0,5},{1,4},{2,7},{3,6},{4,1},{5,0},{6,3},{7,2},{8,13},{9,12},{10,... | collective-permute-start | bytes 393224 | tf_op jit(solution)/shard_map/ppermute | solution.py:391
  25.5 6.1 %collective-permute-start.6 = (f32[128,256]{1,0:T(8,128)S(1)}, f32[128,256]{1,0:T(8,128)S(1)}, u32[]{:S(2)}, u32[]{:S(2)}) collective-permute-start(f32[128,256]{1,0:T(8,128)S(1)} %get-tuple-element.46), channel_id=1, source_target_pairs={{0,1},{1,0},{2,3},{3,2},{4,5},{5,4},{6,7},{7,6},{8,9},{9,8},{10,11... | collective-permute-start | bytes 393224 | tf_op jit(solution)/shard_map/ppermute | solution.py:391
  28.5 6.3 %collective-permute-start.7 = (f32[128,256]{1,0:T(8,128)S(1)}, f32[128,256]{1,0:T(8,128)S(1)}, u32[]{:S(2)}, u32[]{:S(2)}) collective-permute-start(f32[128,256]{1,0:T(8,128)S(1)} %get-tuple-element.47), channel_id=1, source_target_pairs={{0,7},{1,6},{2,5},{3,4},{4,3},{5,2},{6,1},{7,0},{8,15},{9,14},{10,... | collective-permute-start | bytes 393224 | tf_op jit(solution)/shard_map/ppermute | solution.py:391
  36.5 5.4 %collective-permute-start.8 = (f32[8,256]{1,0:T(8,128)S(1)}, f32[8,256]{1,0:T(8,128)S(1)}, u32[]{:S(2)}, u32[]{:S(2)}) collective-permute-start(f32[8,256]{1,0:T(8,128)S(1)} %get-tuple-element.50), channel_id=1, source_target_pairs={{0,8},{8,16},{16,24},{24,0},{1,9},{9,17},{17,25},{25,1},{2,10},{10... | collective-permute-start | bytes 24584 | tf_op jit(solution)/shard_map/ppermute | solution.py:437
  38.1 3.9 %collective-permute-start.9 = (f32[8,256]{1,0:T(8,128)S(1)}, f32[8,256]{1,0:T(8,128)S(1)}, u32[]{:S(2)}, u32[]{:S(2)}) collective-permute-start(f32[8,256]{1,0:T(8,128)S(1)} %get-tuple-element.51), channel_id=1, source_target_pairs={{8,0},{16,8},{24,16},{0,24},{9,1},{17,9},{25,17},{1,25},{10,2},{18... | collective-permute-start | bytes 24584 | tf_op jit(solution)/shard_map/ppermute | solution.py:438
